TPU v7x, 32 devices: a whole 2x2x4 slice. The times are simulated.
32 devices in a mesh: groups: 2 (over x), gx: 16 (over z, y, core).
Axes of the slice: x: 2, y: 2, z: 4, core: 2. Of those that a mesh axis runs over, the one named last changes fastest.
Arguments:
- points: float32 [3, 131072], P(None, ('groups', 'gx')), parts along dimension 1, may hold values from 0 to 32
- noise_var: float32 [131072], P(('groups', 'gx')), parts along dimension 0, may hold values from 0.3 to 3
- probes: float32 [16, 131072], P(None, ('groups', 'gx')), parts along dimension 1, may hold values from -6 to 6
- pair_list: int32 [128, 2], P(('groups', 'gx')), parts along dimension 0, may hold values from 0 to 31, as said below
- counts: int32 [32], P(('groups', 'gx')), parts along dimension 0, may hold values from 2 to 4, as said below
Outputs:
- solution: float32 [16, 131072], P(None, ('groups', 'gx')), parts along dimension 1
- residual: float32 [16, 131072], P(None, ('groups', 'gx')), parts along dimension 1
There are 2 independent parts, one for each index of `groups`. A program takes and returns all parts, laid end to end along the dimension named above; each array names one. Nothing has to cross between parts.
Inputs may be any that keep to these rules, and one draw needn't show every extreme that they name: `pair_list`: rows k * 4 to (k + 1) * 4 - 1 belong to device k of gx: the owner is one of its blocks k * 2 to (k + 1) * 2 - 1 and the partner is owner + d with 0 <= d <= 1; the live rows of a device are distinct. `counts`: the live rows lead each device's rows.
All inputs are finite; a program needn't handle non-finite values.
Results may differ from a plain program's by a relative error of at most 0.0043.
Values may be sent and summed in bfloat16 or wider, within the bound.
No kernel may reach another device: no remote copies, remote signals or barrier semaphores. Data moves between devices by JAX's collectives and lax.ppermute only.
A program may use at most 256 MiB of HBM per device.

v0:
```python
import jax
import jax.numpy as jnp
from jax import lax
from jax.sharding import PartitionSpec as P

BLK = 2048
B_DEV = 2
ITERS = 3


support_radius = 0.5
kernel_scale = 0.25


def from_behind(value, axis, steps):
    count = lax.axis_size(axis)
    first, last = (max(0, -steps), min(count, count - steps))
    return lax.ppermute(value, axis, [(source, source + steps) for source in range(first, last)])


def wendland(left_points, right_points):
    squared = (left_points[0][:, None] - right_points[0][None, :]) ** 2
    squared = squared + (left_points[1][:, None] - right_points[1][None, :]) ** 2
    squared = squared + (left_points[2][:, None] - right_points[2][None, :]) ** 2
    distance = jnp.sqrt(squared) / support_radius
    remain = jnp.maximum(1.0 - distance, 0.0)
    values = kernel_scale * remain**4 * (4.0 * distance + 1.0)
    return values.astype(jnp.bfloat16)


def block_of(source, index):
    return lax.dynamic_slice_in_dim(source, index * BLK, BLK, 1)


def add_into(running, piece, index):
    old_part = lax.dynamic_slice_in_dim(running, index * BLK, BLK, 1)
    return lax.dynamic_update_slice_in_dim(running, old_part + piece, index * BLK, 1)


def times_transposed(vector_block, kernel_block):
    return lax.dot_general(
        vector_block, kernel_block, (((1,), (1,)), ((), ())), preferred_element_type=jnp.float32
    )


def stack_blocks(table, offset, nearby_points):
    built = []
    for slot_index in range(table.shape[0]):
        owner_at = table[slot_index, 0] - offset
        partner = table[slot_index, 1] - offset
        built.append(wendland(block_of(nearby_points, owner_at), block_of(nearby_points, partner)))
    return jnp.stack(built, axis=0)


def on_device(points, noise_var, probes, pair_list, counts):
    span_width = points.shape[1]
    first_block = lax.axis_index("gx") * B_DEV
    live_count = counts[0]
    upper_points = from_behind(points, "gx", -1)
    nearby_points = jnp.concatenate([points, upper_points], axis=1)
    own_stack = stack_blocks(pair_list, first_block, nearby_points)
    solution = jnp.zeros(probes.shape, jnp.float32)
    residual = probes
    direction = probes
    norm_now = lax.psum(jnp.sum(residual * residual, axis=1), "gx")
    for iteration in range(ITERS):
        rounded = direction.astype(jnp.bfloat16)
        upper_part = from_behind(rounded, "gx", -1)
        nearby = jnp.concatenate([rounded, upper_part], axis=1)
        running = jnp.zeros((direction.shape[0], 2 * span_width), jnp.float32)

        def own_slot(slot_index, running):
            owner_at = pair_list[slot_index, 0] - first_block
            partner = pair_list[slot_index, 1] - first_block
            kernel_block = own_stack[slot_index]
            running = add_into(
                running, times_transposed(block_of(nearby, partner), kernel_block), owner_at
            )

            def to_partner(running):
                piece = jnp.dot(
                    block_of(nearby, owner_at), kernel_block, preferred_element_type=jnp.float32
                )
                return add_into(running, piece, partner)

            return lax.cond(partner != owner_at, to_partner, lambda running: running, running)

        running = lax.fori_loop(0, live_count, own_slot, running)
        arrived = from_behind(running[:, span_width:].astype(jnp.bfloat16), "gx", 1).astype(
            jnp.float32
        )
        product = noise_var[None, :] * direction + (running[:, :span_width] + arrived)
        curvature = lax.psum(jnp.sum(direction * product, axis=1), "gx")
        step_size = norm_now / curvature
        solution = solution + step_size[:, None] * direction
        residual = residual - step_size[:, None] * product
        norm_next = lax.psum(jnp.sum(residual * residual, axis=1), "gx")
        direction = residual + (norm_next / norm_now)[:, None] * direction
        norm_now = norm_next
    return (solution, residual)


def solution(mesh):
    placed = (
        P(None, ("groups", "gx")),
        P(("groups", "gx")),
        P(None, ("groups", "gx")),
        P(("groups", "gx"), None),
        P(("groups", "gx")),
    )
    return jax.shard_map(
        on_device,
        mesh=mesh,
        in_specs=placed,
        out_specs=(P(None, ("groups", "gx")), P(None, ("groups", "gx"))),
        check_vma=False,
    )
```

profile of v0, /device:TPU:0, one launch (start us, length us, event | category | flops | bytes accessed | tf_op | source)
XLA Modules:
  0.0 502.2 jit_solution(3845000353345121769)
XLA Ops:
  12.1 29.2 %multiply_convert_fusion.2 = (bf16[1,2048,2048]{2,1,0:T(8,128)(2,1)}, bf16[1,2048,2048]{2,1,0:T(8,128)(2,1)}) fusion(f32[2048]{0:T(1024)S(1)} %bitcast.95, f32[2048]{0:T(1024)S(1)} %bitcast.96, f32[2048]{0:T(1024)S(1)} %bitcast.88, f32[2048]{0:T(1024)S(1)} %bitcast.89, f32[2048]{0:T(1024)S(1)} %bitcast.90, f32[2048]{0:T(1024)S(1)} %bitcast.91, ...), kind=kLoop, calls=%fused_computation.36 | loop fusion | flops 150994944 | bytes 16875520 | tf_op jit(solution)/shard_map/convert_element_type | solution.py:28
  41.3 29.2 %multiply_convert_fusion = (bf16[1,2048,2048]{2,1,0:T(8,128)(2,1)}, bf16[1,2048,2048]{2,1,0:T(8,128)(2,1)}) fusion(f32[2048]{0:T(1024)S(1)} %bitcast.83, f32[2048]{0:T(1024)S(1)} %bitcast.84, f32[2048]{0:T(1024)S(1)} %bitcast.75, f32[2048]{0:T(1024)S(1)} %bitcast.76, f32[2048]{0:T(1024)S(1)} %bitcast.77, f32[2048]{0:T(1024)S(1)} %bitcast.78, ...), kind=kLoop, calls=%fused_computation.34 | loop fusion | flops 150994944 | bytes 16875520 | tf_op jit(solution)/shard_map/convert_element_type | solution.py:28
  70.5 22.7 %pad_maximum_fusion = bf16[4,2048,2048]{2,1,0:T(8,128)(2,1)} fusion(bf16[1,2048,2048]{2,1,0:T(8,128)(2,1)} %get-tuple-element.268, bf16[1,2048,2048]{2,1,0:T(8,128)(2,1)} %get-tuple-element.269, bf16[1,2048,2048]{2,1,0:T(8,128)(2,1)} %get-tuple-element.270, bf16[1,2048,2048]{2,1,0:T(8,128)(2,1)} %get-tuple-element.271), kind=kLoop, calls=%fused_computation.33 | loop fusion | flops 50331648 | bytes 67108864 | tf_op jit(solution)/shard_map/stack | solution.py:52
  93.3 76.2 %while.30 = (s32[]{:T(128)}, f32[16,8192]{1,0:T(8,128)S(1)}, s32[]{:T(128)}, s32[4,2]{0,1:T(2,128)S(1)}, s32[]{:T(128)}, /*index=5*/bf16[16,8192]{1,0:T(8,128)(2...) while((s32[]{:T(128)}, f32[16,8192]{1,0:T(8,128)S(1)}, ...), condition=%wide.region_5.0_spmd, body=%wide.region_2.0_spmd.sunk | while | flops 268500992 | bytes 34210252 | solution.py:88
  96.2 8.2 %dynamic-slice_bitcast_fusion.6 = bf16[2048,2048]{1,0:T(8,128)(2,1)} fusion(bf16[4,2048,2048]{2,1,0:T(8,128)(2,1)} %get-tuple-element.446, s32[]{:T(128)S(6)} %select_n.98), kind=kLoop, calls=%fused_computation.4.clone.1 | loop fusion | bytes 16777220 | tf_op jit(solution)/shard_map/while/body/squeeze | solution.py:75
  104.4 5.6 %fusion.38 = f32[16,8192]{1,0:T(8,128)S(1)} fusion(f32[16,8192]{1,0:T(8,128)S(1)} %get-tuple-element.429, s32[]{:T(128)S(6)} %select_n.99, bf16[2048,2048]{1,0:T(8,128)(2,1)} %dynamic-slice_bitcast_fusion.6, bf16[16,8192]{1,0:T(8,128)(2,1)S(1)} %get-tuple-element.445, s32[]{:T(128)S(6)} %select_n.100), kind=kOutput, calls=%fused_computation.6.clone.1 | convolution fusion | flops 134250496 | bytes 8716296 | tf_op jit(solution)/shard_map/while/body/dot_general | solution.py:41
  112.7 8.2 %dynamic-slice_bitcast_fusion.6 = bf16[2048,2048]{1,0:T(8,128)(2,1)} fusion(bf16[4,2048,2048]{2,1,0:T(8,128)(2,1)} %get-tuple-element.446, s32[]{:T(128)S(6)} %select_n.98), kind=kLoop, calls=%fused_computation.4.clone.1 | loop fusion | bytes 16777220 | tf_op jit(solution)/shard_map/while/body/squeeze | solution.py:75
  133.8 8.2 %dynamic-slice_bitcast_fusion.6 = bf16[2048,2048]{1,0:T(8,128)(2,1)} fusion(bf16[4,2048,2048]{2,1,0:T(8,128)(2,1)} %get-tuple-element.446, s32[]{:T(128)S(6)} %select_n.98), kind=kLoop, calls=%fused_computation.4.clone.1 | loop fusion | bytes 16777220 | tf_op jit(solution)/shard_map/while/body/squeeze | solution.py:75
  154.9 8.2 %dynamic-slice_bitcast_fusion.6 = bf16[2048,2048]{1,0:T(8,128)(2,1)} fusion(bf16[4,2048,2048]{2,1,0:T(8,128)(2,1)} %get-tuple-element.446, s32[]{:T(128)S(6)} %select_n.98), kind=kLoop, calls=%fused_computation.4.clone.1 | loop fusion | bytes 16777220 | tf_op jit(solution)/shard_map/while/body/squeeze | solution.py:75
  174.3 35.6 %all-reduce = (f32[16]{0:T(128)S(1)}, f32[16]{0:T(128)S(1)}) all-reduce(f32[16]{0:T(128)S(1)} %get-tuple-element.177, f32[16]{0:T(128)S(1)} %get-tuple-element.176), channel_id=1, replica_groups=mesh['groups'=2,'gx'=16] {'gx'}, use_global_device_ids=true, to_apply=%region_1.0 | all-reduce | flops 32 | bytes 256 | tf_op jit(solution)/shard_map/psum | solution.py:65
  210.1 29.5 %psum.44 = f32[16]{0:T(128)S(1)} all-reduce(f32[16]{0:T(128)S(1)} %get-tuple-element.226), channel_id=1, replica_groups=mesh['groups'=2,'gx'=16] {'gx'}, use_global_device_ids=true, to_apply=%region_9.0 | all-reduce | flops 16 | bytes 128 | tf_op jit(solution)/shard_map/psum | solution.py:97
  243.0 75.9 %while.31 = (s32[]{:T(128)}, f32[16,8192]{1,0:T(8,128)S(1)}, s32[]{:T(128)}, s32[4,2]{0,1:T(2,128)S(1)}, s32[]{:T(128)}, /*index=5*/bf16[16,8192]{1,0:T(8,128)(2...) while((s32[]{:T(128)}, f32[16,8192]{1,0:T(8,128)S(1)}, ...), condition=%wide.region_13.0_spmd, body=%wide.region_10.0_spmd.sunk | while | flops 268500992 | bytes 34210252 | solution.py:88
  245.7 8.2 %dynamic-slice_bitcast_fusion.7 = bf16[2048,2048]{1,0:T(8,128)(2,1)} fusion(bf16[4,2048,2048]{2,1,0:T(8,128)(2,1)} %get-tuple-element.482, s32[]{:T(128)S(6)} %select_n.101), kind=kLoop, calls=%fused_computation.15.clone.1 | loop fusion | bytes 16777220 | tf_op jit(solution)/shard_map/while/body/squeeze | solution.py:75
  262.2 8.2 %dynamic-slice_bitcast_fusion.7 = bf16[2048,2048]{1,0:T(8,128)(2,1)} fusion(bf16[4,2048,2048]{2,1,0:T(8,128)(2,1)} %get-tuple-element.482, s32[]{:T(128)S(6)} %select_n.101), kind=kLoop, calls=%fused_computation.15.clone.1 | loop fusion | bytes 16777220 | tf_op jit(solution)/shard_map/while/body/squeeze | solution.py:75
  283.3 8.2 %dynamic-slice_bitcast_fusion.7 = bf16[2048,2048]{1,0:T(8,128)(2,1)} fusion(bf16[4,2048,2048]{2,1,0:T(8,128)(2,1)} %get-tuple-element.482, s32[]{:T(128)S(6)} %select_n.101), kind=kLoop, calls=%fused_computation.15.clone.1 | loop fusion | bytes 16777220 | tf_op jit(solution)/shard_map/while/body/squeeze | solution.py:75
  304.4 8.2 %dynamic-slice_bitcast_fusion.7 = bf16[2048,2048]{1,0:T(8,128)(2,1)} fusion(bf16[4,2048,2048]{2,1,0:T(8,128)(2,1)} %get-tuple-element.482, s32[]{:T(128)S(6)} %select_n.101), kind=kLoop, calls=%fused_computation.15.clone.1 | loop fusion | bytes 16777220 | tf_op jit(solution)/shard_map/while/body/squeeze | solution.py:75
  325.0 30.5 %psum.45 = f32[16]{0:T(128)S(1)} all-reduce(f32[16]{0:T(128)S(1)} %multiply_reduce_fusion.2), channel_id=1, replica_groups=mesh['groups'=2,'gx'=16] {'gx'}, use_global_device_ids=true, to_apply=%region_15.0 | all-reduce | flops 16 | bytes 128 | tf_op jit(solution)/shard_map/psum | solution.py:93
  355.7 29.5 %psum.46 = f32[16]{0:T(128)S(1)} all-reduce(f32[16]{0:T(128)S(1)} %get-tuple-element.222), channel_id=1, replica_groups=mesh['groups'=2,'gx'=16] {'gx'}, use_global_device_ids=true, to_apply=%region_17.0 | all-reduce | flops 16 | bytes 128 | tf_op jit(solution)/shard_map/psum | solution.py:97
  388.6 76.1 %while.32 = (s32[]{:T(128)}, f32[16,8192]{1,0:T(8,128)S(1)}, s32[]{:T(128)}, s32[4,2]{0,1:T(2,128)S(1)}, s32[]{:T(128)}, /*index=5*/bf16[16,8192]{1,0:T(8,128)(2...) while((s32[]{:T(128)}, f32[16,8192]{1,0:T(8,128)S(1)}, ...), condition=%wide.region_21.0_spmd, body=%wide.region_18.0_spmd.sunk | while | flops 268500992 | bytes 34210252 | solution.py:88
  391.4 8.2 %dynamic-slice_bitcast_fusion.8 = bf16[2048,2048]{1,0:T(8,128)(2,1)} fusion(bf16[4,2048,2048]{2,1,0:T(8,128)(2,1)} %get-tuple-element.518, s32[]{:T(128)S(6)} %select_n.104), kind=kLoop, calls=%fused_computation.26.clone.1 | loop fusion | bytes 16777220 | tf_op jit(solution)/shard_map/while/body/squeeze | solution.py:75
  407.9 8.2 %dynamic-slice_bitcast_fusion.8 = bf16[2048,2048]{1,0:T(8,128)(2,1)} fusion(bf16[4,2048,2048]{2,1,0:T(8,128)(2,1)} %get-tuple-element.518, s32[]{:T(128)S(6)} %select_n.104), kind=kLoop, calls=%fused_computation.26.clone.1 | loop fusion | bytes 16777220 | tf_op jit(solution)/shard_map/while/body/squeeze | solution.py:75
  429.0 8.2 %dynamic-slice_bitcast_fusion.8 = bf16[2048,2048]{1,0:T(8,128)(2,1)} fusion(bf16[4,2048,2048]{2,1,0:T(8,128)(2,1)} %get-tuple-element.518, s32[]{:T(128)S(6)} %select_n.104), kind=kLoop, calls=%fused_computation.26.clone.1 | loop fusion | bytes 16777220 | tf_op jit(solution)/shard_map/while/body/squeeze | solution.py:75
  450.1 8.2 %dynamic-slice_bitcast_fusion.8 = bf16[2048,2048]{1,0:T(8,128)(2,1)} fusion(bf16[4,2048,2048]{2,1,0:T(8,128)(2,1)} %get-tuple-element.518, s32[]{:T(128)S(6)} %select_n.104), kind=kLoop, calls=%fused_computation.26.clone.1 | loop fusion | bytes 16777220 | tf_op jit(solution)/shard_map/while/body/squeeze | solution.py:75
  470.8 30.5 %psum.47 = f32[16]{0:T(128)S(1)} all-reduce(f32[16]{0:T(128)S(1)} %multiply_reduce_fusion), channel_id=1, replica_groups=mesh['groups'=2,'gx'=16] {'gx'}, use_global_device_ids=true, to_apply=%region_23.0 | all-reduce | flops 16 | bytes 128 | tf_op jit(solution)/shard_map/psum | solution.py:93
  (88 shorter events, 156.6 us)
Async XLA Ops:
  0.6 11.1 %collective-permute-start.1 = (f32[3,4096]{1,0:T(4,128)}, f32[3,4096]{1,0:T(4,128)S(1)}, u32[]{:S(2)}, u32[]{:S(2)}) collective-permute-start(f32[3,4096]{1,0:T(4,128)} %param.17), channel_id=1, source_target_pairs={{1,0},{2,1},{3,2},{4,3},{5,4},{6,5},{7,6},{8,7},{9,8},{10,9},{11,1... | collective-permute-start | bytes 147464 | tf_op jit(solution)/shard_map/ppermute | solution.py:18
  2.9 90.3 %collective-permute-start = (bf16[16,4096]{1,0:T(8,128)(2,1)S(1)}, bf16[16,4096]{1,0:T(8,128)(2,1)S(1)}, u32[]{:S(2)}, u32[]{:S(2)}) collective-permute-start(bf16[16,4096]{1,0:T(8,128)(2,1)S(1)} %convert_element_type.70), channel_id=1, source_target_pairs={{1,0},{2,1},{3,2},{4,3},{5,4},{6,5},{7,6},{8,7},{9,8},{10,9},{11,1... | collective-permute-start | bytes 393224 | tf_op jit(solution)/shard_map/ppermute | solution.py:18
  70.5 22.8 %copy-start.2 = (s32[4,2]{0,1:T(2,128)S(1)}, s32[4,2]{0,1:T(2,128)}, u32[]{:S(2)}) copy-start(s32[4,2]{0,1:T(2,128)} %param.20) | copy-start | bytes 100
  93.3 80.8 %copy-start = (f32[16,4096]{1,0:T(8,128)S(1)}, f32[16,4096]{1,0:T(8,128)}, u32[]{:S(2)}) copy-start(f32[16,4096]{1,0:T(8,128)} %param.19) | copy-start | bytes 786436
  93.3 80.8 %copy-start.1 = (f32[4096]{0:T(1024)S(1)}, f32[4096]{0:T(1024)}, u32[]{:S(2)}) copy-start(f32[4096]{0:T(1024)} %param.18) | copy-start | bytes 49156
  169.5 4.6 collective-permute-start.2
  239.7 3.2 collective-permute-start.3
  319.0 5.8 %collective-permute-start.4 = (bf16[16,4096]{1,0:T(8,128)(2,1)S(1)}, bf16[16,4096]{1,0:T(8,128)(2,1)S(1)}, u32[]{:S(2)}, u32[]{:S(2)}) collective-permute-start(bf16[16,4096]{1,0:T(8,128)(2,1)S(1)} %slice.213), channel_id=1, source_target_pairs={{0,1},{1,2},{2,3},{3,4},{4,5},{5,6},{6,7},{7,8},{8,9},{9,10},{10,1... | collective-permute-start | bytes 393224 | tf_op jit(solution)/shard_map/ppermute | solution.py:18
  385.3 3.2 collective-permute-start.5
  464.7 5.8 %collective-permute-start.6 = (bf16[16,4096]{1,0:T(8,128)(2,1)S(1)}, bf16[16,4096]{1,0:T(8,128)(2,1)S(1)}, u32[]{:S(2)}, u32[]{:S(2)}) collective-permute-start(bf16[16,4096]{1,0:T(8,128)(2,1)S(1)} %slice.212), channel_id=1, source_target_pairs={{0,1},{1,2},{2,3},{3,4},{4,5},{5,6},{6,7},{7,8},{8,9},{9,10},{10,1... | collective-permute-start | bytes 393224 | tf_op jit(solution)/shard_map/ppermute | solution.py:18
where the time goes:
time: 503 us; the launch traced here: 502 us
  blocking collectives  155 us (31%)
  local copies, waits for them, and re-layouts  110 us (22%)
  matrix products  95.3 us (19%)
  other arithmetic  84.4 us (17%)
  loops' own time  26.2 us (5%)
  starting transfers between devices  18.5 us (4%)
  waiting for transfers between devices  6.77 us (1%)
  between operations  5.85 us (1%)
    squeeze x12, local copies, waits for them, and re-layouts, own_slot(): kernel_block = own_stack[slot_index]  99 us
    dot_general x12, matrix products, times_transposed(): lax.dot_general(vector_block, kernel_block, (((1,), (1,)), ((), ())), pre...  67.7 us
    psum x2, blocking collectives, on_device(): curvature = lax.psum(jnp.sum(direction * product, axis=1), 'gx')  60.9 us
    psum x2, blocking collectives, on_device(): norm_next = lax.psum(jnp.sum(residual * residual, axis=1), 'gx')  59 us
    convert_element_type x2, other arithmetic, wendland(): return values.astype(jnp.bfloat16)  58.4 us
    psum x1, blocking collectives, on_device(): norm_now = lax.psum(jnp.sum(residual * residual, axis=1), 'gx')  35.6 us
    dot_general x6, matrix products, to_partner(): jnp.dot(block_of(nearby, owner_at), kernel_block, preferred_element_type=...  27.5 us
    another operation x3, loops' own time, on_device(): running = lax.fori_loop(0, live_count, own_slot, running)  26.2 us
  transfers between devices with their start and end apart: 7, of which 5 were waited for; matrix products, arithmetic and copies ran while one was open for 17% of the time, Pallas kernels for 0%

commit v1 on v0

v1 whole, which is shorter than its diff:
```python
import functools

import jax
import jax.numpy as jnp
from jax import lax
from jax.experimental import pallas as pl
from jax.experimental.pallas import tpu as pltpu
from jax.sharding import PartitionSpec as P

BLK = 2048
STRIP = 256
STRIPS = BLK // STRIP
SUB = 128
SUBS = BLK // SUB
OFF_W = 768
OFF_SUBS = OFF_W // SUB
DIAG_W = 512
N_PROBES = 16
CHUNK = 16
MIB = 1 << 20

VMEM = pl.BlockSpec(memory_space=pltpu.VMEM)
SMEM = pl.BlockSpec(memory_space=pltpu.SMEM)

f32 = jnp.float32
bf16 = jnp.bfloat16

T_LIVE, T_EXTRA, T_START, T_END = 0, 1, 8, 16
T_SIZE = 24


def nt(left, right):
    return lax.dot_general(left, right, (((1,), (1,)), ((), ())), preferred_element_type=f32)


def nn(left, right):
    return jnp.dot(left, right, preferred_element_type=f32)


def split2(value):
    high = value.astype(bf16)
    low = (value - high.astype(f32)).astype(bf16)
    return jnp.concatenate([high, low], axis=0)


def halves(value):
    n = value.shape[0] // 2
    return value[:n] + value[n:]


def split3(value):
    high = value.astype(bf16).astype(f32)
    rest = value - high
    mid = rest.astype(bf16).astype(f32)
    return high, mid, rest - mid


def sort_kernel(blk, pts_ref, nv_ref, pr_ref, out_ref, perm_ref, col_ref, yb_ref, key_ref):
    cols = pl.ds(blk * BLK, BLK)
    y_row = pts_ref[1:2, cols]
    lane = lax.broadcasted_iota(jnp.int32, (1, BLK), 1)
    key_row = (y_row * 4096.0).astype(jnp.int32) * BLK + lane
    for c in range(SUBS):
        piece = jnp.broadcast_to(y_row[:, c * SUB : (c + 1) * SUB], (SUB, SUB)).T
        sub = lax.broadcasted_iota(jnp.int32, (SUB, SUB), 0) + c * SUB
        key_ref[c * SUB : (c + 1) * SUB, :] = (piece * 4096.0).astype(jnp.int32) * BLK + sub
    keys = jnp.broadcast_to(key_row, (8, BLK))

    def count(i, acc):
        mine = key_ref[pl.ds(pl.multiple_of(i * 8, 8), 8), :]
        mine = jnp.concatenate([mine] * SUBS, axis=1)
        return acc + jnp.where(mine < keys, 1, 0)

    acc = lax.fori_loop(0, BLK // 8, count, jnp.zeros((8, BLK), jnp.int32), unroll=8)
    rank = jnp.sum(acc, axis=0, keepdims=True)
    group = lax.shift_right_logical(rank, 8)
    within = jnp.bitwise_and(rank, STRIP - 1)

    pr = pr_ref[:, cols]
    aux = jnp.concatenate(
        [pts_ref[0:3, cols] * 2.0, nv_ref[:, cols], jnp.zeros((4, BLK), f32)], axis=0
    )
    data = jnp.concatenate([*split3(pr), *split3(aux), jnp.zeros((8, BLK), f32)], axis=0).astype(bf16)
    place = lax.broadcasted_iota(jnp.int32, (STRIP, SUB), 0).astype(f32).astype(bf16)
    one = jnp.ones((STRIP, SUB), bf16)
    zero = jnp.zeros((STRIP, SUB), bf16)
    for g in range(STRIPS):
        marked = jnp.where(group == g, within, -1).astype(f32).astype(bf16)
        for c in range(SUBS):
            hit = jnp.broadcast_to(marked[:, c * SUB : (c + 1) * SUB], (STRIP, SUB)) == place
            perm_ref[g * STRIP : (g + 1) * STRIP, c * SUB : (c + 1) * SUB] = jnp.where(hit, one, zero)
        got = nt(data, perm_ref[g * STRIP : (g + 1) * STRIP, :])
        here = slice(g * STRIP, (g + 1) * STRIP)
        out_ref[0:16, here] = (got[0:16] + got[16:32]) + got[32:48]
        out_ref[16:24, here] = (got[48:56] + got[56:64]) + got[64:72]
    for axis in range(3):
        for c in range(SUBS):
            here = slice(c * SUB, (c + 1) * SUB)
            row = out_ref[16 + axis : 17 + axis, here]
            col_ref[axis, here, :] = jnp.broadcast_to(row, (SUB, SUB)).T
    bounds(out_ref, yb_ref)


def bounds(side_ref, yb_ref):
    for c in range(SUBS):
        row = side_ref[17:18, c * SUB : (c + 1) * SUB]
        yb_ref[c] = jnp.min(row)
        yb_ref[SUBS + c] = jnp.max(row)


def sort_block(blk, points, noise, probes):
    return pl.pallas_call(
        functools.partial(sort_kernel, blk),
        out_shape=(
            pltpu.VMEM((24, BLK), f32),
            pltpu.VMEM((BLK, BLK), bf16),
            pltpu.VMEM((3, BLK, SUB), f32),
            jax.ShapeDtypeStruct((2 * SUBS,), f32),
        ),
        in_specs=[VMEM] * 3,
        out_specs=(VMEM, VMEM, VMEM, SMEM),
        scratch_shapes=[pltpu.VMEM((BLK, SUB), jnp.int32)],
        compiler_params=pltpu.CompilerParams(vmem_limit_bytes=12 * MIB),
        cost_estimate=pl.CostEstimate(flops=2 * 80 * BLK * BLK, bytes_accessed=MIB, transcendentals=0),
        name="sort_block",
    )(points, noise, probes)


def live_flag(pair_ref, count_ref, local, ahead):
    flag = jnp.int32(0)
    for s in range(pair_ref.shape[0]):
        owner = pair_ref[s, 0]
        match = (
            (jnp.int32(s) < count_ref[0])
            & (jnp.bitwise_and(owner, 1) == local)
            & (pair_ref[s, 1] - owner == ahead)
        )
        flag = jnp.where(match, jnp.int32(1), flag)
    return flag


def fill_table(tab_ref, base, flag, own_ref, other_ref, diag):
    slack = 1.0 + 1.0 / 1024.0

    def one_strip(i, extra):
        low = jnp.minimum(own_ref[2 * i], own_ref[2 * i + 1]) - slack
        high = jnp.maximum(own_ref[SUBS + 2 * i], own_ref[SUBS + 2 * i + 1]) + slack
        first = jnp.int32(0)
        end = jnp.int32(SUBS)
        for j in range(SUBS):
            first = first + jnp.where(other_ref[SUBS + j] <= low, 1, 0)
            end = end - jnp.where(other_ref[j] >= high, 1, 0)
        if diag:
            start = 2 * i + DIAG_W // SUB - OFF_SUBS
        else:
            start = jnp.minimum(first, SUBS - OFF_SUBS)
        tab_ref[base + T_START + i] = start
        tab_ref[base + T_END + i] = end
        return extra + jnp.maximum(end - (start + OFF_SUBS), 0)

    extra = lax.fori_loop(0, STRIPS, one_strip, jnp.int32(0))
    tab_ref[base + T_LIVE] = flag
    tab_ref[base + T_EXTRA] = extra * flag


def kernel_values(col_ref, row_at, rows):
    width = rows[0].shape[1]
    squared = None
    for axis in range(3):
        mine = col_ref[axis, pl.ds(row_at, CHUNK), :]
        diff = jnp.concatenate([mine] * (width // SUB), axis=1) - rows[axis]
        part = diff * diff
        squared = part if squared is None else squared + part
    squared = jnp.maximum(squared, 1e-30)
    q = squared * lax.rsqrt(squared)
    t = jnp.maximum(1.0 - q, 0.0)
    t2 = t * t
    return ((t2 * t2) * (q + 0.25)).astype(bf16)


def build_strip(store, col_ref, strip, side_ref, start, width):
    at = pl.ds(start, width)
    rows = [jnp.broadcast_to(side_ref[16 + axis : 17 + axis, at], (CHUNK, width)) for axis in range(3)]

    def chunk(i, carry):
        row_at = pl.multiple_of(strip * STRIP + i * CHUNK, CHUNK)
        store(pl.multiple_of(i * CHUNK, CHUNK), kernel_values(col_ref, row_at, rows))
        return carry

    lax.fori_loop(0, STRIP // CHUNK, chunk, 0, unroll=2)


def build_off(k_ref, tab_ref, base, col_ref, side_ref):
    for i in range(STRIPS):
        start = pl.multiple_of(tab_ref[base + T_START + i] * SUB, SUB)
        for h in range(OFF_W // STRIP):

            def store(at, value, i=i, h=h):
                k_ref[i, pl.ds(at, CHUNK), h * STRIP : (h + 1) * STRIP] = value

            build_strip(store, col_ref, i, side_ref, start + h * STRIP, STRIP)


def build_diag(k_ref, col_ref, side_ref):
    for i in range(STRIPS):
        for h in range(min(DIAG_W, BLK - i * STRIP) // STRIP):

            def store(at, value, i=i, h=h):
                k_ref[i, pl.ds(at, CHUNK), h * STRIP : (h + 1) * STRIP] = value

            build_strip(store, col_ref, i, side_ref, (i + h) * STRIP, STRIP)


def to_owner(k_ref, tab_ref, base, v_col, acc_row):
    for i in range(STRIPS):
        start = pl.multiple_of(tab_ref[base + T_START + i] * SUB, SUB)
        acc_row[:, i * STRIP : (i + 1) * STRIP] += halves(nt(v_col[:, pl.ds(start, OFF_W)], k_ref[i]))


def to_partner(k_ref, tab_ref, base, v_row, acc_col):
    for i in range(STRIPS):
        start = pl.multiple_of(tab_ref[base + T_START + i] * SUB, SUB)
        acc_col[:, pl.ds(start, OFF_W)] += halves(nn(v_row[:, i * STRIP : (i + 1) * STRIP], k_ref[i]))


def diag_products(k_ref, v_ref, acc_ref):
    for i in range(STRIPS):
        width = min(DIAG_W, BLK - i * STRIP)
        here = slice(i * STRIP, (i + 1) * STRIP)
        acc_ref[:, here] += halves(nt(v_ref[:, i * STRIP : i * STRIP + width], k_ref[i, :, :width]))
        if width > STRIP:
            after = slice((i + 1) * STRIP, i * STRIP + width)
            acc_ref[:, after] += halves(nn(v_ref[:, here], k_ref[i, :, STRIP:width]))


def extra_tiles(tab_ref, base, col_ref, side_ref, tile_ref, v_row, v_col, acc_row, acc_col):
    @pl.when(tab_ref[base + T_EXTRA] > 0)
    def _():
        def strip(i, carry):
            here = pl.ds(pl.multiple_of(i * STRIP, STRIP), STRIP)

            def tile(j, carry):
                there = pl.ds(pl.multiple_of(j * SUB, SUB), SUB)

                def store(at, value):
                    tile_ref[pl.ds(at, CHUNK), :] = value

                build_strip(store, col_ref, i, side_ref, pl.multiple_of(j * SUB, SUB), SUB)
                if acc_row is not None:
                    acc_row[:, here] += halves(nt(v_col[:, there], tile_ref[...]))
                if acc_col is not None:
                    acc_col[:, there] += halves(nn(v_row[:, here], tile_ref[...]))
                return carry

            return lax.fori_loop(
                tab_ref[base + T_START + i] + OFF_SUBS, tab_ref[base + T_END + i], tile, carry
            )

        lax.fori_loop(0, STRIPS, strip, 0)


TILE = pltpu.VMEM((STRIP, SUB), bf16)
SPLIT = pltpu.VMEM((2 * N_PROBES, BLK), bf16)
FIELD = (N_PROBES, BLK)


def call(body, outs, ins, out_specs, scratch, flops, name, limit=12):
    def run(*args):
        return pl.pallas_call(
            body,
            out_shape=outs,
            in_specs=ins,
            out_specs=out_specs,
            scratch_shapes=scratch,
            compiler_params=pltpu.CompilerParams(vmem_limit_bytes=limit * MIB),
            cost_estimate=pl.CostEstimate(flops=flops, bytes_accessed=MIB, transcendentals=0),
            name=name,
        )(*args)

    return run


def halo_build_kernel(pair, count, yb1, s1, col1, halo, k12, tab, acc1, back, yb2, tile, v1, v2):
    bounds(halo, yb2)
    fill_table(tab, 0, live_flag(pair, count, 1, 1), yb1, yb2, False)
    acc1[...] = jnp.zeros(FIELD, f32)
    back[...] = jnp.zeros(FIELD, f32)

    @pl.when(tab[T_LIVE] > 0)
    def _():
        v1[...] = split2(s1[0:16, :])
        v2[...] = split2(halo[0:16, :])
        build_off(k12, tab, 0, col1, halo)
        to_partner(k12, tab, 0, v1, back)
        to_owner(k12, tab, 0, v2, acc1)
        extra_tiles(tab, 0, col1, halo, tile, v1, v2, acc1, back)


def local_products(tab, k00, k01, k11, s0, s1, col0, col1, tile, v0, v1, acc0, acc1):
    @pl.when(tab[0 * T_SIZE + T_LIVE] > 0)
    def _():
        diag_products(k00, v0, acc0)
        extra_tiles(tab, 0 * T_SIZE, col0, s0, tile, v0, v0, acc0, acc0)

    @pl.when(tab[1 * T_SIZE + T_LIVE] > 0)
    def _():
        to_owner(k01, tab, 1 * T_SIZE, v1, acc0)
        to_partner(k01, tab, 1 * T_SIZE, v0, acc1)
        extra_tiles(tab, 1 * T_SIZE, col0, s1, tile, v0, v1, acc0, acc1)

    @pl.when(tab[2 * T_SIZE + T_LIVE] > 0)
    def _():
        diag_products(k11, v1, acc1)
        extra_tiles(tab, 2 * T_SIZE, col1, s1, tile, v1, v1, acc1, acc1)


def own_build_kernel(
    pair, count, yb0, yb1, s0, s1, col0, col1, acc1_in, k00, k01, k11, tab, acc0, acc1, tile, v0, v1
):
    fill_table(tab, 0 * T_SIZE, live_flag(pair, count, 0, 0), yb0, yb0, True)
    fill_table(tab, 1 * T_SIZE, live_flag(pair, count, 0, 1), yb0, yb1, False)
    fill_table(tab, 2 * T_SIZE, live_flag(pair, count, 1, 0), yb1, yb1, True)
    acc0[...] = jnp.zeros(FIELD, f32)
    acc1[...] = acc1_in[...]
    v0[...] = split2(s0[0:16, :])
    v1[...] = split2(s1[0:16, :])

    @pl.when(tab[0 * T_SIZE + T_LIVE] > 0)
    def _():
        build_diag(k00, col0, s0)

    @pl.when(tab[1 * T_SIZE + T_LIVE] > 0)
    def _():
        build_off(k01, tab, 1 * T_SIZE, col0, s1)

    @pl.when(tab[2 * T_SIZE + T_LIVE] > 0)
    def _():
        build_diag(k11, col1, s1)

    local_products(tab, k00, k01, k11, s0, s1, col0, col1, tile, v0, v1, acc0, acc1)


def own_apply_kernel(tab, k00, k01, k11, s0, s1, col0, col1, w0, w1, acc0, acc1, tile, v0, v1):
    acc0[...] = jnp.zeros(FIELD, f32)
    acc1[...] = jnp.zeros(FIELD, f32)
    v0[...] = split2(w0[0:16, :])
    v1[...] = split2(w1[0:16, :])
    local_products(tab, k00, k01, k11, s0, s1, col0, col1, tile, v0, v1, acc0, acc1)


def inner(left, right):
    product = left * right
    return jnp.sum(product, axis=1, keepdims=True)


def finish_kernel(
    level, tab, k12, s0, s1, col1, halo, halo_w, acc0, acc1, arrived, w0, w1, mom_in, n0, n1, back, mom, tile, v1, v2, acc
):
    live = tab[T_LIVE] > 0
    acc[...] = acc1[...]
    if level > 1:

        @pl.when(live)
        def _():
            v2[...] = split2(halo_w[0:16, :])
            to_owner(k12, tab, 0, v2, acc)
            extra_tiles(tab, 0, col1, halo, tile, None, v2, acc, None)

    before0 = w0[0:16, :]
    before1 = w1[0:16, :]
    next1 = s1[19:20, :] * before1 + acc[...]
    n1[...] = next1
    if level < 3:
        back[...] = jnp.zeros(FIELD, f32)

        @pl.when(live)
        def _():
            v1[...] = split2(next1)
            to_partner(k12, tab, 0, v1, back)
            extra_tiles(tab, 0, col1, halo, tile, v1, None, None, back)

    next0 = s0[19:20, :] * before0 + (acc0[...] + arrived[...])
    n0[...] = next0
    lane = lax.broadcasted_iota(jnp.int32, (N_PROBES, SUB), 1)
    cross = inner(before0, next0) + inner(before1, next1)
    own = inner(next0, next0) + inner(next1, next1)
    total = jnp.where(lane == 2 * level - 1, cross, jnp.where(lane == 2 * level, own, 0.0))
    if level == 1:
        total = jnp.where(lane == 0, inner(before0, before0) + inner(before1, before1), total)
    else:
        total = total + mom_in[...]
    mom[...] = total


def unsort_kernel(perm, wa, wb, wc, out):
    stacked = jnp.concatenate([split2(wa[...]), split2(wb[...]), split2(wc[...])], axis=0)
    for c in range(BLK // STRIP):
        here = slice(c * STRIP, (c + 1) * STRIP)
        got = nn(stacked, perm[:, here])
        for k in range(3):
            out[16 * k : 16 * (k + 1), here] = halves(got[32 * k : 32 * (k + 1)])


def combine_kernel(mom, probes, u0, u1, sol, res):
    lane = lax.broadcasted_iota(jnp.int32, (N_PROBES, SUB), 1)
    mu = [jnp.sum(jnp.where(lane == k, mom[...], 0.0), axis=1, keepdims=True) for k in range(7)]

    def form(left, right, shift):
        total = None
        for i, a in enumerate(left):
            for j, b in enumerate(right):
                part = (a * b) * mu[i + j + shift]
                total = part if total is None else total + part
        return total

    one = jnp.ones((N_PROBES, 1), f32)
    d = [one]
    r = [one]
    s = []
    rr = mu[0]
    for it in range(3):
        step = rr / form(d, d, 1)
        moved = [step * v for v in d]
        s = [a + b for a, b in zip(s + [0.0] * (len(d) - len(s)), moved)]
        r = [r[0]] + [(r[i] if i < len(r) else 0.0) - moved[i - 1] for i in range(1, len(moved) + 1)]
        if it < 2:
            new = form(r, r, 0)
            ratio = new / rr
            d = [r[i] + (ratio * d[i] if i < len(d) else 0.0) for i in range(len(r))]
            rr = new
    for b, u in ((0, u0), (1, u1)):
        here = slice(b * BLK, (b + 1) * BLK)
        w = [probes[:, here], u[0:16, :], u[16:32, :], u[32:48, :]]
        sol[:, here] = (s[0] * w[0] + s[1] * w[1]) + s[2] * w[2]
        res[:, here] = ((r[0] * w[0] + r[1] * w[1]) + r[2] * w[2]) + r[3] * w[3]


def from_behind(value, axis, steps):
    count = lax.axis_size(axis)
    first, last = (max(0, -steps), min(count, count - steps))
    return lax.ppermute(value, axis, [(source, source + steps) for source in range(first, last)])


def sum_over(value, axis):
    count = lax.axis_size(axis)
    if count & (count - 1):
        return lax.psum(value, axis)
    step = 1
    while step < count:
        value = value + lax.ppermute(value, axis, [(k, k ^ step) for k in range(count)])
        step *= 2
    return value


def on_device(points, noise_var, probes, pair_list, counts):
    noise = noise_var.reshape(1, -1)
    field = pltpu.VMEM(FIELD, f32)
    s0, p0, col0, yb0 = sort_block(0, points, noise, probes)
    halo = from_behind(s0, "gx", -1)
    s1, p1, col1, yb1 = sort_block(1, points, noise, probes)

    off = pltpu.VMEM((STRIPS, STRIP, OFF_W), bf16)
    diag = pltpu.VMEM((STRIPS, STRIP, DIAG_W), bf16)
    k12, tabc, acc1, back = call(
        halo_build_kernel,
        (off, jax.ShapeDtypeStruct((T_SIZE,), jnp.int32), field, field),
        [SMEM, SMEM, SMEM, VMEM, VMEM, VMEM],
        (VMEM, SMEM, VMEM, VMEM),
        [pltpu.SMEM((2 * SUBS,), f32), TILE, SPLIT, SPLIT],
        2 * 10**9,
        "halo_build",
    )(pair_list, counts, yb1, s1, col1, halo)
    arrived = from_behind(back, "gx", 1)
    k00, k01, k11, tabb, acc0, acc1 = call(
        own_build_kernel,
        (diag, off, diag, jax.ShapeDtypeStruct((3 * T_SIZE,), jnp.int32), field, field),
        [SMEM, SMEM, SMEM, SMEM, VMEM, VMEM, VMEM, VMEM, VMEM],
        (VMEM, VMEM, VMEM, SMEM, VMEM, VMEM),
        [TILE, SPLIT, SPLIT],
        6 * 10**9,
        "own_build",
    )(pair_list, counts, yb0, yb1, s0, s1, col0, col1, acc1)

    w0, w1 = s0, s1
    halo_w = halo
    mom = jnp.zeros((N_PROBES, SUB), f32)
    kept = []
    for level in range(1, 4):
        w0, w1, back, mom = call(
            functools.partial(finish_kernel, level),
            (field, field, field, pltpu.VMEM((N_PROBES, SUB), f32)),
            [SMEM] + [VMEM] * 12,
            (VMEM,) * 4,
            [TILE, SPLIT, SPLIT, pltpu.VMEM(FIELD, f32)],
            10**9,
            "finish",
        )(tabc, k12, s0, s1, col1, halo, halo_w, acc0, acc1, arrived, w0, w1, mom)
        kept.append((w0, w1))
        if level < 3:
            arrived = from_behind(back, "gx", 1)
            halo_w = from_behind(w0, "gx", -1)
            acc0, acc1 = call(
                own_apply_kernel,
                (field, field),
                [SMEM] + [VMEM] * 9,
                (VMEM, VMEM),
                [TILE, SPLIT, SPLIT],
                2 * 10**9,
                "own_apply",
            )(tabb, k00, k01, k11, s0, s1, col0, col1, w0, w1)
    total = sum_over(mom, "gx")
    given = []
    for b, perm in ((0, p0), (1, p1)):
        given.append(
            call(
                unsort_kernel,
                pltpu.VMEM((3 * N_PROBES, BLK), f32),
                [VMEM] * 4,
                VMEM,
                [],
                2 * 96 * BLK * BLK,
                "unsort",
            )(perm, *[pair[b] for pair in kept])
        )
    return call(
        combine_kernel,
        (jax.ShapeDtypeStruct(probes.shape, f32),) * 2,
        [VMEM] * 4,
        (VMEM, VMEM),
        [],
        10**6,
        "combine",
    )(total, probes, *given)


def solution(mesh):
    placed = (
        P(None, ("groups", "gx")),
        P(("groups", "gx")),
        P(None, ("groups", "gx")),
        P(("groups", "gx"), None),
        P(("groups", "gx")),
    )
    return jax.shard_map(
        on_device,
        mesh=mesh,
        in_specs=placed,
        out_specs=(P(None, ("groups", "gx")), P(None, ("groups", "gx"))),
        check_vma=False,
    )
```

time: 503 us -> 98.3 us (0.20)
  blocking collectives: 155 us -> 0 us
  local copies, waits for them, and re-layouts: 110 us -> 9.05 us
  matrix products: 95.3 us -> 0 us
  other arithmetic: 84.4 us -> 0.01 us
  Pallas kernels: 0 us -> 59.7 us
  loops' own time: 26.2 us -> 0 us
  starting transfers between devices: 18.5 us -> 24.2 us
    psum x5 -> x0, blocking collectives: 155 us -> none  [the longest x2 60.9 us: on_device(): curvature = lax.psum(jnp.sum(direction * product, axis=1), 'gx')]
    squeeze x12 -> x0, local copies, waits for them, and re-layouts: 99 us -> none  [own_slot(): kernel_block = own_stack[slot_index]]
    dot_general x18 -> x0, matrix products: 95.3 us -> none  [the longest x12 67.7 us: times_transposed(): lax.dot_general(vector_block, kernel_block, (((1,), (1,)), ((), ())), pre...]
    pallas_call x0 -> x12, Pallas kernels: none -> 59.7 us  [the longest x10 48.3 us: run(): pl.pallas_call(body, out_shape=outs, in_specs=ins, out_specs=out_specs, s...]
    convert_element_type x5 -> x0, other arithmetic: 59.6 us -> none  [the longest x2 58.4 us: wendland(): return values.astype(jnp.bfloat16)]
    another operation x15 -> x0, loops' own time: 26.2 us -> none  [the longest x3 26.2 us: on_device(): running = lax.fori_loop(0, live_count, own_slot, running)]
    another operation x1 -> x0, other arithmetic: 22.7 us -> none  [stack_blocks(): return jnp.stack(built, axis=0)]
    ppermute x0 -> x4, starting transfers between devices: none -> 10.6 us  [sum_over(): lax.ppermute(value, axis, [(k, k ^ step) for k in range(count)])]
  transfers between devices with their start and end apart: 7 -> 10, of which waited for: 5 -> 4; matrix products, arithmetic and copies ran while one was open for 17% -> 1% of each run, Pallas kernels for 0% -> 39%
where the time goes in v1:
time: 98.3 us; the launch traced here: 97.6 us
  Pallas kernels  59.7 us (61%)
  starting transfers between devices  24.2 us (25%)
  local copies, waits for them, and re-layouts  9.05 us (9%)
  waiting for transfers between devices  3.19 us (3%)
  between operations  1.46 us (1%)
    pallas_call x10, Pallas kernels, run(): pl.pallas_call(body, out_shape=outs, in_specs=ins, out_specs=out_specs, s...  48.3 us
    ppermute x6, starting transfers between devices, from_behind(): lax.ppermute(value, axis, [(source, source + steps) for source in range(f...  13.6 us
    pallas_call x2, Pallas kernels, sort_block(): pl.pallas_call(functools.partial(sort_kernel, blk), out_shape=(pltpu.VMEM...  11.4 us
    ppermute x4, starting transfers between devices, sum_over(): lax.ppermute(value, axis, [(k, k ^ step) for k in range(count)])  10.6 us
    unnamed x21, local copies, waits for them, and re-layouts  9.05 us
    ppermute x4, waiting for transfers between devices, sum_over(): lax.ppermute(value, axis, [(k, k ^ step) for k in range(count)])  3.14 us
  transfers between devices with their start and end apart: 10, of which 4 were waited for; matrix products, arithmetic and copies ran while one was open for 1% of the time, Pallas kernels for 39%

profile of v1, /device:TPU:0, one launch (start us, length us, event | category | flops | bytes accessed | tf_op | source)
XLA Modules:
  0.0 97.6 jit_solution(15553033061347668969)
XLA Ops:
  3.1 5.7 %sort_block.3 = (f32[24,2048]{1,0:T(8,128)S(1)}, bf16[2048,2048]{1,0:T(8,128)(2,1)S(1)}, f32[3,2048,128]{2,1,0:T(8,128)S(1)}, f32[32]{0:T(128)S(1)}) custom-call(f32[3,4096]{1,0:T(4,128)S(1)} %copy-done.4, f32[1,4096]{1,0:T(1,128)S(1)} %bitcast.3, f32[16,4096]{1,0:T(8,128)S(1)} %copy-done.1), custom_call_target="tpu_custom_call" | custom-call | flops 671088640 | bytes 1048576 | tf_op jit(solution)/shard_map/sort_block/pallas_call | solution.py:112
  8.9 3.3 %copy-done = bf16[2048,2048]{1,0:T(8,128)(2,1)} copy-done((bf16[2048,2048]{1,0:T(8,128)(2,1)}, bf16[2048,2048]{1,0:T(8,128)(2,1)S(1)}, u32[]{:S(2)}) %copy-start) | copy-done | bytes 8388632
  12.1 1.3 %collective-permute-start = (f32[24,2048]{1,0:T(8,128)S(1)}, f32[24,2048]{1,0:T(8,128)S(1)}, u32[]{:S(2)}, u32[]{:S(2)}) collective-permute-start(f32[24,2048]{1,0:T(8,128)S(1)} %get-tuple-element.38.s0.w0), channel_id=1, source_target_pairs={{1,0},{2,1},{3,2},{4,3},{5,4},{6,5},{7,6},{8,7},{9,8},{10,9},{11,1... | collective-permute-start | bytes 589832 | tf_op jit(solution)/shard_map/ppermute | solution.py:441
  17.3 5.7 %sort_block.2 = (f32[24,2048]{1,0:T(8,128)S(1)}, bf16[2048,2048]{1,0:T(8,128)(2,1)S(1)}, f32[3,2048,128]{2,1,0:T(8,128)S(1)}, f32[32]{0:T(128)S(1)}) custom-call(f32[3,4096]{1,0:T(4,128)S(1)} %copy-done.5, f32[1,4096]{1,0:T(1,128)S(1)} %bitcast.4, f32[16,4096]{1,0:T(8,128)S(1)} %copy-done.2), custom_call_target="tpu_custom_call" | custom-call | flops 671088640 | bytes 1048576 | tf_op jit(solution)/shard_map/sort_block/pallas_call | solution.py:112
  23.1 9.3 %halo_build.1 = (bf16[8,256,768]{2,1,0:T(8,128)(2,1)S(1)}, s32[24]{0:T(128)S(1)}, f32[16,2048]{1,0:T(8,128)S(1)}, f32[16,2048]{1,0:T(8,128)S(1)}) custom-call(s32[4,2]{1,0:T(4,128)S(1)} %copy.7.pair, s32[1]{0:T(128)S(6)} %copy.9.count, f32[32]{0:T(128)S(1)} %get-tuple-element.35.yb1, f32[24,2048]{1,0:T(8,128)S(1)} %get-tuple-element.36.s1.w1, ...), custom_call_target="tpu_custom_call" | custom-call | flops 2000000000 | bytes 1048576 | tf_op jit(solution)/shard_map/halo_build/pallas_call | solution.py:269
  32.4 3.0 %collective-permute-start.1 = (f32[16,2048]{1,0:T(8,128)S(1)}, f32[16,2048]{1,0:T(8,128)S(1)}, u32[]{:S(2)}, u32[]{:S(2)}) collective-permute-start(f32[16,2048]{1,0:T(8,128)S(1)} %get-tuple-element.46), channel_id=1, source_target_pairs={{0,1},{1,2},{2,3},{3,4},{4,5},{5,6},{6,7},{7,8},{8,9},{9,10},{10,1... | collective-permute-start | bytes 393224 | tf_op jit(solution)/shard_map/ppermute | solution.py:441
  35.4 19.9 %own_build.1 = (bf16[8,256,512]{2,1,0:T(8,128)(2,1)S(1)}, bf16[8,256,768]{2,1,0:T(8,128)(2,1)S(1)}, bf16[8,256,512]{2,1,0:T(8,128)(2,1)S(1)}, s32[72]{0:T(128)S(...) custom-call(s32[4,2]{1,0:T(4,128)S(1)} %copy.7.pair, s32[1]{0:T(128)S(6)} %copy.9.count, ...), custom_call_target="tpu_custom_call" | custom-call | flops 6000000000 | bytes 1048576 | tf_op jit(solution)/shard_map/own_build/pallas_call | solution.py:269
  55.3 1.4 %finish.3 = (f32[16,2048]{1,0:T(8,128)S(1)}, f32[16,2048]{1,0:T(8,128)S(1)}, f32[16,2048]{1,0:T(8,128)S(1)}, f32[16,128]{1,0:T(8,128)S(1)}) custom-call(s32[24]{0:T(128)S(1)} %get-tuple-element.39.tab, bf16[8,256,768]{2,1,0:T(8,128)(2,1)S(1)} %get-tuple-element.40.k12, f32[24,2048]{1,0:T(8,128)S(1)} %get-tuple-element.38.s0.w0, ...), custom_call_target="tpu_custom_call" | custom-call | flops 1000000000 | bytes 1048576 | tf_op jit(solution)/shard_map/finish/pallas_call | solution.py:269
  56.7 1.3 %collective-permute-start.3 = (f32[16,2048]{1,0:T(8,128)S(1)}, f32[16,2048]{1,0:T(8,128)S(1)}, u32[]{:S(2)}, u32[]{:S(2)}) collective-permute-start(f32[16,2048]{1,0:T(8,128)S(1)} %get-tuple-element.55), channel_id=1, source_target_pairs={{0,1},{1,2},{2,3},{3,4},{4,5},{5,6},{6,7},{7,8},{8,9},{9,10},{10,1... | collective-permute-start | bytes 393224 | tf_op jit(solution)/shard_map/ppermute | solution.py:441
  58.0 1.3 %collective-permute-start.2 = (f32[16,2048]{1,0:T(8,128)S(1)}, f32[16,2048]{1,0:T(8,128)S(1)}, u32[]{:S(2)}, u32[]{:S(2)}) collective-permute-start(f32[16,2048]{1,0:T(8,128)S(1)} %get-tuple-element.47.w0.wa), channel_id=1, source_target_pairs={{1,0},{2,1},{3,2},{4,3},{5,4},{6,5},{7,6},{8,7},{9,8},{10,9},{11,1... | collective-permute-start | bytes 393224 | tf_op jit(solution)/shard_map/ppermute | solution.py:441
  59.3 4.8 %own_apply.2 = (f32[16,2048]{1,0:T(8,128)S(1)}, f32[16,2048]{1,0:T(8,128)S(1)}) custom-call(s32[72]{0:T(128)S(1)} %get-tuple-element.48.tab, bf16[8,256,512]{2,1,0:T(8,128)(2,1)S(1)} %get-tuple-element.49.k00, bf16[8,256,768]{2,1,0:T(8,128)(2,1)S(1)} %get-tuple-element.50.k01, bf16[8,256,512]{2,1,0:T(8,128)(2,1)S(1)} %get-tuple-element.51.k11, ...), custom_call_target="tpu_custom_call" | custom-call | flops 2000000000 | bytes 1048576 | tf_op jit(solution)/shard_map/own_apply/pallas_call | solution.py:269
  64.1 2.4 %finish.4 = (f32[16,2048]{1,0:T(8,128)S(1)}, f32[16,2048]{1,0:T(8,128)S(1)}, f32[16,2048]{1,0:T(8,128)S(1)}, f32[16,128]{1,0:T(8,128)S(1)}) custom-call(s32[24]{0:T(128)S(1)} %get-tuple-element.39.tab, bf16[8,256,768]{2,1,0:T(8,128)(2,1)S(1)} %get-tuple-element.40.k12, f32[24,2048]{1,0:T(8,128)S(1)} %get-tuple-element.38.s0.w0, ...), custom_call_target="tpu_custom_call" | custom-call | flops 1000000000 | bytes 1048576 | tf_op jit(solution)/shard_map/finish/pallas_call | solution.py:269
  66.5 5.4 %collective-permute-start.5 = (f32[16,2048]{1,0:T(8,128)S(1)}, f32[16,2048]{1,0:T(8,128)S(1)}, u32[]{:S(2)}, u32[]{:S(2)}) collective-permute-start(f32[16,2048]{1,0:T(8,128)S(1)} %get-tuple-element.61), channel_id=1, source_target_pairs={{0,1},{1,2},{2,3},{3,4},{4,5},{5,6},{6,7},{7,8},{8,9},{9,10},{10,1... | collective-permute-start | bytes 393224 | tf_op jit(solution)/shard_map/ppermute | solution.py:441
  71.9 1.3 %collective-permute-start.4 = (f32[16,2048]{1,0:T(8,128)S(1)}, f32[16,2048]{1,0:T(8,128)S(1)}, u32[]{:S(2)}, u32[]{:S(2)}) collective-permute-start(f32[16,2048]{1,0:T(8,128)S(1)} %get-tuple-element.57.w0.wb), channel_id=1, source_target_pairs={{1,0},{2,1},{3,2},{4,3},{5,4},{6,5},{7,6},{8,7},{9,8},{10,9},{11,1... | collective-permute-start | bytes 393224 | tf_op jit(solution)/shard_map/ppermute | solution.py:441
  73.2 4.8 %own_apply.3 = (f32[16,2048]{1,0:T(8,128)S(1)}, f32[16,2048]{1,0:T(8,128)S(1)}) custom-call(s32[72]{0:T(128)S(1)} %get-tuple-element.48.tab, bf16[8,256,512]{2,1,0:T(8,128)(2,1)S(1)} %get-tuple-element.49.k00, bf16[8,256,768]{2,1,0:T(8,128)(2,1)S(1)} %get-tuple-element.50.k01, bf16[8,256,512]{2,1,0:T(8,128)(2,1)S(1)} %get-tuple-element.51.k11, ...), custom_call_target="tpu_custom_call" | custom-call | flops 2000000000 | bytes 1048576 | tf_op jit(solution)/shard_map/own_apply/pallas_call | solution.py:269
  78.0 2.3 %finish.5 = (f32[16,2048]{1,0:T(8,128)S(1)}, f32[16,2048]{1,0:T(8,128)S(1)}, f32[16,2048]{1,0:T(8,128)}, f32[16,128]{1,0:T(8,128)S(1)}) custom-call(s32[24]{0:T(128)S(1)} %get-tuple-element.39.tab, bf16[8,256,768]{2,1,0:T(8,128)(2,1)S(1)} %get-tuple-element.40.k12, f32[24,2048]{1,0:T(8,128)S(1)} %get-tuple-element.38.s0.w0, ...), custom_call_target="tpu_custom_call" | custom-call | flops 1000000000 | bytes 1048576 | tf_op jit(solution)/shard_map/finish/pallas_call | solution.py:269
  80.2 1.1 %collective-permute-start.6 = (f32[16,128]{1,0:T(8,128)S(1)}, f32[16,128]{1,0:T(8,128)S(1)}, u32[]{:S(2)}, u32[]{:S(2)}) collective-permute-start(f32[16,128]{1,0:T(8,128)S(1)} %get-tuple-element.63), channel_id=1, source_target_pairs={{0,1},{1,0},{2,3},{3,2},{4,5},{5,4},{6,7},{7,6},{8,9},{9,8},{10,11... | collective-permute-start | bytes 24584 | tf_op jit(solution)/shard_map/ppermute | solution.py:450
  82.1 3.0 %collective-permute-start.7 = (f32[16,128]{1,0:T(8,128)S(1)}, f32[16,128]{1,0:T(8,128)S(1)}, u32[]{:S(2)}, u32[]{:S(2)}) collective-permute-start(f32[16,128]{1,0:T(8,128)S(1)} %add.12), channel_id=1, source_target_pairs={{0,2},{1,3},{2,0},{3,1},{4,6},{5,7},{6,4},{7,5},{8,10},{9,11},{10,... | collective-permute-start | bytes 24584 | tf_op jit(solution)/shard_map/ppermute | solution.py:450
  85.2 1.6 %collective-permute-done.7 = f32[16,128]{1,0:T(8,128)S(1)} collective-permute-done((f32[16,128]{1,0:T(8,128)S(1)}, f32[16,128]{1,0:T(8,128)S(1)}, u32[]{:S(2)}, u32[]{:S(2)}) %collective-permute-start.7) | collective-permute-done | bytes 8224 | tf_op jit(solution)/shard_map/ppermute | solution.py:450
  86.8 2.5 %collective-permute-start.8 = (f32[16,128]{1,0:T(8,128)S(1)}, f32[16,128]{1,0:T(8,128)S(1)}, u32[]{:S(2)}, u32[]{:S(2)}) collective-permute-start(f32[16,128]{1,0:T(8,128)S(1)} %add.13), channel_id=1, source_target_pairs={{0,4},{1,5},{2,6},{3,7},{4,0},{5,1},{6,2},{7,3},{8,12},{9,13},{10,... | collective-permute-start | bytes 24584 | tf_op jit(solution)/shard_map/ppermute | solution.py:450
  89.3 1.3 %unsort.3.u1 = f32[48,2048]{1,0:T(8,128)S(1)} custom-call(bf16[2048,2048]{1,0:T(8,128)(2,1)S(1)} %get-tuple-element.66.perm, f32[16,2048]{1,0:T(8,128)S(1)} %get-tuple-element.52.w1.wa, f32[16,2048]{1,0:T(8,128)S(1)} %get-tuple-element.58.w1.wb, f32[16,2048]{1,0:T(8,128)S(1)} %get-tuple-element.67.wc), custom_call_target="tpu_custom_call" | custom-call | flops 805306368 | bytes 1048576 | tf_op jit(solution)/shard_map/unsort/pallas_call | solution.py:269
  91.0 4.0 %collective-permute-start.9 = (f32[16,128]{1,0:T(8,128)S(1)}, f32[16,128]{1,0:T(8,128)S(1)}, u32[]{:S(2)}, u32[]{:S(2)}) collective-permute-start(f32[16,128]{1,0:T(8,128)S(1)} %add.14), channel_id=1, source_target_pairs={{0,8},{1,9},{2,10},{3,11},{4,12},{5,13},{6,14},{7,15},{8,0},{9,1},... | collective-permute-start | bytes 24584 | tf_op jit(solution)/shard_map/ppermute | solution.py:450
  95.0 1.3 %unsort.2.u0 = f32[48,2048]{1,0:T(8,128)S(1)} custom-call(bf16[2048,2048]{1,0:T(8,128)(2,1)S(1)} %bitcast.2, f32[16,2048]{1,0:T(8,128)S(1)} %get-tuple-element.47.w0.wa, f32[16,2048]{1,0:T(8,128)S(1)} %get-tuple-element.57.w0.wb, f32[16,2048]{1,0:T(8,128)S(1)} %get-tuple-element.65.wc), custom_call_target="tpu_custom_call" | custom-call | flops 805306368 | bytes 1048576 | tf_op jit(solution)/shard_map/unsort/pallas_call | solution.py:269
  96.6 1.0 %combine.1 = (f32[16,4096]{1,0:T(8,128)}, f32[16,4096]{1,0:T(8,128)}) custom-call(f32[16,128]{1,0:T(8,128)S(1)} %add.15.mom, f32[16,4096]{1,0:T(8,128)S(1)} %copy-done.3, f32[48,2048]{1,0:T(8,128)S(1)} %unsort.2.u0, f32[48,2048]{1,0:T(8,128)S(1)} %unsort.3.u1), custom_call_target="tpu_custom_call" | custom-call | flops 1000000 | bytes 1048576 | tf_op jit(solution)/shard_map/combine/pallas_call | solution.py:269
  (35 shorter events, 7.4 us)
Async XLA Ops:
  0.6 1.0 copy-start.1
  1.6 0.8 copy-start.4
  2.4 0.7 copy-start.6
  8.9 3.3 %copy-start = (bf16[2048,2048]{1,0:T(8,128)(2,1)}, bf16[2048,2048]{1,0:T(8,128)(2,1)S(1)}, u32[]{:S(2)}) copy-start(bf16[2048,2048]{1,0:T(8,128)(2,1)S(1)} %get-tuple-element.64.perm) | copy-start | bytes 25165828
  12.1 10.9 %collective-permute-start = (f32[24,2048]{1,0:T(8,128)S(1)}, f32[24,2048]{1,0:T(8,128)S(1)}, u32[]{:S(2)}, u32[]{:S(2)}) collective-permute-start(f32[24,2048]{1,0:T(8,128)S(1)} %get-tuple-element.38.s0.w0), channel_id=1, source_target_pairs={{1,0},{2,1},{3,2},{4,3},{5,4},{6,5},{7,6},{8,7},{9,8},{10,9},{11,1... | collective-permute-start | bytes 589832 | tf_op jit(solution)/shard_map/ppermute | solution.py:441
  14.8 0.9 copy-start.2
  15.8 0.8 copy-start.5
  16.6 0.7 copy-start.7
  32.4 23.0 %collective-permute-start.1 = (f32[16,2048]{1,0:T(8,128)S(1)}, f32[16,2048]{1,0:T(8,128)S(1)}, u32[]{:S(2)}, u32[]{:S(2)}) collective-permute-start(f32[16,2048]{1,0:T(8,128)S(1)} %get-tuple-element.46), channel_id=1, source_target_pairs={{0,1},{1,2},{2,3},{3,4},{4,5},{5,6},{6,7},{7,8},{8,9},{9,10},{10,1... | collective-permute-start | bytes 393224 | tf_op jit(solution)/shard_map/ppermute | solution.py:441
  56.7 7.4 %collective-permute-start.3 = (f32[16,2048]{1,0:T(8,128)S(1)}, f32[16,2048]{1,0:T(8,128)S(1)}, u32[]{:S(2)}, u32[]{:S(2)}) collective-permute-start(f32[16,2048]{1,0:T(8,128)S(1)} %get-tuple-element.55), channel_id=1, source_target_pairs={{0,1},{1,2},{2,3},{3,4},{4,5},{5,6},{6,7},{7,8},{8,9},{9,10},{10,1... | collective-permute-start | bytes 393224 | tf_op jit(solution)/shard_map/ppermute | solution.py:441
  58.0 6.1 %collective-permute-start.2 = (f32[16,2048]{1,0:T(8,128)S(1)}, f32[16,2048]{1,0:T(8,128)S(1)}, u32[]{:S(2)}, u32[]{:S(2)}) collective-permute-start(f32[16,2048]{1,0:T(8,128)S(1)} %get-tuple-element.47.w0.wa), channel_id=1, source_target_pairs={{1,0},{2,1},{3,2},{4,3},{5,4},{6,5},{7,6},{8,7},{9,8},{10,9},{11,1... | collective-permute-start | bytes 393224 | tf_op jit(solution)/shard_map/ppermute | solution.py:441
  66.5 11.4 %collective-permute-start.5 = (f32[16,2048]{1,0:T(8,128)S(1)}, f32[16,2048]{1,0:T(8,128)S(1)}, u32[]{:S(2)}, u32[]{:S(2)}) collective-permute-start(f32[16,2048]{1,0:T(8,128)S(1)} %get-tuple-element.61), channel_id=1, source_target_pairs={{0,1},{1,2},{2,3},{3,4},{4,5},{5,6},{6,7},{7,8},{8,9},{9,10},{10,1... | collective-permute-start | bytes 393224 | tf_op jit(solution)/shard_map/ppermute | solution.py:441
  71.9 6.1 %collective-permute-start.4 = (f32[16,2048]{1,0:T(8,128)S(1)}, f32[16,2048]{1,0:T(8,128)S(1)}, u32[]{:S(2)}, u32[]{:S(2)}) collective-permute-start(f32[16,2048]{1,0:T(8,128)S(1)} %get-tuple-element.57.w0.wb), channel_id=1, source_target_pairs={{1,0},{2,1},{3,2},{4,3},{5,4},{6,5},{7,6},{8,7},{9,8},{10,9},{11,1... | collective-permute-start | bytes 393224 | tf_op jit(solution)/shard_map/ppermute | solution.py:441
  78.0 17.0 %slice-start = ((s8[8388608]{0:T(1024)(128)(4,1)}), s8[4194304]{0:T(1024)(128)(4,1)S(1)}, s32[]{:S(2)}) async-start(s8[8388608]{0:T(1024)(128)(4,1)} %bitcast.1), calls=%async_computation | async-start | bytes 8388608
  80.2 1.9 %collective-permute-start.6 = (f32[16,128]{1,0:T(8,128)S(1)}, f32[16,128]{1,0:T(8,128)S(1)}, u32[]{:S(2)}, u32[]{:S(2)}) collective-permute-start(f32[16,128]{1,0:T(8,128)S(1)} %get-tuple-element.63), channel_id=1, source_target_pairs={{0,1},{1,0},{2,3},{3,2},{4,5},{5,4},{6,7},{7,6},{8,9},{9,8},{10,11... | collective-permute-start | bytes 24584 | tf_op jit(solution)/shard_map/ppermute | solution.py:450
  82.1 4.7 %collective-permute-start.7 = (f32[16,128]{1,0:T(8,128)S(1)}, f32[16,128]{1,0:T(8,128)S(1)}, u32[]{:S(2)}, u32[]{:S(2)}) collective-permute-start(f32[16,128]{1,0:T(8,128)S(1)} %add.12), channel_id=1, source_target_pairs={{0,2},{1,3},{2,0},{3,1},{4,6},{5,7},{6,4},{7,5},{8,10},{9,11},{10,... | collective-permute-start | bytes 24584 | tf_op jit(solution)/shard_map/ppermute | solution.py:450
  86.8 4.1 %collective-permute-start.8 = (f32[16,128]{1,0:T(8,128)S(1)}, f32[16,128]{1,0:T(8,128)S(1)}, u32[]{:S(2)}, u32[]{:S(2)}) collective-permute-start(f32[16,128]{1,0:T(8,128)S(1)} %add.13), channel_id=1, source_target_pairs={{0,4},{1,5},{2,6},{3,7},{4,0},{5,1},{6,2},{7,3},{8,12},{9,13},{10,... | collective-permute-start | bytes 24584 | tf_op jit(solution)/shard_map/ppermute | solution.py:450
  89.3 5.6 %slice-start.1 = ((s8[8388608]{0:T(1024)(128)(4,1)}), s8[4194304]{0:T(1024)(128)(4,1)S(1)}, s32[]{:S(2)}) async-start(s8[8388608]{0:T(1024)(128)(4,1)} %bitcast.1), calls=%async_computation.1 | async-start | bytes 8388608
  91.0 5.6 %collective-permute-start.9 = (f32[16,128]{1,0:T(8,128)S(1)}, f32[16,128]{1,0:T(8,128)S(1)}, u32[]{:S(2)}, u32[]{:S(2)}) collective-permute-start(f32[16,128]{1,0:T(8,128)S(1)} %add.14), channel_id=1, source_target_pairs={{0,8},{1,9},{2,10},{3,11},{4,12},{5,13},{6,14},{7,15},{8,0},{9,1},... | collective-permute-start | bytes 24584 | tf_op jit(solution)/shard_map/ppermute | solution.py:450
  95.0 1.6 %copy-start.3 = (f32[16,4096]{1,0:T(8,128)S(1)}, f32[16,4096]{1,0:T(8,128)}, u32[]{:S(2)}) copy-start(f32[16,4096]{1,0:T(8,128)} %probes.1) | copy-start | bytes 786436

commit v2 on v1

--- a/solution.py
+++ b/solution.py
@@ -16,7 +16,7 @@
 OFF_SUBS = OFF_W // SUB
 DIAG_W = 512
 N_PROBES = 16
-CHUNK = 16
+ROWS = 32
 MIB = 1 << 20
 
 VMEM = pl.BlockSpec(memory_space=pltpu.VMEM)
@@ -55,9 +55,22 @@
     return high, mid, rest - mid
 
 
-def sort_kernel(blk, pts_ref, nv_ref, pr_ref, out_ref, perm_ref, col_ref, yb_ref, key_ref):
-    cols = pl.ds(blk * BLK, BLK)
-    y_row = pts_ref[1:2, cols]
+def one_hot(marked, g, c, place):
+    hit = jnp.broadcast_to(marked[:, c * SUB : (c + 1) * SUB], (STRIP, SUB)) == place
+    return jnp.where(hit, jnp.ones((STRIP, SUB), bf16), jnp.zeros((STRIP, SUB), bf16))
+
+
+def places():
+    return lax.broadcasted_iota(jnp.int32, (STRIP, SUB), 0).astype(f32).astype(bf16)
+
+
+def marks(rank, g):
+    group = lax.shift_right_logical(rank, 8)
+    within = jnp.bitwise_and(rank, STRIP - 1)
+    return jnp.where(group == g, within, -1).astype(f32).astype(bf16)
+
+
+def rank_of(y_row, key_ref):
     lane = lax.broadcasted_iota(jnp.int32, (1, BLK), 1)
     key_row = (y_row * 4096.0).astype(jnp.int32) * BLK + lane
     for c in range(SUBS):
@@ -72,33 +85,52 @@
         return acc + jnp.where(mine < keys, 1, 0)
 
     acc = lax.fori_loop(0, BLK // 8, count, jnp.zeros((8, BLK), jnp.int32), unroll=8)
-    rank = jnp.sum(acc, axis=0, keepdims=True)
-    group = lax.shift_right_logical(rank, 8)
-    within = jnp.bitwise_and(rank, STRIP - 1)
-
-    pr = pr_ref[:, cols]
-    aux = jnp.concatenate(
-        [pts_ref[0:3, cols] * 2.0, nv_ref[:, cols], jnp.zeros((4, BLK), f32)], axis=0
-    )
-    data = jnp.concatenate([*split3(pr), *split3(aux), jnp.zeros((8, BLK), f32)], axis=0).astype(bf16)
-    place = lax.broadcasted_iota(jnp.int32, (STRIP, SUB), 0).astype(f32).astype(bf16)
-    one = jnp.ones((STRIP, SUB), bf16)
-    zero = jnp.zeros((STRIP, SUB), bf16)
-    for g in range(STRIPS):
-        marked = jnp.where(group == g, within, -1).astype(f32).astype(bf16)
-        for c in range(SUBS):
-            hit = jnp.broadcast_to(marked[:, c * SUB : (c + 1) * SUB], (STRIP, SUB)) == place
-            perm_ref[g * STRIP : (g + 1) * STRIP, c * SUB : (c + 1) * SUB] = jnp.where(hit, one, zero)
-        got = nt(data, perm_ref[g * STRIP : (g + 1) * STRIP, :])
-        here = slice(g * STRIP, (g + 1) * STRIP)
-        out_ref[0:16, here] = (got[0:16] + got[16:32]) + got[32:48]
-        out_ref[16:24, here] = (got[48:56] + got[56:64]) + got[64:72]
-    for axis in range(3):
-        for c in range(SUBS):
-            here = slice(c * SUB, (c + 1) * SUB)
-            row = out_ref[16 + axis : 17 + axis, here]
-            col_ref[axis, here, :] = jnp.broadcast_to(row, (SUB, SUB)).T
-    bounds(out_ref, yb_ref)
+    return jnp.sum(acc, axis=0, keepdims=True)
+
+
+def sort_kernel(
+    pts_hbm, nv_hbm, pr_hbm, pair, count, s0, s1, col0, col1, yb0, yb1, rank0, rank1, flags,
+    pts_ref, nv_ref, pr_ref, key_ref, perm_ref, sems
+):
+    copies = [
+        pltpu.make_async_copy(src, dst, sems.at[k])
+        for k, (src, dst) in enumerate(((pts_hbm, pts_ref), (nv_hbm, nv_ref), (pr_hbm, pr_ref)))
+    ]
+    for copy in copies:
+        copy.start()
+    for local in range(2):
+        for ahead in range(2):
+            flags[2 * local + ahead] = live_flag(pair, count, local, ahead)
+    copies[0].wait()
+    for blk, rank_ref in enumerate((rank0, rank1)):
+        rank_ref[...] = rank_of(pts_ref[1:2, blk * BLK : (blk + 1) * BLK], key_ref)
+    copies[1].wait()
+    copies[2].wait()
+    for blk, (out_ref, col_ref, rank_ref) in enumerate(((s0, col0, rank0), (s1, col1, rank1))):
+        cols = slice(blk * BLK, (blk + 1) * BLK)
+        aux = jnp.concatenate(
+            [pts_ref[0:3, cols] * 2.0, nv_ref[:, cols], jnp.zeros((4, BLK), f32)], axis=0
+        )
+        data = jnp.concatenate(
+            [*split3(pr_ref[:, cols]), *split3(aux), jnp.zeros((8, BLK), f32)], axis=0
+        ).astype(bf16)
+        rank = rank_ref[...]
+        place = places()
+        for g in range(STRIPS):
+            marked = marks(rank, g)
+            for c in range(SUBS):
+                perm_ref[g % 2, :, c * SUB : (c + 1) * SUB] = one_hot(marked, g, c, place)
+            got = nt(data, perm_ref[g % 2])
+            here = slice(g * STRIP, (g + 1) * STRIP)
+            out_ref[0:16, here] = (got[0:16] + got[16:32]) + got[32:48]
+            out_ref[16:24, here] = (got[48:56] + got[56:64]) + got[64:72]
+        for axis in range(3):
+            for c in range(SUBS):
+                here = slice(c * SUB, (c + 1) * SUB)
+                row = out_ref[16 + axis : 17 + axis, here]
+                col_ref[axis, here, :] = jnp.broadcast_to(row, (SUB, SUB)).T
+    bounds(s0, yb0)
+    bounds(s1, yb1)
 
 
 def bounds(side_ref, yb_ref):
@@ -106,24 +138,6 @@
         row = side_ref[17:18, c * SUB : (c + 1) * SUB]
         yb_ref[c] = jnp.min(row)
         yb_ref[SUBS + c] = jnp.max(row)
-
-
-def sort_block(blk, points, noise, probes):
-    return pl.pallas_call(
-        functools.partial(sort_kernel, blk),
-        out_shape=(
-            pltpu.VMEM((24, BLK), f32),
-            pltpu.VMEM((BLK, BLK), bf16),
-            pltpu.VMEM((3, BLK, SUB), f32),
-            jax.ShapeDtypeStruct((2 * SUBS,), f32),
-        ),
-        in_specs=[VMEM] * 3,
-        out_specs=(VMEM, VMEM, VMEM, SMEM),
-        scratch_shapes=[pltpu.VMEM((BLK, SUB), jnp.int32)],
-        compiler_params=pltpu.CompilerParams(vmem_limit_bytes=12 * MIB),
-        cost_estimate=pl.CostEstimate(flops=2 * 80 * BLK * BLK, bytes_accessed=MIB, transcendentals=0),
-        name="sort_block",
-    )(points, noise, probes)
 
 
 def live_flag(pair_ref, count_ref, local, ahead):
@@ -167,7 +181,7 @@
     width = rows[0].shape[1]
     squared = None
     for axis in range(3):
-        mine = col_ref[axis, pl.ds(row_at, CHUNK), :]
+        mine = col_ref[axis, pl.ds(row_at, ROWS), :]
         diff = jnp.concatenate([mine] * (width // SUB), axis=1) - rows[axis]
         part = diff * diff
         squared = part if squared is None else squared + part
@@ -178,27 +192,28 @@
     return ((t2 * t2) * (q + 0.25)).astype(bf16)
 
 
-def build_strip(store, col_ref, strip, side_ref, start, width):
+def build_strip(store, col_ref, strip, side_ref, start, width, unroll=2):
     at = pl.ds(start, width)
-    rows = [jnp.broadcast_to(side_ref[16 + axis : 17 + axis, at], (CHUNK, width)) for axis in range(3)]
+    rows = [jnp.broadcast_to(side_ref[16 + axis : 17 + axis, at], (ROWS, width)) for axis in range(3)]
 
     def chunk(i, carry):
-        row_at = pl.multiple_of(strip * STRIP + i * CHUNK, CHUNK)
-        store(pl.multiple_of(i * CHUNK, CHUNK), kernel_values(col_ref, row_at, rows))
+        row_at = pl.multiple_of(strip * STRIP + i * ROWS, ROWS)
+        store(pl.multiple_of(i * ROWS, ROWS), kernel_values(col_ref, row_at, rows))
         return carry
 
-    lax.fori_loop(0, STRIP // CHUNK, chunk, 0, unroll=2)
+    lax.fori_loop(0, STRIP // ROWS, chunk, 0, unroll=unroll)
 
 
 def build_off(k_ref, tab_ref, base, col_ref, side_ref):
+    part = OFF_W // 2
     for i in range(STRIPS):
         start = pl.multiple_of(tab_ref[base + T_START + i] * SUB, SUB)
-        for h in range(OFF_W // STRIP):
+        for h in range(2):
 
             def store(at, value, i=i, h=h):
-                k_ref[i, pl.ds(at, CHUNK), h * STRIP : (h + 1) * STRIP] = value
-
-            build_strip(store, col_ref, i, side_ref, start + h * STRIP, STRIP)
+                k_ref[i, pl.ds(at, ROWS), h * part : (h + 1) * part] = value
+
+            build_strip(store, col_ref, i, side_ref, pl.multiple_of(start + h * part, SUB), part)
 
 
 def build_diag(k_ref, col_ref, side_ref):
@@ -206,9 +221,9 @@
         for h in range(min(DIAG_W, BLK - i * STRIP) // STRIP):
 
             def store(at, value, i=i, h=h):
-                k_ref[i, pl.ds(at, CHUNK), h * STRIP : (h + 1) * STRIP] = value
-
-            build_strip(store, col_ref, i, side_ref, (i + h) * STRIP, STRIP)
+                k_ref[i, pl.ds(at, ROWS), h * STRIP : (h + 1) * STRIP] = value
+
+            build_strip(store, col_ref, i, side_ref, (i + h) * STRIP, STRIP, 4)
 
 
 def to_owner(k_ref, tab_ref, base, v_col, acc_row):
@@ -243,7 +258,7 @@
                 there = pl.ds(pl.multiple_of(j * SUB, SUB), SUB)
 
                 def store(at, value):
-                    tile_ref[pl.ds(at, CHUNK), :] = value
+                    tile_ref[pl.ds(at, ROWS), :] = value
 
                 build_strip(store, col_ref, i, side_ref, pl.multiple_of(j * SUB, SUB), SUB)
                 if acc_row is not None:
@@ -280,13 +295,27 @@
     return run
 
 
-def halo_build_kernel(pair, count, yb1, s1, col1, halo, k12, tab, acc1, back, yb2, tile, v1, v2):
+def diag_build_kernel(flags, yb0, yb1, s0, s1, col0, col1, k00, k11, tab):
+    fill_table(tab, 0 * T_SIZE, flags[0], yb0, yb0, True)
+    fill_table(tab, 1 * T_SIZE, flags[1], yb0, yb1, False)
+    fill_table(tab, 2 * T_SIZE, flags[2], yb1, yb1, True)
+
+    @pl.when(flags[0] > 0)
+    def _():
+        build_diag(k00, col0, s0)
+
+    @pl.when(flags[2] > 0)
+    def _():
+        build_diag(k11, col1, s1)
+
+
+def halo_build_kernel(flags, yb1, s1, col1, halo, k12, tab, acc1, back, yb2, tile, v1, v2):
     bounds(halo, yb2)
-    fill_table(tab, 0, live_flag(pair, count, 1, 1), yb1, yb2, False)
+    fill_table(tab, 0, flags[3], yb1, yb2, False)
     acc1[...] = jnp.zeros(FIELD, f32)
     back[...] = jnp.zeros(FIELD, f32)
 
-    @pl.when(tab[T_LIVE] > 0)
+    @pl.when(flags[3] > 0)
     def _():
         v1[...] = split2(s1[0:16, :])
         v2[...] = split2(halo[0:16, :])
@@ -314,28 +343,15 @@
         extra_tiles(tab, 2 * T_SIZE, col1, s1, tile, v1, v1, acc1, acc1)
 
 
-def own_build_kernel(
-    pair, count, yb0, yb1, s0, s1, col0, col1, acc1_in, k00, k01, k11, tab, acc0, acc1, tile, v0, v1
-):
-    fill_table(tab, 0 * T_SIZE, live_flag(pair, count, 0, 0), yb0, yb0, True)
-    fill_table(tab, 1 * T_SIZE, live_flag(pair, count, 0, 1), yb0, yb1, False)
-    fill_table(tab, 2 * T_SIZE, live_flag(pair, count, 1, 0), yb1, yb1, True)
+def own_build_kernel(tab, s0, s1, col0, col1, k00, k11, acc1_in, k01, acc0, acc1, tile, v0, v1):
     acc0[...] = jnp.zeros(FIELD, f32)
     acc1[...] = acc1_in[...]
     v0[...] = split2(s0[0:16, :])
     v1[...] = split2(s1[0:16, :])
 
-    @pl.when(tab[0 * T_SIZE + T_LIVE] > 0)
-    def _():
-        build_diag(k00, col0, s0)
-
     @pl.when(tab[1 * T_SIZE + T_LIVE] > 0)
     def _():
         build_off(k01, tab, 1 * T_SIZE, col0, s1)
-
-    @pl.when(tab[2 * T_SIZE + T_LIVE] > 0)
-    def _():
-        build_diag(k11, col1, s1)
 
     local_products(tab, k00, k01, k11, s0, s1, col0, col1, tile, v0, v1, acc0, acc1)
 
@@ -370,14 +386,13 @@
     before1 = w1[0:16, :]
     next1 = s1[19:20, :] * before1 + acc[...]
     n1[...] = next1
-    if level < 3:
-        back[...] = jnp.zeros(FIELD, f32)
-
-        @pl.when(live)
-        def _():
-            v1[...] = split2(next1)
-            to_partner(k12, tab, 0, v1, back)
-            extra_tiles(tab, 0, col1, halo, tile, v1, None, None, back)
+    back[...] = jnp.zeros(FIELD, f32)
+
+    @pl.when(live)
+    def _():
+        v1[...] = split2(next1)
+        to_partner(k12, tab, 0, v1, back)
+        extra_tiles(tab, 0, col1, halo, tile, v1, None, None, back)
 
     next0 = s0[19:20, :] * before0 + (acc0[...] + arrived[...])
     n0[...] = next0
@@ -392,18 +407,46 @@
     mom[...] = total
 
 
-def unsort_kernel(perm, wa, wb, wc, out):
+def moment_kernel(s0, s1, acc0, acc1, arrived, w0, w1, mom_in, mom):
+    lane = lax.broadcasted_iota(jnp.int32, (N_PROBES, SUB), 1)
+    one = w0[...]
+    two = w1[...]
+    cross = inner(one, s0[19:20, :] * one + (acc0[...] + 2.0 * arrived[...]))
+    cross = cross + inner(two, s1[19:20, :] * two + acc1[...])
+    mom[...] = mom_in[...] + jnp.where(lane == 5, cross, 0.0)
+
+
+def last_kernel(tab, k12, s0, s1, col1, halo, halo_w, acc0, acc1, arrived, w0, w1, n0, n1, tile, v2):
+    n1[...] = s1[19:20, :] * w1[...] + acc1[...]
+    n0[...] = s0[19:20, :] * w0[...] + (acc0[...] + arrived[...])
+
+    @pl.when(tab[T_LIVE] > 0)
+    def _():
+        v2[...] = split2(halo_w[...])
+        to_owner(k12, tab, 0, v2, n1)
+        extra_tiles(tab, 0, col1, halo, tile, None, v2, n1, None)
+
+
+def unsort_kernel(rank_ref, wa, wb, wc, out, perm_ref):
     stacked = jnp.concatenate([split2(wa[...]), split2(wb[...]), split2(wc[...])], axis=0)
+    rank = rank_ref[...]
+    place = places()
+    marked = [marks(rank, g) for g in range(STRIPS)]
     for c in range(BLK // STRIP):
         here = slice(c * STRIP, (c + 1) * STRIP)
-        got = nn(stacked, perm[:, here])
+        for g in range(STRIPS):
+            for h in range(2):
+                perm_ref[c % 2, g * STRIP : (g + 1) * STRIP, h * SUB : (h + 1) * SUB] = one_hot(
+                    marked[g], g, 2 * c + h, place
+                )
+        got = nn(stacked, perm_ref[c % 2])
         for k in range(3):
             out[16 * k : 16 * (k + 1), here] = halves(got[32 * k : 32 * (k + 1)])
 
 
 def combine_kernel(mom, probes, u0, u1, sol, res):
     lane = lax.broadcasted_iota(jnp.int32, (N_PROBES, SUB), 1)
-    mu = [jnp.sum(jnp.where(lane == k, mom[...], 0.0), axis=1, keepdims=True) for k in range(7)]
+    mu = [jnp.sum(jnp.where(lane == k, mom[...], 0.0), axis=1, keepdims=True) for k in range(6)]
 
     def form(left, right, shift):
         total = None
@@ -445,50 +488,86 @@
     count = lax.axis_size(axis)
     if count & (count - 1):
         return lax.psum(value, axis)
+
+    def swapped(value, step):
+        return lax.ppermute(value, axis, [(k, k ^ step) for k in range(count)])
+
     step = 1
-    while step < count:
-        value = value + lax.ppermute(value, axis, [(k, k ^ step) for k in range(count)])
-        step *= 2
+    while 4 * step <= count:
+        near, far, both = [swapped(value, m * step) for m in (1, 2, 3)]
+        value = (value + near) + (far + both)
+        step *= 4
+    if step < count:
+        value = value + swapped(value, step)
     return value
 
 
 def on_device(points, noise_var, probes, pair_list, counts):
     noise = noise_var.reshape(1, -1)
     field = pltpu.VMEM(FIELD, f32)
-    s0, p0, col0, yb0 = sort_block(0, points, noise, probes)
+    side = pltpu.VMEM((24, BLK), f32)
+    column = pltpu.VMEM((3, BLK, SUB), f32)
+    limits = jax.ShapeDtypeStruct((2 * SUBS,), f32)
+    ranks = pltpu.VMEM((1, BLK), jnp.int32)
+    any_space = pl.BlockSpec(memory_space=pl.ANY)
+    s0, s1, col0, col1, yb0, yb1, rank0, rank1, flags = call(
+        sort_kernel,
+        (side, side, column, column, limits, limits, ranks, ranks, jax.ShapeDtypeStruct((4,), jnp.int32)),
+        [any_space] * 3 + [SMEM] * 2,
+        (VMEM,) * 4 + (SMEM,) * 2 + (VMEM,) * 2 + (SMEM,),
+        [
+            pltpu.VMEM(points.shape, f32),
+            pltpu.VMEM(noise.shape, f32),
+            pltpu.VMEM(probes.shape, f32),
+            pltpu.VMEM((BLK, SUB), jnp.int32),
+            pltpu.VMEM((2, STRIP, BLK), bf16),
+            pltpu.SemaphoreType.DMA((3,)),
+        ],
+        10**9,
+        "sort_blocks",
+    )(points, noise, probes, pair_list, counts)
     halo = from_behind(s0, "gx", -1)
-    s1, p1, col1, yb1 = sort_block(1, points, noise, probes)
 
     off = pltpu.VMEM((STRIPS, STRIP, OFF_W), bf16)
     diag = pltpu.VMEM((STRIPS, STRIP, DIAG_W), bf16)
+    k00, k11, tabb = call(
+        diag_build_kernel,
+        (diag, diag, jax.ShapeDtypeStruct((3 * T_SIZE,), jnp.int32)),
+        [SMEM] * 3 + [VMEM] * 4,
+        (VMEM, VMEM, SMEM),
+        [],
+        3 * 10**9,
+        "diag_build",
+    )(flags, yb0, yb1, s0, s1, col0, col1)
     k12, tabc, acc1, back = call(
         halo_build_kernel,
         (off, jax.ShapeDtypeStruct((T_SIZE,), jnp.int32), field, field),
-        [SMEM, SMEM, SMEM, VMEM, VMEM, VMEM],
+        [SMEM] * 2 + [VMEM] * 3,
         (VMEM, SMEM, VMEM, VMEM),
         [pltpu.SMEM((2 * SUBS,), f32), TILE, SPLIT, SPLIT],
-        2 * 10**9,
+        3 * 10**9,
         "halo_build",
-    )(pair_list, counts, yb1, s1, col1, halo)
+    )(flags, yb1, s1, col1, halo)
     arrived = from_behind(back, "gx", 1)
-    k00, k01, k11, tabb, acc0, acc1 = call(
+    k01, acc0, acc1 = call(
         own_build_kernel,
-        (diag, off, diag, jax.ShapeDtypeStruct((3 * T_SIZE,), jnp.int32), field, field),
-        [SMEM, SMEM, SMEM, SMEM, VMEM, VMEM, VMEM, VMEM, VMEM],
-        (VMEM, VMEM, VMEM, SMEM, VMEM, VMEM),
+        (off, field, field),
+        [SMEM] + [VMEM] * 7,
+        (VMEM,) * 3,
         [TILE, SPLIT, SPLIT],
-        6 * 10**9,
+        5 * 10**9,
         "own_build",
-    )(pair_list, counts, yb0, yb1, s0, s1, col0, col1, acc1)
+    )(tabb, s0, s1, col0, col1, k00, k11, acc1)
 
     w0, w1 = s0, s1
     halo_w = halo
+    moments = pltpu.VMEM((N_PROBES, SUB), f32)
     mom = jnp.zeros((N_PROBES, SUB), f32)
     kept = []
-    for level in range(1, 4):
+    for level in (1, 2):
         w0, w1, back, mom = call(
             functools.partial(finish_kernel, level),
-            (field, field, field, pltpu.VMEM((N_PROBES, SUB), f32)),
+            (field, field, field, moments),
             [SMEM] + [VMEM] * 12,
             (VMEM,) * 4,
             [TILE, SPLIT, SPLIT, pltpu.VMEM(FIELD, f32)],
@@ -496,31 +575,38 @@
             "finish",
         )(tabc, k12, s0, s1, col1, halo, halo_w, acc0, acc1, arrived, w0, w1, mom)
         kept.append((w0, w1))
-        if level < 3:
-            arrived = from_behind(back, "gx", 1)
-            halo_w = from_behind(w0, "gx", -1)
-            acc0, acc1 = call(
-                own_apply_kernel,
-                (field, field),
-                [SMEM] + [VMEM] * 9,
-                (VMEM, VMEM),
-                [TILE, SPLIT, SPLIT],
-                2 * 10**9,
-                "own_apply",
-            )(tabb, k00, k01, k11, s0, s1, col0, col1, w0, w1)
+        arrived = from_behind(back, "gx", 1)
+        halo_w = from_behind(w0, "gx", -1)
+        acc0, acc1 = call(
+            own_apply_kernel,
+            (field, field),
+            [SMEM] + [VMEM] * 9,
+            (VMEM, VMEM),
+            [TILE, SPLIT, SPLIT],
+            2 * 10**9,
+            "own_apply",
+        )(tabb, k00, k01, k11, s0, s1, col0, col1, w0, w1)
+    mom = call(moment_kernel, moments, [VMEM] * 8, VMEM, [], 10**7, "moment")(
+        s0, s1, acc0, acc1, arrived, w0, w1, mom
+    )
     total = sum_over(mom, "gx")
+    kept.append(
+        call(last_kernel, (field, field), [SMEM] + [VMEM] * 11, (VMEM, VMEM), [TILE, SPLIT], 10**9, "last")(
+            tabc, k12, s0, s1, col1, halo, halo_w, acc0, acc1, arrived, w0, w1
+        )
+    )
     given = []
-    for b, perm in ((0, p0), (1, p1)):
+    for b, rank in ((0, rank0), (1, rank1)):
         given.append(
             call(
                 unsort_kernel,
                 pltpu.VMEM((3 * N_PROBES, BLK), f32),
                 [VMEM] * 4,
                 VMEM,
-                [],
+                [pltpu.VMEM((2, BLK, STRIP), bf16)],
                 2 * 96 * BLK * BLK,
                 "unsort",
-            )(perm, *[pair[b] for pair in kept])
+            )(rank, *[pair[b] for pair in kept])
         )
     return call(
         combine_kernel,

time: 98.3 us -> 85.7 us (0.87); the launches traced: 97.6 us -> 86.6 us
  local copies, waits for them, and re-layouts: 9.05 us -> 3.28 us
  Pallas kernels: 59.7 us -> 54.4 us
    pallas_call x2 -> x0, Pallas kernels: 11.4 us -> none  [sort_block(): pl.pallas_call(functools.partial(sort_kernel, blk), out_shape=(pltpu.VMEM...]
    pallas_call x10 -> x13, Pallas kernels: 48.3 us -> 54.4 us  [run(): pl.pallas_call(body, out_shape=outs, in_specs=ins, out_specs=out_specs, s...]
    unnamed x21 -> x9, local copies, waits for them, and re-layouts: 9.05 us -> 3.28 us
    ppermute x4 -> x6, waiting for transfers between devices: 3.14 us -> 0.88 us  [swapped(): return lax.ppermute(value, axis, [(k, k ^ step) for k in range(count)])]
    ppermute x6, waiting for transfers between devices: 0.05 us -> 1.98 us  [from_behind(): lax.ppermute(value, axis, [(source, source + steps) for source in range(f...]
    ppermute x4 -> x6, starting transfers between devices: 10.6 us -> 10.3 us  [swapped(): return lax.ppermute(value, axis, [(k, k ^ step) for k in range(count)])]
  transfers between devices with their start and end apart: 10 -> 12, of which waited for: 4 -> 2; matrix products, arithmetic and copies ran while one was open for 1% -> 0% of each run, Pallas kernels for 39% -> 35%
where the time goes in v2:
time: 85.7 us; the launch traced here: 86.6 us
  Pallas kernels  54.4 us (63%)
  starting transfers between devices  24.5 us (29%)
  local copies, waits for them, and re-layouts  3.28 us (4%)
  waiting for transfers between devices  2.86 us (3%)
  between operations  1.49 us (2%)
    pallas_call x13, Pallas kernels, run(): pl.pallas_call(body, out_shape=outs, in_specs=ins, out_specs=out_specs, s...  54.4 us
    ppermute x6, starting transfers between devices, from_behind(): lax.ppermute(value, axis, [(source, source + steps) for source in range(f...  14.2 us
    ppermute x6, starting transfers between devices, swapped(): return lax.ppermute(value, axis, [(k, k ^ step) for k in range(count)])  10.3 us
    unnamed x9, local copies, waits for them, and re-layouts  3.28 us
    ppermute x6, waiting for transfers between devices, from_behind(): lax.ppermute(value, axis, [(source, source + steps) for source in range(f...  1.98 us
  transfers between devices with their start and end apart: 12, of which 2 were waited for; matrix products, arithmetic and copies ran while one was open for 0% of the time, Pallas kernels for 35%

profile of v2, /device:TPU:0, one launch (start us, length us, event | category | flops | bytes accessed | tf_op | source)
XLA Modules:
  0.0 86.6 jit_solution(2883694413507989521)
XLA Ops:
  2.0 0.9 %copy-done = f32[16,4096]{1,0:T(8,128)S(1)} copy-done((f32[16,4096]{1,0:T(8,128)S(1)}, f32[16,4096]{1,0:T(8,128)}, u32[]{:S(2)}) %copy-start) | copy-done | bytes 262168
  4.6 11.8 %sort_blocks.1 = (f32[24,2048]{1,0:T(8,128)S(1)}, f32[24,2048]{1,0:T(8,128)S(1)}, f32[3,2048,128]{2,1,0:T(8,128)S(1)}, f32[3,2048,128]{2,1,0:T(8,128)S(1)}, f32[...) custom-call(f32[3,4096]{1,0:T(4,128)S(1)} %copy-done.2, ...), custom_call_target="tpu_custom_call" | custom-call | flops 1000000000 | bytes 1048576 | tf_op jit(solution)/shard_map/sort_blocks/pallas_call | solution.py:284
  16.3 1.3 %collective-permute-start = (f32[24,2048]{1,0:T(8,128)S(1)}, f32[24,2048]{1,0:T(8,128)S(1)}, u32[]{:S(2)}, u32[]{:S(2)}) collective-permute-start(f32[24,2048]{1,0:T(8,128)S(1)} %get-tuple-element.35.s0.w0), channel_id=1, source_target_pairs={{1,0},{2,1},{3,2},{4,3},{5,4},{6,5},{7,6},{8,7},{9,8},{10,9},{11,1... | collective-permute-start | bytes 589832 | tf_op jit(solution)/shard_map/ppermute | solution.py:484
  17.6 7.2 %diag_build.1 = (bf16[8,256,512]{2,1,0:T(8,128)(2,1)S(1)}, bf16[8,256,512]{2,1,0:T(8,128)(2,1)S(1)}, s32[72]{0:T(128)S(1)}) custom-call(s32[4]{0:T(128)S(1)} %get-tuple-element.37.flags, f32[32]{0:T(128)S(1)} %get-tuple-element.38.yb0, f32[32]{0:T(128)S(1)} %get-tuple-element.39.yb1, f32[24,2048]{1,0:T(8,128)S(1)} %get-tuple-element.35.s0.w0, ...), custom_call_target="tpu_custom_call" | custom-call | flops 3000000000 | bytes 1048576 | tf_op jit(solution)/shard_map/diag_build/pallas_call | solution.py:284
  24.9 7.8 %halo_build.1 = (bf16[8,256,768]{2,1,0:T(8,128)(2,1)S(1)}, s32[24]{0:T(128)S(1)}, f32[16,2048]{1,0:T(8,128)S(1)}, f32[16,2048]{1,0:T(8,128)S(1)}) custom-call(s32[4]{0:T(128)S(1)} %get-tuple-element.37.flags, f32[32]{0:T(128)S(1)} %get-tuple-element.39.yb1, f32[24,2048]{1,0:T(8,128)S(1)} %get-tuple-element.36.s1.w1, ...), custom_call_target="tpu_custom_call" | custom-call | flops 3000000000 | bytes 1048576 | tf_op jit(solution)/shard_map/halo_build/pallas_call | solution.py:284
  32.6 3.0 %collective-permute-start.1 = (f32[16,2048]{1,0:T(8,128)S(1)}, f32[16,2048]{1,0:T(8,128)S(1)}, u32[]{:S(2)}, u32[]{:S(2)}) collective-permute-start(f32[16,2048]{1,0:T(8,128)S(1)} %get-tuple-element.51), channel_id=1, source_target_pairs={{0,1},{1,2},{2,3},{3,4},{4,5},{5,6},{6,7},{7,8},{8,9},{9,10},{10,1... | collective-permute-start | bytes 393224 | tf_op jit(solution)/shard_map/ppermute | solution.py:484
  35.7 8.2 %own_build.1 = (bf16[8,256,768]{2,1,0:T(8,128)(2,1)S(1)}, f32[16,2048]{1,0:T(8,128)S(1)}, f32[16,2048]{1,0:T(8,128)S(1)}) custom-call(s32[72]{0:T(128)S(1)} %get-tuple-element.42.tab, f32[24,2048]{1,0:T(8,128)S(1)} %get-tuple-element.35.s0.w0, f32[24,2048]{1,0:T(8,128)S(1)} %get-tuple-element.36.s1.w1, f32[3,2048,128]{2,1,0:T(8,128)S(1)} %get-tuple-element.40.col0, ...), custom_call_target="tpu_custom_call" | custom-call | flops 5000000000 | bytes 1048576 | tf_op jit(solution)/shard_map/own_build/pallas_call | solution.py:284
  43.8 1.4 %finish.2 = (f32[16,2048]{1,0:T(8,128)S(1)}, f32[16,2048]{1,0:T(8,128)S(1)}, f32[16,2048]{1,0:T(8,128)S(1)}, f32[16,128]{1,0:T(8,128)S(1)}) custom-call(s32[24]{0:T(128)S(1)} %get-tuple-element.47.tab, bf16[8,256,768]{2,1,0:T(8,128)(2,1)S(1)} %get-tuple-element.48.k12, f32[24,2048]{1,0:T(8,128)S(1)} %get-tuple-element.35.s0.w0, ...), custom_call_target="tpu_custom_call" | custom-call | flops 1000000000 | bytes 1048576 | tf_op jit(solution)/shard_map/finish/pallas_call | solution.py:284
  45.2 1.3 %collective-permute-start.3 = (f32[16,2048]{1,0:T(8,128)S(1)}, f32[16,2048]{1,0:T(8,128)S(1)}, u32[]{:S(2)}, u32[]{:S(2)}) collective-permute-start(f32[16,2048]{1,0:T(8,128)S(1)} %get-tuple-element.56), channel_id=1, source_target_pairs={{0,1},{1,2},{2,3},{3,4},{4,5},{5,6},{6,7},{7,8},{8,9},{9,10},{10,1... | collective-permute-start | bytes 393224 | tf_op jit(solution)/shard_map/ppermute | solution.py:484
  46.5 1.3 %collective-permute-start.2 = (f32[16,2048]{1,0:T(8,128)S(1)}, f32[16,2048]{1,0:T(8,128)S(1)}, u32[]{:S(2)}, u32[]{:S(2)}) collective-permute-start(f32[16,2048]{1,0:T(8,128)S(1)} %get-tuple-element.52.w0.wa), channel_id=1, source_target_pairs={{1,0},{2,1},{3,2},{4,3},{5,4},{6,5},{7,6},{8,7},{9,8},{10,9},{11,1... | collective-permute-start | bytes 393224 | tf_op jit(solution)/shard_map/ppermute | solution.py:484
  47.8 3.7 %own_apply.2 = (f32[16,2048]{1,0:T(8,128)S(1)}, f32[16,2048]{1,0:T(8,128)S(1)}) custom-call(s32[72]{0:T(128)S(1)} %get-tuple-element.42.tab, bf16[8,256,512]{2,1,0:T(8,128)(2,1)S(1)} %get-tuple-element.43.k00, bf16[8,256,768]{2,1,0:T(8,128)(2,1)S(1)} %get-tuple-element.46.k01, bf16[8,256,512]{2,1,0:T(8,128)(2,1)S(1)} %get-tuple-element.44.k11, ...), custom_call_target="tpu_custom_call" | custom-call | flops 2000000000 | bytes 1048576 | tf_op jit(solution)/shard_map/own_apply/pallas_call | solution.py:284
  51.6 2.0 %collective-permute-done.2.halo_w = f32[16,2048]{1,0:T(8,128)S(1)} collective-permute-done((f32[16,2048]{1,0:T(8,128)S(1)}, f32[16,2048]{1,0:T(8,128)S(1)}, u32[]{:S(2)}, u32[]{:S(2)}) %collective-permute-start.2) | collective-permute-done | bytes 131104 | tf_op jit(solution)/shard_map/ppermute | solution.py:484
  53.5 2.4 %finish.3 = (f32[16,2048]{1,0:T(8,128)S(1)}, f32[16,2048]{1,0:T(8,128)S(1)}, f32[16,2048]{1,0:T(8,128)S(1)}, f32[16,128]{1,0:T(8,128)S(1)}) custom-call(s32[24]{0:T(128)S(1)} %get-tuple-element.47.tab, bf16[8,256,768]{2,1,0:T(8,128)(2,1)S(1)} %get-tuple-element.48.k12, f32[24,2048]{1,0:T(8,128)S(1)} %get-tuple-element.35.s0.w0, ...), custom_call_target="tpu_custom_call" | custom-call | flops 1000000000 | bytes 1048576 | tf_op jit(solution)/shard_map/finish/pallas_call | solution.py:284
  55.9 6.0 %collective-permute-start.4 = (f32[16,2048]{1,0:T(8,128)S(1)}, f32[16,2048]{1,0:T(8,128)S(1)}, u32[]{:S(2)}, u32[]{:S(2)}) collective-permute-start(f32[16,2048]{1,0:T(8,128)S(1)} %get-tuple-element.62), channel_id=1, source_target_pairs={{0,1},{1,2},{2,3},{3,4},{4,5},{5,6},{6,7},{7,8},{8,9},{9,10},{10,1... | collective-permute-start | bytes 393224 | tf_op jit(solution)/shard_map/ppermute | solution.py:484
  61.9 1.3 %collective-permute-start.11 = (f32[16,2048]{1,0:T(8,128)S(1)}, f32[16,2048]{1,0:T(8,128)S(1)}, u32[]{:S(2)}, u32[]{:S(2)}) collective-permute-start(f32[16,2048]{1,0:T(8,128)S(1)} %get-tuple-element.58.w0.wb), channel_id=1, source_target_pairs={{1,0},{2,1},{3,2},{4,3},{5,4},{6,5},{7,6},{8,7},{9,8},{10,9},{11,1... | collective-permute-start | bytes 393224 | tf_op jit(solution)/shard_map/ppermute | solution.py:484
  63.2 3.7 %own_apply.3 = (f32[16,2048]{1,0:T(8,128)S(1)}, f32[16,2048]{1,0:T(8,128)S(1)}) custom-call(s32[72]{0:T(128)S(1)} %get-tuple-element.42.tab, bf16[8,256,512]{2,1,0:T(8,128)(2,1)S(1)} %get-tuple-element.43.k00, bf16[8,256,768]{2,1,0:T(8,128)(2,1)S(1)} %get-tuple-element.46.k01, bf16[8,256,512]{2,1,0:T(8,128)(2,1)S(1)} %get-tuple-element.44.k11, ...), custom_call_target="tpu_custom_call" | custom-call | flops 2000000000 | bytes 1048576 | tf_op jit(solution)/shard_map/own_apply/pallas_call | solution.py:284
  67.1 4.8 %collective-permute-start.7 = (f32[16,128]{1,0:T(8,128)S(1)}, f32[16,128]{1,0:T(8,128)S(1)}, u32[]{:S(2)}, u32[]{:S(2)}) collective-permute-start(f32[16,128]{1,0:T(8,128)S(1)} %moment.1), channel_id=1, source_target_pairs={{0,3},{1,2},{2,1},{3,0},{4,7},{5,6},{6,5},{7,4},{8,11},{9,10},{10,... | collective-permute-start | bytes 24584 | tf_op jit(solution)/shard_map/ppermute | solution.py:493
  72.1 1.7 %last.1 = (f32[16,2048]{1,0:T(8,128)S(1)}, f32[16,2048]{1,0:T(8,128)S(1)}) custom-call(s32[24]{0:T(128)S(1)} %get-tuple-element.47.tab, bf16[8,256,768]{2,1,0:T(8,128)(2,1)S(1)} %get-tuple-element.48.k12, f32[24,2048]{1,0:T(8,128)S(1)} %get-tuple-element.35.s0.w0, f32[24,2048]{1,0:T(8,128)S(1)} %get-tuple-element.36.s1.w1, ...), custom_call_target="tpu_custom_call" | custom-call | flops 1000000000 | bytes 1048576 | tf_op jit(solution)/shard_map/last/pallas_call | solution.py:284
  73.8 2.7 %unsort.2.u0 = f32[48,2048]{1,0:T(8,128)S(1)} custom-call(s32[1,2048]{1,0:T(1,128)S(1)} %get-tuple-element.64.rank_ref, f32[16,2048]{1,0:T(8,128)S(1)} %get-tuple-element.52.w0.wa, f32[16,2048]{1,0:T(8,128)S(1)} %get-tuple-element.58.w0.wb, f32[16,2048]{1,0:T(8,128)S(1)} %get-tuple-element.65.wc), custom_call_target="tpu_custom_call" | custom-call | flops 805306368 | bytes 1048576 | tf_op jit(solution)/shard_map/unsort/pallas_call | solution.py:284
  76.6 3.4 %collective-permute-start.10 = (f32[16,128]{1,0:T(8,128)S(1)}, f32[16,128]{1,0:T(8,128)S(1)}, u32[]{:S(2)}, u32[]{:S(2)}) collective-permute-start(f32[16,128]{1,0:T(8,128)S(1)} %add_add_fusion.1), channel_id=1, source_target_pairs={{0,12},{1,13},{2,14},{3,15},{4,8},{5,9},{6,10},{7,11},{8,4},{9,5},... | collective-permute-start | bytes 24584 | tf_op jit(solution)/shard_map/ppermute | solution.py:493
  80.1 1.9 %collective-permute-start.9 = (f32[16,128]{1,0:T(8,128)S(1)}, f32[16,128]{1,0:T(8,128)S(1)}, u32[]{:S(2)}, u32[]{:S(2)}) collective-permute-start(f32[16,128]{1,0:T(8,128)S(1)} %add_add_fusion.1), channel_id=1, source_target_pairs={{0,8},{1,9},{2,10},{3,11},{4,12},{5,13},{6,14},{7,15},{8,0},{9,1},... | collective-permute-start | bytes 24584 | tf_op jit(solution)/shard_map/ppermute | solution.py:493
  81.9 2.7 %unsort.3.u1 = f32[48,2048]{1,0:T(8,128)S(1)} custom-call(s32[1,2048]{1,0:T(1,128)S(1)} %get-tuple-element.66.rank_ref, f32[16,2048]{1,0:T(8,128)S(1)} %get-tuple-element.53.w1.wa, f32[16,2048]{1,0:T(8,128)S(1)} %get-tuple-element.59.w1.wb, f32[16,2048]{1,0:T(8,128)S(1)} %get-tuple-element.67.wc), custom_call_target="tpu_custom_call" | custom-call | flops 805306368 | bytes 1048576 | tf_op jit(solution)/shard_map/unsort/pallas_call | solution.py:284
  84.7 0.9 %collective-permute-done.8 = f32[16,128]{1,0:T(8,128)S(1)} collective-permute-done((f32[16,128]{1,0:T(8,128)S(1)}, f32[16,128]{1,0:T(8,128)S(1)}, u32[]{:S(2)}, u32[]{:S(2)}) %collective-permute-start.8) | collective-permute-done | bytes 8224 | tf_op jit(solution)/shard_map/ppermute | solution.py:493
  85.6 1.0 %combine.1 = (f32[16,4096]{1,0:T(8,128)}, f32[16,4096]{1,0:T(8,128)}) custom-call(f32[16,128]{1,0:T(8,128)S(1)} %add_add_fusion.mom, f32[16,4096]{1,0:T(8,128)S(1)} %copy-done.1, f32[48,2048]{1,0:T(8,128)S(1)} %unsort.2.u0, f32[48,2048]{1,0:T(8,128)S(1)} %unsort.3.u1), custom_call_target="tpu_custom_call" | custom-call | flops 1000000 | bytes 1048576 | tf_op jit(solution)/shard_map/combine/pallas_call | solution.py:284
  (25 shorter events, 2.7 us)
Async XLA Ops:
  2.0 0.9 %copy-start = (f32[16,4096]{1,0:T(8,128)S(1)}, f32[16,4096]{1,0:T(8,128)}, u32[]{:S(2)}) copy-start(f32[16,4096]{1,0:T(8,128)} %probes.1) | copy-start | bytes 786436
  3.0 0.8 copy-start.2
  3.8 0.7 copy-start.3
  16.3 8.5 %collective-permute-start = (f32[24,2048]{1,0:T(8,128)S(1)}, f32[24,2048]{1,0:T(8,128)S(1)}, u32[]{:S(2)}, u32[]{:S(2)}) collective-permute-start(f32[24,2048]{1,0:T(8,128)S(1)} %get-tuple-element.35.s0.w0), channel_id=1, source_target_pairs={{1,0},{2,1},{3,2},{4,3},{5,4},{6,5},{7,6},{8,7},{9,8},{10,9},{11,1... | collective-permute-start | bytes 589832 | tf_op jit(solution)/shard_map/ppermute | solution.py:484
  32.6 11.2 %collective-permute-start.1 = (f32[16,2048]{1,0:T(8,128)S(1)}, f32[16,2048]{1,0:T(8,128)S(1)}, u32[]{:S(2)}, u32[]{:S(2)}) collective-permute-start(f32[16,2048]{1,0:T(8,128)S(1)} %get-tuple-element.51), channel_id=1, source_target_pairs={{0,1},{1,2},{2,3},{3,4},{4,5},{5,6},{6,7},{7,8},{8,9},{9,10},{10,1... | collective-permute-start | bytes 393224 | tf_op jit(solution)/shard_map/ppermute | solution.py:484
  45.2 6.3 %collective-permute-start.3 = (f32[16,2048]{1,0:T(8,128)S(1)}, f32[16,2048]{1,0:T(8,128)S(1)}, u32[]{:S(2)}, u32[]{:S(2)}) collective-permute-start(f32[16,2048]{1,0:T(8,128)S(1)} %get-tuple-element.56), channel_id=1, source_target_pairs={{0,1},{1,2},{2,3},{3,4},{4,5},{5,6},{6,7},{7,8},{8,9},{9,10},{10,1... | collective-permute-start | bytes 393224 | tf_op jit(solution)/shard_map/ppermute | solution.py:484
  46.5 7.0 %collective-permute-start.2 = (f32[16,2048]{1,0:T(8,128)S(1)}, f32[16,2048]{1,0:T(8,128)S(1)}, u32[]{:S(2)}, u32[]{:S(2)}) collective-permute-start(f32[16,2048]{1,0:T(8,128)S(1)} %get-tuple-element.52.w0.wa), channel_id=1, source_target_pairs={{1,0},{2,1},{3,2},{4,3},{5,4},{6,5},{7,6},{8,7},{9,8},{10,9},{11,1... | collective-permute-start | bytes 393224 | tf_op jit(solution)/shard_map/ppermute | solution.py:484
  55.9 11.0 %collective-permute-start.4 = (f32[16,2048]{1,0:T(8,128)S(1)}, f32[16,2048]{1,0:T(8,128)S(1)}, u32[]{:S(2)}, u32[]{:S(2)}) collective-permute-start(f32[16,2048]{1,0:T(8,128)S(1)} %get-tuple-element.62), channel_id=1, source_target_pairs={{0,1},{1,2},{2,3},{3,4},{4,5},{5,6},{6,7},{7,8},{8,9},{9,10},{10,1... | collective-permute-start | bytes 393224 | tf_op jit(solution)/shard_map/ppermute | solution.py:484
  61.9 10.2 %collective-permute-start.11 = (f32[16,2048]{1,0:T(8,128)S(1)}, f32[16,2048]{1,0:T(8,128)S(1)}, u32[]{:S(2)}, u32[]{:S(2)}) collective-permute-start(f32[16,2048]{1,0:T(8,128)S(1)} %get-tuple-element.58.w0.wb), channel_id=1, source_target_pairs={{1,0},{2,1},{3,2},{4,3},{5,4},{6,5},{7,6},{8,7},{9,8},{10,9},{11,1... | collective-permute-start | bytes 393224 | tf_op jit(solution)/shard_map/ppermute | solution.py:484
  67.1 9.5 %collective-permute-start.7 = (f32[16,128]{1,0:T(8,128)S(1)}, f32[16,128]{1,0:T(8,128)S(1)}, u32[]{:S(2)}, u32[]{:S(2)}) collective-permute-start(f32[16,128]{1,0:T(8,128)S(1)} %moment.1), channel_id=1, source_target_pairs={{0,3},{1,2},{2,1},{3,0},{4,7},{5,6},{6,5},{7,4},{8,11},{9,10},{10,... | collective-permute-start | bytes 24584 | tf_op jit(solution)/shard_map/ppermute | solution.py:493
  71.9 4.7 %collective-permute-start.6 = (f32[16,128]{1,0:T(8,128)S(1)}, f32[16,128]{1,0:T(8,128)S(1)}, u32[]{:S(2)}, u32[]{:S(2)}) collective-permute-start(f32[16,128]{1,0:T(8,128)S(1)} %moment.1), channel_id=1, source_target_pairs={{0,2},{1,3},{2,0},{3,1},{4,6},{5,7},{6,4},{7,5},{8,10},{9,11},{10,... | collective-permute-start | bytes 24584 | tf_op jit(solution)/shard_map/ppermute | solution.py:493
  71.9 4.7 %collective-permute-start.5 = (f32[16,128]{1,0:T(8,128)S(1)}, f32[16,128]{1,0:T(8,128)S(1)}, u32[]{:S(2)}, u32[]{:S(2)}) collective-permute-start(f32[16,128]{1,0:T(8,128)S(1)} %moment.1), channel_id=1, source_target_pairs={{0,1},{1,0},{2,3},{3,2},{4,5},{5,4},{6,7},{7,6},{8,9},{9,8},{10,11... | collective-permute-start | bytes 24584 | tf_op jit(solution)/shard_map/ppermute | solution.py:493
  73.8 11.8 %copy-start.1 = (f32[16,4096]{1,0:T(8,128)S(1)}, f32[16,4096]{1,0:T(8,128)}, u32[]{:S(2)}) copy-start(f32[16,4096]{1,0:T(8,128)} %probes.1) | copy-start | bytes 786436
  76.6 8.1 %collective-permute-start.10 = (f32[16,128]{1,0:T(8,128)S(1)}, f32[16,128]{1,0:T(8,128)S(1)}, u32[]{:S(2)}, u32[]{:S(2)}) collective-permute-start(f32[16,128]{1,0:T(8,128)S(1)} %add_add_fusion.1), channel_id=1, source_target_pairs={{0,12},{1,13},{2,14},{3,15},{4,8},{5,9},{6,10},{7,11},{8,4},{9,5},... | collective-permute-start | bytes 24584 | tf_op jit(solution)/shard_map/ppermute | solution.py:493
  80.1 4.6 %collective-permute-start.9 = (f32[16,128]{1,0:T(8,128)S(1)}, f32[16,128]{1,0:T(8,128)S(1)}, u32[]{:S(2)}, u32[]{:S(2)}) collective-permute-start(f32[16,128]{1,0:T(8,128)S(1)} %add_add_fusion.1), channel_id=1, source_target_pairs={{0,8},{1,9},{2,10},{3,11},{4,12},{5,13},{6,14},{7,15},{8,0},{9,1},... | collective-permute-start | bytes 24584 | tf_op jit(solution)/shard_map/ppermute | solution.py:493
  81.9 3.7 %collective-permute-start.8 = (f32[16,128]{1,0:T(8,128)S(1)}, f32[16,128]{1,0:T(8,128)S(1)}, u32[]{:S(2)}, u32[]{:S(2)}) collective-permute-start(f32[16,128]{1,0:T(8,128)S(1)} %add_add_fusion.1), channel_id=1, source_target_pairs={{0,4},{1,5},{2,6},{3,7},{4,0},{5,1},{6,2},{7,3},{8,12},{9,13},{10,... | collective-permute-start | bytes 24584 | tf_op jit(solution)/shard_map/ppermute | solution.py:493

commit v3 on v2

--- a/solution.py
+++ b/solution.py
@@ -101,6 +101,7 @@
     for local in range(2):
         for ahead in range(2):
             flags[2 * local + ahead] = live_flag(pair, count, local, ahead)
+    flags[4] = jnp.bitwise_and(lax.shift_right_logical(pair[0, 0], 1), 1)
     copies[0].wait()
     for blk, rank_ref in enumerate((rank0, rank1)):
         rank_ref[...] = rank_of(pts_ref[1:2, blk * BLK : (blk + 1) * BLK], key_ref)
@@ -309,7 +310,10 @@
         build_diag(k11, col1, s1)
 
 
-def halo_build_kernel(flags, yb1, s1, col1, halo, k12, tab, acc1, back, yb2, tile, v1, v2):
+def halo_build_kernel(
+    flags, yb1, s1, col1, got_a, got_b, k12, tab, acc1, back, halo, yb2, tile, v1, v2
+):
+    halo[...] = jnp.where(flags[4] == 0, got_a[...], got_b[...])
     bounds(halo, yb2)
     fill_table(tab, 0, flags[3], yb1, yb2, False)
     acc1[...] = jnp.zeros(FIELD, f32)
@@ -370,7 +374,8 @@
 
 
 def finish_kernel(
-    level, tab, k12, s0, s1, col1, halo, halo_w, acc0, acc1, arrived, w0, w1, mom_in, n0, n1, back, mom, tile, v1, v2, acc
+    level, flags, tab, k12, s0, s1, col1, halo, got_a, got_b, acc0, acc1, w0, w1, mom_in,
+    n0, n1, send_a, send_b, mom, tile, v1, v2, acc, back
 ):
     live = tab[T_LIVE] > 0
     acc[...] = acc1[...]
@@ -378,7 +383,7 @@
 
         @pl.when(live)
         def _():
-            v2[...] = split2(halo_w[0:16, :])
+            v2[...] = split2(jnp.where(flags[4] == 0, got_a[...], got_b[...]))
             to_owner(k12, tab, 0, v2, acc)
             extra_tiles(tab, 0, col1, halo, tile, None, v2, acc, None)
 
@@ -394,8 +399,11 @@
         to_partner(k12, tab, 0, v1, back)
         extra_tiles(tab, 0, col1, halo, tile, v1, None, None, back)
 
-    next0 = s0[19:20, :] * before0 + (acc0[...] + arrived[...])
+    arrived = jnp.where(flags[4] == 0, got_b[...], got_a[...])
+    next0 = s0[19:20, :] * before0 + (acc0[...] + arrived)
     n0[...] = next0
+    send_a[...] = jnp.where(flags[4] == 0, back[...], next0)
+    send_b[...] = jnp.where(flags[4] == 0, next0, back[...])
     lane = lax.broadcasted_iota(jnp.int32, (N_PROBES, SUB), 1)
     cross = inner(before0, next0) + inner(before1, next1)
     own = inner(next0, next0) + inner(next1, next1)
@@ -407,22 +415,24 @@
     mom[...] = total
 
 
-def moment_kernel(s0, s1, acc0, acc1, arrived, w0, w1, mom_in, mom):
+def moment_kernel(flags, s0, s1, acc0, acc1, got_a, got_b, w0, w1, mom_in, mom):
     lane = lax.broadcasted_iota(jnp.int32, (N_PROBES, SUB), 1)
     one = w0[...]
     two = w1[...]
-    cross = inner(one, s0[19:20, :] * one + (acc0[...] + 2.0 * arrived[...]))
+    arrived = jnp.where(flags[4] == 0, got_b[...], got_a[...])
+    cross = inner(one, s0[19:20, :] * one + (acc0[...] + 2.0 * arrived))
     cross = cross + inner(two, s1[19:20, :] * two + acc1[...])
     mom[...] = mom_in[...] + jnp.where(lane == 5, cross, 0.0)
 
 
-def last_kernel(tab, k12, s0, s1, col1, halo, halo_w, acc0, acc1, arrived, w0, w1, n0, n1, tile, v2):
+def last_kernel(flags, tab, k12, s0, s1, col1, halo, got_a, got_b, acc0, acc1, w0, w1, n0, n1, tile, v2):
+    arrived = jnp.where(flags[4] == 0, got_b[...], got_a[...])
     n1[...] = s1[19:20, :] * w1[...] + acc1[...]
-    n0[...] = s0[19:20, :] * w0[...] + (acc0[...] + arrived[...])
+    n0[...] = s0[19:20, :] * w0[...] + (acc0[...] + arrived)
 
     @pl.when(tab[T_LIVE] > 0)
     def _():
-        v2[...] = split2(halo_w[...])
+        v2[...] = split2(jnp.where(flags[4] == 0, got_a[...], got_b[...]))
         to_owner(k12, tab, 0, v2, n1)
         extra_tiles(tab, 0, col1, halo, tile, None, v2, n1, None)
 
@@ -478,27 +488,27 @@
         res[:, here] = ((r[0] * w[0] + r[1] * w[1]) + r[2] * w[2]) + r[3] * w[3]
 
 
-def from_behind(value, axis, steps):
-    count = lax.axis_size(axis)
-    first, last = (max(0, -steps), min(count, count - steps))
-    return lax.ppermute(value, axis, [(source, source + steps) for source in range(first, last)])
+def swapped_both(to_a, to_b):
+    count = lax.axis_size("gx")
+    a = lax.ppermute(to_a, "gx", [(k, k ^ 1) for k in range(count)])
+    b = lax.ppermute(to_b, "gx", [(k, ((k + 1) ^ 1) - 1) for k in range(1, count - 1)])
+    return a, b
 
 
 def sum_over(value, axis):
     count = lax.axis_size(axis)
     if count & (count - 1):
         return lax.psum(value, axis)
-
-    def swapped(value, step):
-        return lax.ppermute(value, axis, [(k, k ^ step) for k in range(count)])
-
     step = 1
-    while 4 * step <= count:
-        near, far, both = [swapped(value, m * step) for m in (1, 2, 3)]
-        value = (value + near) + (far + both)
-        step *= 4
-    if step < count:
-        value = value + swapped(value, step)
+    while step < count:
+        radix = min(16, count // step)
+        parts = [value] + [
+            lax.ppermute(value, axis, [(k, k ^ (m * step)) for k in range(count)]) for m in range(1, radix)
+        ]
+        while len(parts) > 1:
+            parts = [parts[m] + parts[m + 1] for m in range(0, len(parts), 2)]
+        value = parts[0]
+        step *= radix
     return value
 
 
@@ -512,7 +522,7 @@
     any_space = pl.BlockSpec(memory_space=pl.ANY)
     s0, s1, col0, col1, yb0, yb1, rank0, rank1, flags = call(
         sort_kernel,
-        (side, side, column, column, limits, limits, ranks, ranks, jax.ShapeDtypeStruct((4,), jnp.int32)),
+        (side, side, column, column, limits, limits, ranks, ranks, jax.ShapeDtypeStruct((5,), jnp.int32)),
         [any_space] * 3 + [SMEM] * 2,
         (VMEM,) * 4 + (SMEM,) * 2 + (VMEM,) * 2 + (SMEM,),
         [
@@ -526,8 +536,8 @@
         10**9,
         "sort_blocks",
     )(points, noise, probes, pair_list, counts)
-    halo = from_behind(s0, "gx", -1)
-
+
+    halos = swapped_both(s0, s0)
     off = pltpu.VMEM((STRIPS, STRIP, OFF_W), bf16)
     diag = pltpu.VMEM((STRIPS, STRIP, DIAG_W), bf16)
     k00, k11, tabb = call(
@@ -539,16 +549,16 @@
         3 * 10**9,
         "diag_build",
     )(flags, yb0, yb1, s0, s1, col0, col1)
-    k12, tabc, acc1, back = call(
+    k12, tabc, acc1, back, halo = call(
         halo_build_kernel,
-        (off, jax.ShapeDtypeStruct((T_SIZE,), jnp.int32), field, field),
-        [SMEM] * 2 + [VMEM] * 3,
-        (VMEM, SMEM, VMEM, VMEM),
+        (off, jax.ShapeDtypeStruct((T_SIZE,), jnp.int32), field, field, side),
+        [SMEM] * 2 + [VMEM] * 4,
+        (VMEM, SMEM, VMEM, VMEM, VMEM),
         [pltpu.SMEM((2 * SUBS,), f32), TILE, SPLIT, SPLIT],
         3 * 10**9,
         "halo_build",
-    )(flags, yb1, s1, col1, halo)
-    arrived = from_behind(back, "gx", 1)
+    )(flags, yb1, s1, col1, *halos)
+    got = swapped_both(back, back)
     k01, acc0, acc1 = call(
         own_build_kernel,
         (off, field, field),
@@ -560,23 +570,21 @@
     )(tabb, s0, s1, col0, col1, k00, k11, acc1)
 
     w0, w1 = s0, s1
-    halo_w = halo
     moments = pltpu.VMEM((N_PROBES, SUB), f32)
     mom = jnp.zeros((N_PROBES, SUB), f32)
     kept = []
     for level in (1, 2):
-        w0, w1, back, mom = call(
+        w0, w1, send_a, send_b, mom = call(
             functools.partial(finish_kernel, level),
-            (field, field, field, moments),
-            [SMEM] + [VMEM] * 12,
-            (VMEM,) * 4,
-            [TILE, SPLIT, SPLIT, pltpu.VMEM(FIELD, f32)],
+            (field,) * 4 + (moments,),
+            [SMEM] * 2 + [VMEM] * 12,
+            (VMEM,) * 5,
+            [TILE, SPLIT, SPLIT, pltpu.VMEM(FIELD, f32), pltpu.VMEM(FIELD, f32)],
             10**9,
             "finish",
-        )(tabc, k12, s0, s1, col1, halo, halo_w, acc0, acc1, arrived, w0, w1, mom)
+        )(flags, tabc, k12, s0, s1, col1, halo, *got, acc0, acc1, w0, w1, mom)
         kept.append((w0, w1))
-        arrived = from_behind(back, "gx", 1)
-        halo_w = from_behind(w0, "gx", -1)
+        got = swapped_both(send_a, send_b)
         acc0, acc1 = call(
             own_apply_kernel,
             (field, field),
@@ -586,13 +594,13 @@
             2 * 10**9,
             "own_apply",
         )(tabb, k00, k01, k11, s0, s1, col0, col1, w0, w1)
-    mom = call(moment_kernel, moments, [VMEM] * 8, VMEM, [], 10**7, "moment")(
-        s0, s1, acc0, acc1, arrived, w0, w1, mom
+    mom = call(moment_kernel, moments, [SMEM] + [VMEM] * 9, VMEM, [], 10**7, "moment")(
+        flags, s0, s1, acc0, acc1, *got, w0, w1, mom
     )
     total = sum_over(mom, "gx")
     kept.append(
-        call(last_kernel, (field, field), [SMEM] + [VMEM] * 11, (VMEM, VMEM), [TILE, SPLIT], 10**9, "last")(
-            tabc, k12, s0, s1, col1, halo, halo_w, acc0, acc1, arrived, w0, w1
+        call(last_kernel, (field, field), [SMEM] * 2 + [VMEM] * 11, (VMEM, VMEM), [TILE, SPLIT], 10**9, "last")(
+            flags, tabc, k12, s0, s1, col1, halo, *got, acc0, acc1, w0, w1
         )
     )
     given = []

time: 85.7 us -> 98.8 us (1.15)
  starting transfers between devices: 24.5 us -> 38.6 us
  waiting for transfers between devices: 2.86 us -> 0.79 us
    ppermute x12 -> x23, starting transfers between devices: 24.5 us -> 38.6 us  [the longest x15 26.2 us: sum_over(): lax.ppermute(value, axis, [(k, k ^ m * step) for k in range(count)])]
    ppermute x12 -> x23, waiting for transfers between devices: 2.86 us -> 0.79 us  [the longest x15 0.71 us: sum_over(): lax.ppermute(value, axis, [(k, k ^ m * step) for k in range(count)])]
  transfers between devices with their start and end apart: 12 -> 23, of which waited for: 2 -> 1; matrix products, arithmetic and copies ran while one was open for 0% -> 0% of each run, Pallas kernels for 35% -> 30%
where the time goes in v3:
time: 98.8 us; the launch traced here: 99.3 us
  Pallas kernels  55.1 us (56%)
  starting transfers between devices  38.6 us (39%)
  local copies, waits for them, and re-layouts  3.28 us (3%)
  between operations  1.51 us (2%)
    pallas_call x13, Pallas kernels, run(): pl.pallas_call(body, out_shape=outs, in_specs=ins, out_specs=out_specs, s...  55.1 us
    ppermute x15, starting transfers between devices, sum_over(): lax.ppermute(value, axis, [(k, k ^ m * step) for k in range(count)])  26.2 us
    ppermute x4, starting transfers between devices, swapped_both(): a = lax.ppermute(to_a, 'gx', [(k, k ^ 1) for k in range(count)])  9.78 us
    unnamed x9, local copies, waits for them, and re-layouts  3.28 us
    ppermute x4, starting transfers between devices, swapped_both(): lax.ppermute(to_b, 'gx', [(k, (k + 1 ^ 1) - 1) for k in range(1, count -...  2.67 us
  transfers between devices with their start and end apart: 23, of which 1 were waited for; matrix products, arithmetic and copies ran while one was open for 0% of the time, Pallas kernels for 30%

profile of v3, /device:TPU:0, one launch (start us, length us, event | category | flops | bytes accessed | tf_op | source)
XLA Modules:
  0.0 99.3 jit_solution(1657357705675480649)
XLA Ops:
  2.0 0.9 copy-done
  4.6 11.8 %sort_blocks.1 = (f32[24,2048]{1,0:T(8,128)S(1)}, f32[24,2048]{1,0:T(8,128)S(1)}, f32[3,2048,128]{2,1,0:T(8,128)S(1)}, f32[3,2048,128]{2,1,0:T(8,128)S(1)}, f32[...) custom-call(f32[3,4096]{1,0:T(4,128)S(1)} %copy-done.2, ...), custom_call_target="tpu_custom_call" | custom-call | flops 1000000000 | bytes 1048576 | tf_op jit(solution)/shard_map/sort_blocks/pallas_call | solution.py:285
  17.0 4.4 %collective-permute-start = (f32[24,2048]{1,0:T(8,128)S(1)}, f32[24,2048]{1,0:T(8,128)S(1)}, u32[]{:S(2)}, u32[]{:S(2)}) collective-permute-start(f32[24,2048]{1,0:T(8,128)S(1)} %get-tuple-element.39.s0.w0), channel_id=1, source_target_pairs={{0,1},{1,0},{2,3},{3,2},{4,5},{5,4},{6,7},{7,6},{8,9},{9,8},{10,11... | collective-permute-start | bytes 589832 | tf_op jit(solution)/shard_map/ppermute | solution.py:493
  21.4 7.2 %diag_build.1 = (bf16[8,256,512]{2,1,0:T(8,128)(2,1)S(1)}, bf16[8,256,512]{2,1,0:T(8,128)(2,1)S(1)}, s32[72]{0:T(128)S(1)}) custom-call(s32[5]{0:T(128)S(1)} %get-tuple-element.38.flags, f32[32]{0:T(128)S(1)} %get-tuple-element.41.yb0, f32[32]{0:T(128)S(1)} %get-tuple-element.42.yb1, f32[24,2048]{1,0:T(8,128)S(1)} %get-tuple-element.39.s0.w0, ...), custom_call_target="tpu_custom_call" | custom-call | flops 3000000000 | bytes 1048576 | tf_op jit(solution)/shard_map/diag_build/pallas_call | solution.py:285
  28.6 7.8 %halo_build.1 = (bf16[8,256,768]{2,1,0:T(8,128)(2,1)S(1)}, s32[24]{0:T(128)S(1)}, f32[16,2048]{1,0:T(8,128)S(1)}, f32[16,2048]{1,0:T(8,128)S(1)}, f32[24,2048]{1,0:T(8,128)S(1)}) custom-call(s32[5]{0:T(128)S(1)} %get-tuple-element.38.flags, f32[32]{0:T(128)S(1)} %get-tuple-element.42.yb1, f32[24,2048]{1,0:T(8,128)S(1)} %get-tuple-element.40.s1.w1, ...), custom_call_target="tpu_custom_call" | custom-call | flops 3000000000 | bytes 1048576 | tf_op jit(solution)/shard_map/halo_build/pallas_call | solution.py:285
  37.1 2.9 %collective-permute-start.2 = (f32[16,2048]{1,0:T(8,128)S(1)}, f32[16,2048]{1,0:T(8,128)S(1)}, u32[]{:S(2)}, u32[]{:S(2)}) collective-permute-start(f32[16,2048]{1,0:T(8,128)S(1)} %get-tuple-element.53), channel_id=1, source_target_pairs={{0,1},{1,0},{2,3},{3,2},{4,5},{5,4},{6,7},{7,6},{8,9},{9,8},{10,11... | collective-permute-start | bytes 393224 | tf_op jit(solution)/shard_map/ppermute | solution.py:493
  40.0 8.2 %own_build.1 = (bf16[8,256,768]{2,1,0:T(8,128)(2,1)S(1)}, f32[16,2048]{1,0:T(8,128)S(1)}, f32[16,2048]{1,0:T(8,128)S(1)}) custom-call(s32[72]{0:T(128)S(1)} %get-tuple-element.45.tab, f32[24,2048]{1,0:T(8,128)S(1)} %get-tuple-element.39.s0.w0, f32[24,2048]{1,0:T(8,128)S(1)} %get-tuple-element.40.s1.w1, f32[3,2048,128]{2,1,0:T(8,128)S(1)} %get-tuple-element.43.col0, ...), custom_call_target="tpu_custom_call" | custom-call | flops 5000000000 | bytes 1048576 | tf_op jit(solution)/shard_map/own_build/pallas_call | solution.py:285
  48.2 1.4 %finish.2 = (f32[16,2048]{1,0:T(8,128)S(1)}, f32[16,2048]{1,0:T(8,128)S(1)}, f32[16,2048]{1,0:T(8,128)S(1)}, f32[16,2048]{1,0:T(8,128)S(1)}, f32[16,128]{1,0:T(8,128)S(1)}) custom-call(s32[5]{0:T(128)S(1)} %get-tuple-element.38.flags, s32[24]{0:T(128)S(1)} %get-tuple-element.50.tab, bf16[8,256,768]{2,1,0:T(8,128)(2,1)S(1)} %get-tuple-element.51.k12, ...), custom_call_target="tpu_custom_call" | custom-call | flops 1000000000 | bytes 1048576 | tf_op jit(solution)/shard_map/finish/pallas_call | solution.py:285
  50.4 3.7 %own_apply.2 = (f32[16,2048]{1,0:T(8,128)S(1)}, f32[16,2048]{1,0:T(8,128)S(1)}) custom-call(s32[72]{0:T(128)S(1)} %get-tuple-element.45.tab, bf16[8,256,512]{2,1,0:T(8,128)(2,1)S(1)} %get-tuple-element.46.k00, bf16[8,256,768]{2,1,0:T(8,128)(2,1)S(1)} %get-tuple-element.49.k01, bf16[8,256,512]{2,1,0:T(8,128)(2,1)S(1)} %get-tuple-element.47.k11, ...), custom_call_target="tpu_custom_call" | custom-call | flops 2000000000 | bytes 1048576 | tf_op jit(solution)/shard_map/own_apply/pallas_call | solution.py:285
  54.2 2.4 %finish.3 = (f32[16,2048]{1,0:T(8,128)S(1)}, f32[16,2048]{1,0:T(8,128)S(1)}, f32[16,2048]{1,0:T(8,128)S(1)}, f32[16,2048]{1,0:T(8,128)S(1)}, f32[16,128]{1,0:T(8,128)S(1)}) custom-call(s32[5]{0:T(128)S(1)} %get-tuple-element.38.flags, s32[24]{0:T(128)S(1)} %get-tuple-element.50.tab, bf16[8,256,768]{2,1,0:T(8,128)(2,1)S(1)} %get-tuple-element.51.k12, ...), custom_call_target="tpu_custom_call" | custom-call | flops 1000000000 | bytes 1048576 | tf_op jit(solution)/shard_map/finish/pallas_call | solution.py:285
  56.6 2.4 %collective-permute-start.6 = (f32[16,2048]{1,0:T(8,128)S(1)}, f32[16,2048]{1,0:T(8,128)S(1)}, u32[]{:S(2)}, u32[]{:S(2)}) collective-permute-start(f32[16,2048]{1,0:T(8,128)S(1)} %get-tuple-element.67), channel_id=1, source_target_pairs={{0,1},{1,0},{2,3},{3,2},{4,5},{5,4},{6,7},{7,6},{8,9},{9,8},{10,11... | collective-permute-start | bytes 393224 | tf_op jit(solution)/shard_map/ppermute | solution.py:493
  59.6 3.7 %own_apply.3 = (f32[16,2048]{1,0:T(8,128)S(1)}, f32[16,2048]{1,0:T(8,128)S(1)}) custom-call(s32[72]{0:T(128)S(1)} %get-tuple-element.45.tab, bf16[8,256,512]{2,1,0:T(8,128)(2,1)S(1)} %get-tuple-element.46.k00, bf16[8,256,768]{2,1,0:T(8,128)(2,1)S(1)} %get-tuple-element.49.k01, bf16[8,256,512]{2,1,0:T(8,128)(2,1)S(1)} %get-tuple-element.47.k11, ...), custom_call_target="tpu_custom_call" | custom-call | flops 2000000000 | bytes 1048576 | tf_op jit(solution)/shard_map/own_apply/pallas_call | solution.py:285
  64.1 7.4 %collective-permute-start.21 = (f32[16,128]{1,0:T(8,128)S(1)}, f32[16,128]{1,0:T(8,128)S(1)}, u32[]{:S(2)}, u32[]{:S(2)}) collective-permute-start(f32[16,128]{1,0:T(8,128)S(1)} %moment.1), channel_id=1, source_target_pairs={{0,14},{1,15},{2,12},{3,13},{4,10},{5,11},{6,8},{7,9},{8,6},{9,7},... | collective-permute-start | bytes 24584 | tf_op jit(solution)/shard_map/ppermute | solution.py:506
  71.5 3.1 %collective-permute-start.20 = (f32[16,128]{1,0:T(8,128)S(1)}, f32[16,128]{1,0:T(8,128)S(1)}, u32[]{:S(2)}, u32[]{:S(2)}) collective-permute-start(f32[16,128]{1,0:T(8,128)S(1)} %moment.1), channel_id=1, source_target_pairs={{0,13},{1,12},{2,15},{3,14},{4,9},{5,8},{6,11},{7,10},{8,5},{9,4},... | collective-permute-start | bytes 24584 | tf_op jit(solution)/shard_map/ppermute | solution.py:506
  74.6 1.1 %collective-permute-start.19 = (f32[16,128]{1,0:T(8,128)S(1)}, f32[16,128]{1,0:T(8,128)S(1)}, u32[]{:S(2)}, u32[]{:S(2)}) collective-permute-start(f32[16,128]{1,0:T(8,128)S(1)} %moment.1), channel_id=1, source_target_pairs={{0,12},{1,13},{2,14},{3,15},{4,8},{5,9},{6,10},{7,11},{8,4},{9,5},... | collective-permute-start | bytes 24584 | tf_op jit(solution)/shard_map/ppermute | solution.py:506
  76.0 1.7 %last.1 = (f32[16,2048]{1,0:T(8,128)S(1)}, f32[16,2048]{1,0:T(8,128)S(1)}) custom-call(s32[5]{0:T(128)S(1)} %get-tuple-element.38.flags, s32[24]{0:T(128)S(1)} %get-tuple-element.50.tab, bf16[8,256,768]{2,1,0:T(8,128)(2,1)S(1)} %get-tuple-element.51.k12, f32[24,2048]{1,0:T(8,128)S(1)} %get-tuple-element.39.s0.w0, f32[24,2048]{1,0:T(8,128)S(1)} %get-tuple-element.40.s1.w1, ...), custom_call_target="tpu_custom_call" | custom-call | flops 1000000000 | bytes 1048576 | tf_op jit(solution)/shard_map/last/pallas_call | solution.py:285
  77.7 3.3 %collective-permute-start.17 = (f32[16,128]{1,0:T(8,128)S(1)}, f32[16,128]{1,0:T(8,128)S(1)}, u32[]{:S(2)}, u32[]{:S(2)}) collective-permute-start(f32[16,128]{1,0:T(8,128)S(1)} %moment.1), channel_id=1, source_target_pairs={{0,10},{1,11},{2,8},{3,9},{4,14},{5,15},{6,12},{7,13},{8,2},{9,3},... | collective-permute-start | bytes 24584 | tf_op jit(solution)/shard_map/ppermute | solution.py:506
  81.0 2.2 %collective-permute-start.16 = (f32[16,128]{1,0:T(8,128)S(1)}, f32[16,128]{1,0:T(8,128)S(1)}, u32[]{:S(2)}, u32[]{:S(2)}) collective-permute-start(f32[16,128]{1,0:T(8,128)S(1)} %moment.1), channel_id=1, source_target_pairs={{0,9},{1,8},{2,11},{3,10},{4,13},{5,12},{6,15},{7,14},{8,1},{9,0},... | collective-permute-start | bytes 24584 | tf_op jit(solution)/shard_map/ppermute | solution.py:506
  83.7 1.9 %collective-permute-start.14 = (f32[16,128]{1,0:T(8,128)S(1)}, f32[16,128]{1,0:T(8,128)S(1)}, u32[]{:S(2)}, u32[]{:S(2)}) collective-permute-start(f32[16,128]{1,0:T(8,128)S(1)} %moment.1), channel_id=1, source_target_pairs={{0,7},{1,6},{2,5},{3,4},{4,3},{5,2},{6,1},{7,0},{8,15},{9,14},{10,... | collective-permute-start | bytes 24584 | tf_op jit(solution)/shard_map/ppermute | solution.py:506
  86.3 2.7 %unsort.2.u0 = f32[48,2048]{1,0:T(8,128)S(1)} custom-call(s32[1,2048]{1,0:T(1,128)S(1)} %get-tuple-element.70.rank_ref, f32[16,2048]{1,0:T(8,128)S(1)} %get-tuple-element.58.w0.wa, f32[16,2048]{1,0:T(8,128)S(1)} %get-tuple-element.63.w0.wb, f32[16,2048]{1,0:T(8,128)S(1)} %get-tuple-element.71.wc), custom_call_target="tpu_custom_call" | custom-call | flops 805306368 | bytes 1048576 | tf_op jit(solution)/shard_map/unsort/pallas_call | solution.py:285
  89.1 2.3 %collective-permute-start.12 = (f32[16,128]{1,0:T(8,128)S(1)}, f32[16,128]{1,0:T(8,128)S(1)}, u32[]{:S(2)}, u32[]{:S(2)}) collective-permute-start(f32[16,128]{1,0:T(8,128)S(1)} %moment.1), channel_id=1, source_target_pairs={{0,5},{1,4},{2,7},{3,6},{4,1},{5,0},{6,3},{7,2},{8,13},{9,12},{10,... | collective-permute-start | bytes 24584 | tf_op jit(solution)/shard_map/ppermute | solution.py:506
  91.7 2.8 %collective-permute-start.10 = (f32[16,128]{1,0:T(8,128)S(1)}, f32[16,128]{1,0:T(8,128)S(1)}, u32[]{:S(2)}, u32[]{:S(2)}) collective-permute-start(f32[16,128]{1,0:T(8,128)S(1)} %moment.1), channel_id=1, source_target_pairs={{0,3},{1,2},{2,1},{3,0},{4,7},{5,6},{6,5},{7,4},{8,11},{9,10},{10,... | collective-permute-start | bytes 24584 | tf_op jit(solution)/shard_map/ppermute | solution.py:506
  94.8 2.8 %unsort.3.u1 = f32[48,2048]{1,0:T(8,128)S(1)} custom-call(s32[1,2048]{1,0:T(1,128)S(1)} %get-tuple-element.72.rank_ref, f32[16,2048]{1,0:T(8,128)S(1)} %get-tuple-element.59.w1.wa, f32[16,2048]{1,0:T(8,128)S(1)} %get-tuple-element.64.w1.wb, f32[16,2048]{1,0:T(8,128)S(1)} %get-tuple-element.73.wc), custom_call_target="tpu_custom_call" | custom-call | flops 805306368 | bytes 1048576 | tf_op jit(solution)/shard_map/unsort/pallas_call | solution.py:285
  98.2 1.0 %combine.1 = (f32[16,4096]{1,0:T(8,128)}, f32[16,4096]{1,0:T(8,128)}) custom-call(f32[16,128]{1,0:T(8,128)S(1)} %add_add_fusion.mom, f32[16,4096]{1,0:T(8,128)S(1)} %copy-done.1, f32[48,2048]{1,0:T(8,128)S(1)} %unsort.2.u0, f32[48,2048]{1,0:T(8,128)S(1)} %unsort.3.u1), custom_call_target="tpu_custom_call" | custom-call | flops 1000000 | bytes 1048576 | tf_op jit(solution)/shard_map/combine/pallas_call | solution.py:285
  (46 shorter events, 8.5 us)
Async XLA Ops:
  16.3 12.3 %collective-permute-start.1 = (f32[24,2048]{1,0:T(8,128)S(1)}, f32[24,2048]{1,0:T(8,128)S(1)}, u32[]{:S(2)}, u32[]{:S(2)}) collective-permute-start(f32[24,2048]{1,0:T(8,128)S(1)} %get-tuple-element.39.s0.w0), channel_id=1, source_target_pairs={{1,2},{2,1},{3,4},{4,3},{5,6},{6,5},{7,8},{8,7},{9,10},{10,9},{11,... | collective-permute-start | bytes 589832 | tf_op jit(solution)/shard_map/ppermute | solution.py:494
  17.0 11.6 %collective-permute-start = (f32[24,2048]{1,0:T(8,128)S(1)}, f32[24,2048]{1,0:T(8,128)S(1)}, u32[]{:S(2)}, u32[]{:S(2)}) collective-permute-start(f32[24,2048]{1,0:T(8,128)S(1)} %get-tuple-element.39.s0.w0), channel_id=1, source_target_pairs={{0,1},{1,0},{2,3},{3,2},{4,5},{5,4},{6,7},{7,6},{8,9},{9,8},{10,11... | collective-permute-start | bytes 589832 | tf_op jit(solution)/shard_map/ppermute | solution.py:493
  36.4 11.8 %collective-permute-start.3 = (f32[16,2048]{1,0:T(8,128)S(1)}, f32[16,2048]{1,0:T(8,128)S(1)}, u32[]{:S(2)}, u32[]{:S(2)}) collective-permute-start(f32[16,2048]{1,0:T(8,128)S(1)} %get-tuple-element.53), channel_id=1, source_target_pairs={{1,2},{2,1},{3,4},{4,3},{5,6},{6,5},{7,8},{8,7},{9,10},{10,9},{11,... | collective-permute-start | bytes 393224 | tf_op jit(solution)/shard_map/ppermute | solution.py:494
  37.1 11.1 %collective-permute-start.2 = (f32[16,2048]{1,0:T(8,128)S(1)}, f32[16,2048]{1,0:T(8,128)S(1)}, u32[]{:S(2)}, u32[]{:S(2)}) collective-permute-start(f32[16,2048]{1,0:T(8,128)S(1)} %get-tuple-element.53), channel_id=1, source_target_pairs={{0,1},{1,0},{2,3},{3,2},{4,5},{5,4},{6,7},{7,6},{8,9},{9,8},{10,11... | collective-permute-start | bytes 393224 | tf_op jit(solution)/shard_map/ppermute | solution.py:493
  49.7 4.5 %collective-permute-start.4 = (f32[16,2048]{1,0:T(8,128)S(1)}, f32[16,2048]{1,0:T(8,128)S(1)}, u32[]{:S(2)}, u32[]{:S(2)}) collective-permute-start(f32[16,2048]{1,0:T(8,128)S(1)} %get-tuple-element.56), channel_id=1, source_target_pairs={{0,1},{1,0},{2,3},{3,2},{4,5},{5,4},{6,7},{7,6},{8,9},{9,8},{10,11... | collective-permute-start | bytes 393224 | tf_op jit(solution)/shard_map/ppermute | solution.py:493
  49.7 4.4 %collective-permute-start.5 = (f32[16,2048]{1,0:T(8,128)S(1)}, f32[16,2048]{1,0:T(8,128)S(1)}, u32[]{:S(2)}, u32[]{:S(2)}) collective-permute-start(f32[16,2048]{1,0:T(8,128)S(1)} %get-tuple-element.57), channel_id=1, source_target_pairs={{1,2},{2,1},{3,4},{4,3},{5,6},{6,5},{7,8},{8,7},{9,10},{10,9},{11,... | collective-permute-start | bytes 393224 | tf_op jit(solution)/shard_map/ppermute | solution.py:494
  56.6 6.8 %collective-permute-start.6 = (f32[16,2048]{1,0:T(8,128)S(1)}, f32[16,2048]{1,0:T(8,128)S(1)}, u32[]{:S(2)}, u32[]{:S(2)}) collective-permute-start(f32[16,2048]{1,0:T(8,128)S(1)} %get-tuple-element.67), channel_id=1, source_target_pairs={{0,1},{1,0},{2,3},{3,2},{4,5},{5,4},{6,7},{7,6},{8,9},{9,8},{10,11... | collective-permute-start | bytes 393224 | tf_op jit(solution)/shard_map/ppermute | solution.py:493
  59.0 4.4 %collective-permute-start.7 = (f32[16,2048]{1,0:T(8,128)S(1)}, f32[16,2048]{1,0:T(8,128)S(1)}, u32[]{:S(2)}, u32[]{:S(2)}) collective-permute-start(f32[16,2048]{1,0:T(8,128)S(1)} %get-tuple-element.68), channel_id=1, source_target_pairs={{1,2},{2,1},{3,4},{4,3},{5,6},{6,5},{7,8},{8,7},{9,10},{10,9},{11,... | collective-permute-start | bytes 393224 | tf_op jit(solution)/shard_map/ppermute | solution.py:494
  64.1 13.7 %collective-permute-start.22 = (f32[16,128]{1,0:T(8,128)S(1)}, f32[16,128]{1,0:T(8,128)S(1)}, u32[]{:S(2)}, u32[]{:S(2)}) collective-permute-start(f32[16,128]{1,0:T(8,128)S(1)} %moment.1), channel_id=1, source_target_pairs={{0,15},{1,14},{2,13},{3,12},{4,11},{5,10},{6,9},{7,8},{8,7},{9,6},... | collective-permute-start | bytes 24584 | tf_op jit(solution)/shard_map/ppermute | solution.py:506
  64.1 16.9 %collective-permute-start.21 = (f32[16,128]{1,0:T(8,128)S(1)}, f32[16,128]{1,0:T(8,128)S(1)}, u32[]{:S(2)}, u32[]{:S(2)}) collective-permute-start(f32[16,128]{1,0:T(8,128)S(1)} %moment.1), channel_id=1, source_target_pairs={{0,14},{1,15},{2,12},{3,13},{4,10},{5,11},{6,8},{7,9},{8,6},{9,7},... | collective-permute-start | bytes 24584 | tf_op jit(solution)/shard_map/ppermute | solution.py:506
  71.5 11.8 %collective-permute-start.20 = (f32[16,128]{1,0:T(8,128)S(1)}, f32[16,128]{1,0:T(8,128)S(1)}, u32[]{:S(2)}, u32[]{:S(2)}) collective-permute-start(f32[16,128]{1,0:T(8,128)S(1)} %moment.1), channel_id=1, source_target_pairs={{0,13},{1,12},{2,15},{3,14},{4,9},{5,8},{6,11},{7,10},{8,5},{9,4},... | collective-permute-start | bytes 24584 | tf_op jit(solution)/shard_map/ppermute | solution.py:506
  74.6 9.1 %collective-permute-start.19 = (f32[16,128]{1,0:T(8,128)S(1)}, f32[16,128]{1,0:T(8,128)S(1)}, u32[]{:S(2)}, u32[]{:S(2)}) collective-permute-start(f32[16,128]{1,0:T(8,128)S(1)} %moment.1), channel_id=1, source_target_pairs={{0,12},{1,13},{2,14},{3,15},{4,8},{5,9},{6,10},{7,11},{8,4},{9,5},... | collective-permute-start | bytes 24584 | tf_op jit(solution)/shard_map/ppermute | solution.py:506
  75.7 9.9 %collective-permute-start.18 = (f32[16,128]{1,0:T(8,128)S(1)}, f32[16,128]{1,0:T(8,128)S(1)}, u32[]{:S(2)}, u32[]{:S(2)}) collective-permute-start(f32[16,128]{1,0:T(8,128)S(1)} %moment.1), channel_id=1, source_target_pairs={{0,11},{1,10},{2,9},{3,8},{4,15},{5,14},{6,13},{7,12},{8,3},{9,2},... | collective-permute-start | bytes 24584 | tf_op jit(solution)/shard_map/ppermute | solution.py:506
  77.7 20.5 %copy-start.1 = (f32[16,4096]{1,0:T(8,128)S(1)}, f32[16,4096]{1,0:T(8,128)}, u32[]{:S(2)}) copy-start(f32[16,4096]{1,0:T(8,128)} %probes.1) | copy-start | bytes 786436
  77.7 11.3 %collective-permute-start.17 = (f32[16,128]{1,0:T(8,128)S(1)}, f32[16,128]{1,0:T(8,128)S(1)}, u32[]{:S(2)}, u32[]{:S(2)}) collective-permute-start(f32[16,128]{1,0:T(8,128)S(1)} %moment.1), channel_id=1, source_target_pairs={{0,10},{1,11},{2,8},{3,9},{4,14},{5,15},{6,12},{7,13},{8,2},{9,3},... | collective-permute-start | bytes 24584 | tf_op jit(solution)/shard_map/ppermute | solution.py:506
  81.0 10.4 %collective-permute-start.16 = (f32[16,128]{1,0:T(8,128)S(1)}, f32[16,128]{1,0:T(8,128)S(1)}, u32[]{:S(2)}, u32[]{:S(2)}) collective-permute-start(f32[16,128]{1,0:T(8,128)S(1)} %moment.1), channel_id=1, source_target_pairs={{0,9},{1,8},{2,11},{3,10},{4,13},{5,12},{6,15},{7,14},{8,1},{9,0},... | collective-permute-start | bytes 24584 | tf_op jit(solution)/shard_map/ppermute | solution.py:506
  83.2 8.5 %collective-permute-start.15 = (f32[16,128]{1,0:T(8,128)S(1)}, f32[16,128]{1,0:T(8,128)S(1)}, u32[]{:S(2)}, u32[]{:S(2)}) collective-permute-start(f32[16,128]{1,0:T(8,128)S(1)} %moment.1), channel_id=1, source_target_pairs={{0,8},{1,9},{2,10},{3,11},{4,12},{5,13},{6,14},{7,15},{8,0},{9,1},... | collective-permute-start | bytes 24584 | tf_op jit(solution)/shard_map/ppermute | solution.py:506
  83.7 10.9 %collective-permute-start.14 = (f32[16,128]{1,0:T(8,128)S(1)}, f32[16,128]{1,0:T(8,128)S(1)}, u32[]{:S(2)}, u32[]{:S(2)}) collective-permute-start(f32[16,128]{1,0:T(8,128)S(1)} %moment.1), channel_id=1, source_target_pairs={{0,7},{1,6},{2,5},{3,4},{4,3},{5,2},{6,1},{7,0},{8,15},{9,14},{10,... | collective-permute-start | bytes 24584 | tf_op jit(solution)/shard_map/ppermute | solution.py:506
  85.6 9.0 %collective-permute-start.13 = (f32[16,128]{1,0:T(8,128)S(1)}, f32[16,128]{1,0:T(8,128)S(1)}, u32[]{:S(2)}, u32[]{:S(2)}) collective-permute-start(f32[16,128]{1,0:T(8,128)S(1)} %moment.1), channel_id=1, source_target_pairs={{0,6},{1,7},{2,4},{3,5},{4,2},{5,3},{6,0},{7,1},{8,14},{9,15},{10,... | collective-permute-start | bytes 24584 | tf_op jit(solution)/shard_map/ppermute | solution.py:506
  89.1 8.4 %collective-permute-start.12 = (f32[16,128]{1,0:T(8,128)S(1)}, f32[16,128]{1,0:T(8,128)S(1)}, u32[]{:S(2)}, u32[]{:S(2)}) collective-permute-start(f32[16,128]{1,0:T(8,128)S(1)} %moment.1), channel_id=1, source_target_pairs={{0,5},{1,4},{2,7},{3,6},{4,1},{5,0},{6,3},{7,2},{8,13},{9,12},{10,... | collective-permute-start | bytes 24584 | tf_op jit(solution)/shard_map/ppermute | solution.py:506
  91.4 6.1 %collective-permute-start.11 = (f32[16,128]{1,0:T(8,128)S(1)}, f32[16,128]{1,0:T(8,128)S(1)}, u32[]{:S(2)}, u32[]{:S(2)}) collective-permute-start(f32[16,128]{1,0:T(8,128)S(1)} %moment.1), channel_id=1, source_target_pairs={{0,4},{1,5},{2,6},{3,7},{4,0},{5,1},{6,2},{7,3},{8,12},{9,13},{10,... | collective-permute-start | bytes 24584 | tf_op jit(solution)/shard_map/ppermute | solution.py:506
  91.7 5.8 %collective-permute-start.10 = (f32[16,128]{1,0:T(8,128)S(1)}, f32[16,128]{1,0:T(8,128)S(1)}, u32[]{:S(2)}, u32[]{:S(2)}) collective-permute-start(f32[16,128]{1,0:T(8,128)S(1)} %moment.1), channel_id=1, source_target_pairs={{0,3},{1,2},{2,1},{3,0},{4,7},{5,6},{6,5},{7,4},{8,11},{9,10},{10,... | collective-permute-start | bytes 24584 | tf_op jit(solution)/shard_map/ppermute | solution.py:506
  94.6 3.7 %collective-permute-start.9 = (f32[16,128]{1,0:T(8,128)S(1)}, f32[16,128]{1,0:T(8,128)S(1)}, u32[]{:S(2)}, u32[]{:S(2)}) collective-permute-start(f32[16,128]{1,0:T(8,128)S(1)} %moment.1), channel_id=1, source_target_pairs={{0,2},{1,3},{2,0},{3,1},{4,6},{5,7},{6,4},{7,5},{8,10},{9,11},{10,... | collective-permute-start | bytes 24584 | tf_op jit(solution)/shard_map/ppermute | solution.py:506
  94.6 3.6 %collective-permute-start.8 = (f32[16,128]{1,0:T(8,128)S(1)}, f32[16,128]{1,0:T(8,128)S(1)}, u32[]{:S(2)}, u32[]{:S(2)}) collective-permute-start(f32[16,128]{1,0:T(8,128)S(1)} %moment.1), channel_id=1, source_target_pairs={{0,1},{1,0},{2,3},{3,2},{4,5},{5,4},{6,7},{7,6},{8,9},{9,8},{10,11... | collective-permute-start | bytes 24584 | tf_op jit(solution)/shard_map/ppermute | solution.py:506
  (3 other events, 2.5 us)

commit v4 on v3

v4 whole, which is shorter than its diff:
```python
import functools

import jax
import jax.numpy as jnp
from jax import lax
from jax.experimental import pallas as pl
from jax.experimental.pallas import tpu as pltpu
from jax.sharding import PartitionSpec as P

BLK = 2048
STRIP = 256
STRIPS = BLK // STRIP
SUB = 128
SUBS = BLK // SUB
OFF_W = 768
OFF_SUBS = OFF_W // SUB
DIAG_W = 512
N_PROBES = 16
N_FEATURES = 64
MIB = 1 << 20

VMEM = pl.BlockSpec(memory_space=pltpu.VMEM)
SMEM = pl.BlockSpec(memory_space=pltpu.SMEM)

f32 = jnp.float32
bf16 = jnp.bfloat16

T_LIVE, T_EXTRA, T_START, T_END = 0, 1, 8, 16
T_SIZE = 24


def nt(left, right):
    return lax.dot_general(left, right, (((1,), (1,)), ((), ())), preferred_element_type=f32)


def nn(left, right):
    return jnp.dot(left, right, preferred_element_type=f32)


def split2(value):
    high = value.astype(bf16)
    low = (value - high.astype(f32)).astype(bf16)
    return jnp.concatenate([high, low], axis=0)


def halves(value):
    n = value.shape[0] // 2
    return value[:n] + value[n:]


def split3(value):
    high = value.astype(bf16).astype(f32)
    rest = value - high
    mid = rest.astype(bf16).astype(f32)
    return high, mid, rest - mid


def one_hot(marked, c, place):
    parts = []
    for h in range(2):
        at = c * STRIP + h * SUB
        hit = jnp.broadcast_to(marked[:, at : at + SUB], (STRIP, SUB)) == place
        parts.append(jnp.where(hit, jnp.ones((STRIP, SUB), bf16), jnp.zeros((STRIP, SUB), bf16)))
    return jnp.concatenate(parts, axis=1)


def places():
    return lax.broadcasted_iota(jnp.int32, (STRIP, SUB), 0).astype(f32).astype(bf16)


def marks(rank, g):
    group = lax.shift_right_logical(rank, 8)
    within = jnp.bitwise_and(rank, STRIP - 1)
    return jnp.where(group == g, within, -1).astype(f32).astype(bf16)


def rank_of(y_row, key_ref):
    lane = lax.broadcasted_iota(jnp.int32, (1, BLK), 1)
    key_row = (y_row * 4096.0).astype(jnp.int32) * BLK + lane
    for c in range(SUBS):
        piece = jnp.broadcast_to(y_row[:, c * SUB : (c + 1) * SUB], (SUB, SUB)).T
        sub = lax.broadcasted_iota(jnp.int32, (SUB, SUB), 0) + c * SUB
        key_ref[c * SUB : (c + 1) * SUB, :] = (piece * 4096.0).astype(jnp.int32) * BLK + sub
    keys = jnp.broadcast_to(key_row, (8, BLK))

    def count(i, acc):
        mine = key_ref[pl.ds(pl.multiple_of(i * 8, 8), 8), :]
        mine = jnp.concatenate([mine] * SUBS, axis=1)
        return acc + jnp.where(mine < keys, 1, 0)

    acc = lax.fori_loop(0, BLK // 8, count, jnp.zeros((8, BLK), jnp.int32), unroll=8)
    return jnp.sum(acc, axis=0, keepdims=True)


def row_id(width):
    return lax.broadcasted_iota(jnp.int32, (8, width), 0)


def features(offset, left):
    first, second, third = split3(offset)
    norm = jnp.sum(offset * offset, axis=0, keepdims=True)
    n1, n2, n3 = split3(norm)
    ids = row_id(offset.shape[1])
    own, other = (0, 3) if left else (3, 0)
    norms = jnp.where(ids == own, n1, jnp.where(ids == own + 1, n2, jnp.where(ids == own + 2, n3, 0.0)))
    norms = jnp.where((ids >= other) & (ids < other + 3), 1.0, norms)
    if left:
        first, second, third = -2.0 * first, -2.0 * second, -2.0 * third
        parts = [first, first, first, second, second, third]
    else:
        parts = [first, second, third, first, second, first]
    return jnp.concatenate(parts + [norms, jnp.zeros_like(norms)], axis=0), norm


def sort_kernel(
    pts_hbm, nv_hbm, pr_hbm, pair_hbm, count, s0, s1, lhs0, lhs1, yb0, yb1, rank0, rank1, flags,
    pts_ref, nv_ref, pr_ref, pair, key_ref, sems
):
    copies = [
        pltpu.make_async_copy(src, dst, sems.at[k])
        for k, (src, dst) in enumerate(
            ((pts_hbm, pts_ref), (nv_hbm, nv_ref), (pr_hbm, pr_ref), (pair_hbm, pair))
        )
    ]
    for copy in copies:
        copy.start()
    copies[0].wait()
    for blk, rank_ref in enumerate((rank0, rank1)):
        rank_ref[...] = rank_of(pts_ref[1:2, blk * BLK : (blk + 1) * BLK], key_ref)
    for copy in copies[1:]:
        copy.wait()
    for local in range(2):
        for ahead in range(2):
            flags[2 * local + ahead] = live_flag(pair, count, local, ahead)
    flags[4] = jnp.bitwise_and(lax.shift_right_logical(pair[0, 0], 1), 1)
    place = places()
    for blk, (out_ref, lhs_ref, rank_ref) in enumerate(((s0, lhs0, rank0), (s1, lhs1, rank1))):
        cols = slice(blk * BLK, (blk + 1) * BLK)
        aux = jnp.concatenate(
            [pts_ref[0:3, cols] * 2.0, nv_ref[:, cols], jnp.zeros((4, BLK), f32)], axis=0
        )
        data = jnp.concatenate(
            [*split3(pr_ref[:, cols]), *split3(aux), jnp.zeros((8, BLK), f32)], axis=0
        ).astype(bf16)
        rank = rank_ref[...]
        centre = 0.5 * (jnp.min(aux, axis=1, keepdims=True) + jnp.max(aux, axis=1, keepdims=True))
        centre = jnp.concatenate([jnp.zeros((4, 1), f32), centre[0:3], jnp.zeros((1, 1), f32)], axis=0)
        for g in range(STRIPS):
            marked = marks(rank, g)
            got = None
            for c in range(STRIPS):
                part = nt(data[:, c * STRIP : (c + 1) * STRIP], one_hot(marked, c, place))
                got = part if got is None else got + part
            here = slice(g * STRIP, (g + 1) * STRIP)
            out_ref[0:16, here] = (got[0:16] + got[16:32]) + got[32:48]
            out_ref[16:24, here] = ((got[48:56] + got[56:64]) + got[64:72]) + centre
        offset = offset_of(out_ref, out_ref)
        rows, _ = features(offset, True)
        for c in range(SUBS):
            here = slice(c * SUB, (c + 1) * SUB)
            lhs_ref[here, :] = rows[:, here].T.astype(bf16)
    bounds(s0, yb0)
    bounds(s1, yb1)


def offset_of(side_ref, centre_ref):
    centre = jnp.concatenate([centre_ref[20:23, 0:1], jnp.zeros((5, 1), f32)], axis=0)
    return jnp.where(row_id(BLK) < 3, side_ref[16:24, :] - centre, 0.0)


def bounds(side_ref, yb_ref):
    for c in range(SUBS):
        row = side_ref[17:18, c * SUB : (c + 1) * SUB]
        yb_ref[c] = jnp.min(row)
        yb_ref[SUBS + c] = jnp.max(row)


def live_flag(pair_ref, count_ref, local, ahead):
    flag = jnp.int32(0)
    for s in range(pair_ref.shape[1]):
        owner = pair_ref[0, s]
        match = (
            (jnp.int32(s) < count_ref[0])
            & (jnp.bitwise_and(owner, 1) == local)
            & (pair_ref[1, s] - owner == ahead)
        )
        flag = jnp.where(match, jnp.int32(1), flag)
    return flag


def fill_table(tab_ref, base, flag, own_ref, other_ref, diag):
    slack = 1.0 + 1.0 / 1024.0

    def one_strip(i, extra):
        low = jnp.minimum(own_ref[2 * i], own_ref[2 * i + 1]) - slack
        high = jnp.maximum(own_ref[SUBS + 2 * i], own_ref[SUBS + 2 * i + 1]) + slack
        first = jnp.int32(0)
        end = jnp.int32(SUBS)
        for j in range(SUBS):
            first = first + jnp.where(other_ref[SUBS + j] <= low, 1, 0)
            end = end - jnp.where(other_ref[j] >= high, 1, 0)
        if diag:
            start = 2 * i + DIAG_W // SUB - OFF_SUBS
        else:
            start = jnp.minimum(first, SUBS - OFF_SUBS)
        tab_ref[base + T_START + i] = start
        tab_ref[base + T_END + i] = end
        return extra + jnp.maximum(end - (start + OFF_SUBS), 0)

    extra = lax.fori_loop(0, STRIPS, one_strip, jnp.int32(0))
    tab_ref[base + T_LIVE] = flag
    tab_ref[base + T_EXTRA] = extra * flag


def kernel_values(squared):
    squared = jnp.maximum(squared, 1e-30)
    t = jnp.maximum(1.0 - squared * lax.rsqrt(squared), 0.0)
    t2 = t * t
    return ((t2 * t2) * (1.25 - t)).astype(bf16)


def tile_by_difference(row_side, row_at, col_side, col_at):
    squared = None
    for axis in range(16, 19):
        mine = jnp.broadcast_to(row_side[axis : axis + 1, pl.ds(row_at, SUB)], (SUB, SUB)).T
        diff = mine - col_side[axis : axis + 1, pl.ds(col_at, SUB)]
        part = diff * diff
        squared = part if squared is None else squared + part
    return kernel_values(squared)


def fast_strip(k_ref, i, lhs, rhs, start, width):
    for h in range(width // STRIP):
        right = rhs[:, pl.ds(start + h * STRIP, STRIP)]
        for g in range(STRIP // SUB):
            rows = slice(i * STRIP + g * SUB, i * STRIP + (g + 1) * SUB)
            k_ref[i, g * SUB : (g + 1) * SUB, h * STRIP : (h + 1) * STRIP] = kernel_values(nn(lhs[rows, :], right))


def slow_build(k_ref, row_side, col_side, first_group, groups):
    def strip(i, carry):
        def tile(j, carry):
            for g in range(STRIP // SUB):
                at = pl.multiple_of(i * STRIP + g * SUB, SUB)
                col_at = pl.multiple_of(jnp.minimum(first_group(i) + j, SUBS - 1) * SUB, SUB)
                k_ref[i, g * SUB : (g + 1) * SUB, pl.ds(pl.multiple_of(j * SUB, SUB), SUB)] = (
                    tile_by_difference(row_side, at, col_side, col_at)
                )
            return carry

        return lax.fori_loop(0, groups, tile, carry)

    lax.fori_loop(0, STRIPS, strip, 0)


def right_features(rhs, row_side, col_side):
    offset = offset_of(col_side, row_side)
    rows, norm = features(offset, False)
    rhs[...] = rows.astype(bf16)
    offset = offset_of(row_side, row_side)
    return jnp.maximum(jnp.max(norm), jnp.max(jnp.sum(offset * offset, axis=0, keepdims=True))) <= 100.0


def off_pair(k_ref, tab_ref, base, lhs, rhs, row_side, col_side, v_row, v_col, acc_row, acc_col):
    near = right_features(rhs, row_side, col_side)

    @pl.when(near)
    def _():
        for i in range(STRIPS):
            start = pl.multiple_of(tab_ref[base + T_START + i] * SUB, SUB)
            fast_strip(k_ref, i, lhs, rhs, start, OFF_W)
            owner_strip(k_ref, i, start, v_col, acc_row)
            partner_strip(k_ref, i, start, v_row, acc_col)

    @pl.when(jnp.logical_not(near))
    def _():
        slow_build(k_ref, row_side, col_side, lambda i: tab_ref[base + T_START + i], OFF_SUBS)
        to_owner(k_ref, tab_ref, base, v_col, acc_row)
        to_partner(k_ref, tab_ref, base, v_row, acc_col)


def diag_pair(k_ref, lhs, rhs, side, v, acc):
    near = right_features(rhs, side, side)

    @pl.when(near)
    def _():
        for i in range(STRIPS):
            fast_strip(k_ref, i, lhs, rhs, i * STRIP, min(DIAG_W, BLK - i * STRIP))
            diag_strip(k_ref, i, v, acc)

    @pl.when(jnp.logical_not(near))
    def _():
        slow_build(k_ref, side, side, lambda i: 2 * i, DIAG_W // SUB)
        diag_products(k_ref, v, acc)


def owner_strip(k_ref, i, start, v_col, acc_row):
    acc_row[:, i * STRIP : (i + 1) * STRIP] += halves(nt(v_col[:, pl.ds(start, OFF_W)], k_ref[i]))


def partner_strip(k_ref, i, start, v_row, acc_col):
    acc_col[:, pl.ds(start, OFF_W)] += halves(nn(v_row[:, i * STRIP : (i + 1) * STRIP], k_ref[i]))


def to_owner(k_ref, tab_ref, base, v_col, acc_row):
    for i in range(STRIPS):
        owner_strip(k_ref, i, pl.multiple_of(tab_ref[base + T_START + i] * SUB, SUB), v_col, acc_row)


def to_partner(k_ref, tab_ref, base, v_row, acc_col):
    for i in range(STRIPS):
        partner_strip(k_ref, i, pl.multiple_of(tab_ref[base + T_START + i] * SUB, SUB), v_row, acc_col)


def diag_strip(k_ref, i, v_ref, acc_ref):
    width = min(DIAG_W, BLK - i * STRIP)
    here = slice(i * STRIP, (i + 1) * STRIP)
    acc_ref[:, here] += halves(nt(v_ref[:, i * STRIP : i * STRIP + width], k_ref[i, :, :width]))
    if width > STRIP:
        after = slice((i + 1) * STRIP, i * STRIP + width)
        acc_ref[:, after] += halves(nn(v_ref[:, here], k_ref[i, :, STRIP:width]))


def diag_products(k_ref, v_ref, acc_ref):
    for i in range(STRIPS):
        diag_strip(k_ref, i, v_ref, acc_ref)


def extra_tiles(tab_ref, base, row_side, col_side, tile_ref, v_row, v_col, acc_row, acc_col):
    @pl.when(tab_ref[base + T_EXTRA] > 0)
    def _():
        def strip(i, carry):
            here = pl.ds(pl.multiple_of(i * STRIP, STRIP), STRIP)

            def tile(j, carry):
                col_at = pl.multiple_of(j * SUB, SUB)
                there = pl.ds(col_at, SUB)
                for g in range(STRIP // SUB):
                    row_at = pl.multiple_of(i * STRIP + g * SUB, SUB)
                    tile_ref[g * SUB : (g + 1) * SUB, :] = tile_by_difference(row_side, row_at, col_side, col_at)
                if acc_row is not None:
                    acc_row[:, here] += halves(nt(v_col[:, there], tile_ref[...]))
                if acc_col is not None:
                    acc_col[:, there] += halves(nn(v_row[:, here], tile_ref[...]))
                return carry

            return lax.fori_loop(
                tab_ref[base + T_START + i] + OFF_SUBS, tab_ref[base + T_END + i], tile, carry
            )

        lax.fori_loop(0, STRIPS, strip, 0)


TILE = pltpu.VMEM((STRIP, SUB), bf16)
SPLIT = pltpu.VMEM((2 * N_PROBES, BLK), bf16)
FIELD = (N_PROBES, BLK)


def call(body, outs, ins, out_specs, scratch, flops, name, limit=12):
    def run(*args):
        return pl.pallas_call(
            body,
            out_shape=outs,
            in_specs=ins,
            out_specs=out_specs,
            scratch_shapes=scratch,
            compiler_params=pltpu.CompilerParams(vmem_limit_bytes=limit * MIB),
            cost_estimate=pl.CostEstimate(flops=flops, bytes_accessed=MIB, transcendentals=0),
            name=name,
        )(*args)

    return run


def diag_build_kernel(
    flags, yb0, yb1, s0, s1, lhs0, lhs1, k00, k11, tab, acc0, acc1, tile, v0, v1, rhs
):
    fill_table(tab, 0 * T_SIZE, flags[0], yb0, yb0, True)
    fill_table(tab, 1 * T_SIZE, flags[1], yb0, yb1, False)
    fill_table(tab, 2 * T_SIZE, flags[2], yb1, yb1, True)
    acc0[...] = jnp.zeros(FIELD, f32)
    acc1[...] = jnp.zeros(FIELD, f32)
    v0[...] = split2(s0[0:16, :])
    v1[...] = split2(s1[0:16, :])

    @pl.when(flags[0] > 0)
    def _():
        diag_pair(k00, lhs0, rhs, s0, v0, acc0)
        extra_tiles(tab, 0 * T_SIZE, s0, s0, tile, v0, v0, acc0, acc0)

    @pl.when(flags[2] > 0)
    def _():
        diag_pair(k11, lhs1, rhs, s1, v1, acc1)
        extra_tiles(tab, 2 * T_SIZE, s1, s1, tile, v1, v1, acc1, acc1)


def halo_build_kernel(
    flags, yb1, s1, lhs1, got_a, got_b, acc1_in, k12, tab, acc1, back, halo, yb2, tile, v1, v2, rhs
):
    halo[...] = jnp.where(flags[4] == 0, got_a[...], got_b[...])
    bounds(halo, yb2)
    fill_table(tab, 0, flags[3], yb1, yb2, False)
    acc1[...] = acc1_in[...]
    back[...] = jnp.zeros(FIELD, f32)

    @pl.when(flags[3] > 0)
    def _():
        v1[...] = split2(s1[0:16, :])
        v2[...] = split2(halo[0:16, :])
        off_pair(k12, tab, 0, lhs1, rhs, s1, halo, v1, v2, acc1, back)
        extra_tiles(tab, 0, s1, halo, tile, v1, v2, acc1, back)


def own_build_kernel(tab, s0, s1, lhs0, acc0_in, acc1_in, k01, acc0, acc1, tile, v0, v1, rhs):
    base = 1 * T_SIZE
    acc0[...] = acc0_in[...]
    acc1[...] = acc1_in[...]

    @pl.when(tab[base + T_LIVE] > 0)
    def _():
        v0[...] = split2(s0[0:16, :])
        v1[...] = split2(s1[0:16, :])
        off_pair(k01, tab, base, lhs0, rhs, s0, s1, v0, v1, acc0, acc1)
        extra_tiles(tab, base, s0, s1, tile, v0, v1, acc0, acc1)


def own_apply_kernel(tab, k00, k01, k11, s0, s1, w0, w1, acc0, acc1, tile, v0, v1):
    acc0[...] = jnp.zeros(FIELD, f32)
    acc1[...] = jnp.zeros(FIELD, f32)
    v0[...] = split2(w0[...])
    v1[...] = split2(w1[...])

    @pl.when(tab[0 * T_SIZE + T_LIVE] > 0)
    def _():
        diag_products(k00, v0, acc0)
        extra_tiles(tab, 0 * T_SIZE, s0, s0, tile, v0, v0, acc0, acc0)

    @pl.when(tab[1 * T_SIZE + T_LIVE] > 0)
    def _():
        to_owner(k01, tab, 1 * T_SIZE, v1, acc0)
        to_partner(k01, tab, 1 * T_SIZE, v0, acc1)
        extra_tiles(tab, 1 * T_SIZE, s0, s1, tile, v0, v1, acc0, acc1)

    @pl.when(tab[2 * T_SIZE + T_LIVE] > 0)
    def _():
        diag_products(k11, v1, acc1)
        extra_tiles(tab, 2 * T_SIZE, s1, s1, tile, v1, v1, acc1, acc1)


def inner(left, right):
    product = left * right
    return jnp.sum(product, axis=1, keepdims=True)


def finish_kernel(
    level, flags, tab, k12, s0, s1, halo, got_a, got_b, acc0, acc1, w0, w1, mom_in,
    n0, n1, send_a, send_b, mom, tile, v1, v2, acc, back
):
    live = tab[T_LIVE] > 0
    acc[...] = acc1[...]
    if level > 1:

        @pl.when(live)
        def _():
            v2[...] = split2(jnp.where(flags[4] == 0, got_a[...], got_b[...]))
            to_owner(k12, tab, 0, v2, acc)
            extra_tiles(tab, 0, s1, halo, tile, None, v2, acc, None)

    before0 = w0[0:16, :]
    before1 = w1[0:16, :]
    next1 = s1[19:20, :] * before1 + acc[...]
    n1[...] = next1
    back[...] = jnp.zeros(FIELD, f32)

    @pl.when(live)
    def _():
        v1[...] = split2(next1)
        to_partner(k12, tab, 0, v1, back)
        extra_tiles(tab, 0, s1, halo, tile, v1, None, None, back)

    arrived = jnp.where(flags[4] == 0, got_b[...], got_a[...])
    next0 = s0[19:20, :] * before0 + (acc0[...] + arrived)
    n0[...] = next0
    send_a[...] = jnp.where(flags[4] == 0, back[...], next0)
    send_b[...] = jnp.where(flags[4] == 0, next0, back[...])
    lane = lax.broadcasted_iota(jnp.int32, (N_PROBES, SUB), 1)
    cross = inner(before0, next0) + inner(before1, next1)
    own = inner(next0, next0) + inner(next1, next1)
    total = jnp.where(lane == 2 * level - 1, cross, jnp.where(lane == 2 * level, own, 0.0))
    if level == 1:
        total = jnp.where(lane == 0, inner(before0, before0) + inner(before1, before1), total)
    else:
        total = total + mom_in[...]
    mom[...] = total


def moment_kernel(flags, s0, s1, acc0, acc1, got_a, got_b, w0, w1, mom_in, mom):
    lane = lax.broadcasted_iota(jnp.int32, (N_PROBES, SUB), 1)
    one = w0[...]
    two = w1[...]
    arrived = jnp.where(flags[4] == 0, got_b[...], got_a[...])
    cross = inner(one, s0[19:20, :] * one + (acc0[...] + 2.0 * arrived))
    cross = cross + inner(two, s1[19:20, :] * two + acc1[...])
    mom[...] = mom_in[...] + jnp.where(lane == 5, cross, 0.0)


def last_kernel(flags, tab, k12, s0, s1, halo, got_a, got_b, acc0, acc1, w0, w1, n0, n1, tile, v2):
    arrived = jnp.where(flags[4] == 0, got_b[...], got_a[...])
    n1[...] = s1[19:20, :] * w1[...] + acc1[...]
    n0[...] = s0[19:20, :] * w0[...] + (acc0[...] + arrived)

    @pl.when(tab[T_LIVE] > 0)
    def _():
        v2[...] = split2(jnp.where(flags[4] == 0, got_a[...], got_b[...]))
        to_owner(k12, tab, 0, v2, n1)
        extra_tiles(tab, 0, s1, halo, tile, None, v2, n1, None)


def unsort_kernel(rank_ref, wa, wb, wc, out):
    stacked = jnp.concatenate([split2(wa[...]), split2(wb[...]), split2(wc[...])], axis=0)
    rank = rank_ref[...]
    place = places()
    marked = [marks(rank, g) for g in range(STRIPS)]
    for c in range(STRIPS):
        here = slice(c * STRIP, (c + 1) * STRIP)
        got = None
        for g in range(STRIPS):
            part = nn(stacked[:, g * STRIP : (g + 1) * STRIP], one_hot(marked[g], c, place))
            got = part if got is None else got + part
        for k in range(3):
            out[16 * k : 16 * (k + 1), here] = halves(got[32 * k : 32 * (k + 1)])


def combine_kernel(mom, probes, u0, u1, sol, res):
    lane = lax.broadcasted_iota(jnp.int32, (N_PROBES, SUB), 1)
    mu = [jnp.sum(jnp.where(lane == k, mom[...], 0.0), axis=1, keepdims=True) for k in range(6)]

    def form(left, right, shift):
        total = None
        for i, a in enumerate(left):
            for j, b in enumerate(right):
                part = (a * b) * mu[i + j + shift]
                total = part if total is None else total + part
        return total

    one = jnp.ones((N_PROBES, 1), f32)
    d = [one]
    r = [one]
    s = []
    rr = mu[0]
    for it in range(3):
        step = rr / form(d, d, 1)
        moved = [step * v for v in d]
        s = [a + b for a, b in zip(s + [0.0] * (len(d) - len(s)), moved)]
        r = [r[0]] + [(r[i] if i < len(r) else 0.0) - moved[i - 1] for i in range(1, len(moved) + 1)]
        if it < 2:
            new = form(r, r, 0)
            ratio = new / rr
            d = [r[i] + (ratio * d[i] if i < len(d) else 0.0) for i in range(len(r))]
            rr = new
    for b, u in ((0, u0), (1, u1)):
        here = slice(b * BLK, (b + 1) * BLK)
        w = [probes[:, here], u[0:16, :], u[16:32, :], u[32:48, :]]
        sol[:, here] = (s[0] * w[0] + s[1] * w[1]) + s[2] * w[2]
        res[:, here] = ((r[0] * w[0] + r[1] * w[1]) + r[2] * w[2]) + r[3] * w[3]


def swapped_both(to_a, to_b):
    count = lax.axis_size("gx")
    a = lax.ppermute(to_a, "gx", [(k, k ^ 1) for k in range(count)])
    b = lax.ppermute(to_b, "gx", [(k, ((k + 1) ^ 1) - 1) for k in range(1, count - 1)])
    return a, b


def sum_over(value, axis):
    return jnp.sum(lax.all_gather(value, axis), axis=0)


def on_device(points, noise_var, probes, pair_list, counts):
    noise = noise_var.reshape(1, -1)
    field = pltpu.VMEM(FIELD, f32)
    side = pltpu.VMEM((24, BLK), f32)
    left = pltpu.VMEM((BLK, N_FEATURES), bf16)
    right = pltpu.VMEM((N_FEATURES, BLK), bf16)
    limits = jax.ShapeDtypeStruct((2 * SUBS,), f32)
    ranks = pltpu.VMEM((1, BLK), jnp.int32)
    far_space = pl.BlockSpec(memory_space=pltpu.HBM)
    s0, s1, lhs0, lhs1, yb0, yb1, rank0, rank1, flags = call(
        sort_kernel,
        (side, side, left, left, limits, limits, ranks, ranks, jax.ShapeDtypeStruct((5,), jnp.int32)),
        [far_space] * 4 + [SMEM],
        (VMEM,) * 4 + (SMEM,) * 2 + (VMEM,) * 2 + (SMEM,),
        [
            pltpu.VMEM(points.shape, f32),
            pltpu.VMEM(noise.shape, f32),
            pltpu.VMEM(probes.shape, f32),
            pltpu.SMEM(pair_list.shape[::-1], jnp.int32),
            pltpu.VMEM((BLK, SUB), jnp.int32),
            pltpu.SemaphoreType.DMA((4,)),
        ],
        10**9,
        "sort_blocks",
    )(*[pltpu.with_memory_space_constraint(x, pltpu.HBM) for x in (points, noise, probes, pair_list.T)], counts)

    halos = swapped_both(s0, s0)
    off = pltpu.VMEM((STRIPS, STRIP, OFF_W), bf16)
    diag = pltpu.VMEM((STRIPS, STRIP, DIAG_W), bf16)
    k00, k11, tabb, acc0, acc1 = call(
        diag_build_kernel,
        (diag, diag, jax.ShapeDtypeStruct((3 * T_SIZE,), jnp.int32), field, field),
        [SMEM] * 3 + [VMEM] * 4,
        (VMEM, VMEM, SMEM, VMEM, VMEM),
        [TILE, SPLIT, SPLIT, right],
        3 * 10**9,
        "diag_build",
    )(flags, yb0, yb1, s0, s1, lhs0, lhs1)
    k12, tabc, acc1, back, halo = call(
        halo_build_kernel,
        (off, jax.ShapeDtypeStruct((T_SIZE,), jnp.int32), field, field, side),
        [SMEM] * 2 + [VMEM] * 5,
        (VMEM, SMEM, VMEM, VMEM, VMEM),
        [pltpu.SMEM((2 * SUBS,), f32), TILE, SPLIT, SPLIT, right],
        3 * 10**9,
        "halo_build",
    )(flags, yb1, s1, lhs1, *halos, acc1)
    got = swapped_both(back, back)
    k01, acc0, acc1 = call(
        own_build_kernel,
        (off, field, field),
        [SMEM] + [VMEM] * 5,
        (VMEM,) * 3,
        [TILE, SPLIT, SPLIT, right],
        5 * 10**9,
        "own_build",
    )(tabb, s0, s1, lhs0, acc0, acc1)

    w0, w1 = s0, s1
    moments = pltpu.VMEM((N_PROBES, SUB), f32)
    mom = jnp.zeros((N_PROBES, SUB), f32)
    kept = []
    for level in (1, 2):
        w0, w1, send_a, send_b, mom = call(
            functools.partial(finish_kernel, level),
            (field,) * 4 + (moments,),
            [SMEM] * 2 + [VMEM] * 11,
            (VMEM,) * 5,
            [TILE, SPLIT, SPLIT, pltpu.VMEM(FIELD, f32), pltpu.VMEM(FIELD, f32)],
            10**9,
            "finish",
        )(flags, tabc, k12, s0, s1, halo, *got, acc0, acc1, w0, w1, mom)
        kept.append((w0, w1))
        got = swapped_both(send_a, send_b)
        acc0, acc1 = call(
            own_apply_kernel,
            (field, field),
            [SMEM] + [VMEM] * 7,
            (VMEM, VMEM),
            [TILE, SPLIT, SPLIT],
            2 * 10**9,
            "own_apply",
        )(tabb, k00, k01, k11, s0, s1, w0, w1)
    mom = call(moment_kernel, moments, [SMEM] + [VMEM] * 9, VMEM, [], 10**7, "moment")(
        flags, s0, s1, acc0, acc1, *got, w0, w1, mom
    )
    total = sum_over(mom, "gx")
    kept.append(
        call(last_kernel, (field, field), [SMEM] * 2 + [VMEM] * 10, (VMEM, VMEM), [TILE, SPLIT], 10**9, "last")(
            flags, tabc, k12, s0, s1, halo, *got, acc0, acc1, w0, w1
        )
    )
    given = []
    for b, rank in ((0, rank0), (1, rank1)):
        given.append(
            call(
                unsort_kernel,
                pltpu.VMEM((3 * N_PROBES, BLK), f32),
                [VMEM] * 4,
                VMEM,
                [],
                2 * 96 * BLK * BLK,
                "unsort",
            )(rank, *[pair[b] for pair in kept])
        )
    return call(
        combine_kernel,
        (jax.ShapeDtypeStruct(probes.shape, f32),) * 2,
        [VMEM] * 4,
        (VMEM, VMEM),
        [],
        10**6,
        "combine",
    )(total, probes, *given)


def solution(mesh):
    placed = (
        P(None, ("groups", "gx")),
        P(("groups", "gx")),
        P(None, ("groups", "gx")),
        P(("groups", "gx"), None),
        P(("groups", "gx")),
    )
    return jax.shard_map(
        on_device,
        mesh=mesh,
        in_specs=placed,
        out_specs=(P(None, ("groups", "gx")), P(None, ("groups", "gx"))),
        check_vma=False,
    )
```

time: 98.8 us -> 95.8 us (0.970)
  blocking collectives: 0 us -> 27.6 us
  starting transfers between devices: 38.6 us -> 13 us
  Pallas kernels: 55.1 us -> 46.6 us
  local copies, waits for them, and re-layouts: 3.28 us -> 6.46 us
    all_gather x0 -> x1, blocking collectives: none -> 27.6 us  [sum_over(): return jnp.sum(lax.all_gather(value, axis), axis=0)]
    ppermute x15 -> x0, starting transfers between devices: 26.2 us -> none  [sum_over(): lax.ppermute(value, axis, [(k, k ^ m * step) for k in range(count)])]
    pallas_call x13, Pallas kernels: 55.1 us -> 46.6 us  [run(): pl.pallas_call(body, out_shape=outs, in_specs=ins, out_specs=out_specs, s...]
    unnamed x9 -> x46, local copies, waits for them, and re-layouts: 3.28 us -> 6.46 us
  transfers between devices with their start and end apart: 23 -> 8, of which waited for: 1 -> 0; matrix products, arithmetic and copies ran while one was open for 0% -> 0% of each run, Pallas kernels for 30% -> 21%
where the time goes in v4:
time: 95.8 us; the launch traced here: 96.3 us
  Pallas kernels  46.6 us (49%)
  blocking collectives  27.6 us (29%)
  starting transfers between devices  13 us (14%)
  local copies, waits for them, and re-layouts  6.46 us (7%)
  between operations  1.6 us (2%)
    pallas_call x13, Pallas kernels, run(): pl.pallas_call(body, out_shape=outs, in_specs=ins, out_specs=out_specs, s...  46.6 us
    all_gather x1, blocking collectives, sum_over(): return jnp.sum(lax.all_gather(value, axis), axis=0)  27.6 us
    ppermute x4, starting transfers between devices, swapped_both(): a = lax.ppermute(to_a, 'gx', [(k, k ^ 1) for k in range(count)])  10.3 us
    unnamed x46, local copies, waits for them, and re-layouts  6.46 us
    ppermute x4, starting transfers between devices, swapped_both(): lax.ppermute(to_b, 'gx', [(k, (k + 1 ^ 1) - 1) for k in range(1, count -...  2.66 us
  transfers between devices with their start and end apart: 8, of which 0 were waited for; matrix products, arithmetic and copies ran while one was open for 0% of the time, Pallas kernels for 21%

profile of v4, /device:TPU:0, one launch (start us, length us, event | category | flops | bytes accessed | tf_op | source)
XLA Modules:
  0.0 96.3 jit_solution(3396076006334663537)
XLA Ops:
  1.3 11.1 %sort_blocks.1 = (f32[24,2048]{1,0:T(8,128)S(1)}, f32[24,2048]{1,0:T(8,128)S(1)}, bf16[2048,64]{1,0:T(8,128)(2,1)S(1)}, bf16[2048,64]{1,0:T(8,128)(2,1)S(1)}, f3...) custom-call(f32[3,4096]{1,0:T(4,128)} %pts_hbm.1, ...), custom_call_target="tpu_custom_call" | custom-call | flops 1000000000 | bytes 1048576 | tf_op jit(solution)/shard_map/sort_blocks/pallas_call | solution.py:361
  13.1 4.4 %collective-permute-start = (f32[24,2048]{1,0:T(8,128)S(1)}, f32[24,2048]{1,0:T(8,128)S(1)}, u32[]{:S(2)}, u32[]{:S(2)}) collective-permute-start(f32[24,2048]{1,0:T(8,128)S(1)} %get-tuple-element.41.s0.w0), channel_id=1, source_target_pairs={{0,1},{1,0},{2,3},{3,2},{4,5},{5,4},{6,7},{7,6},{8,9},{9,8},{10,11... | collective-permute-start | bytes 589832 | tf_op jit(solution)/shard_map/ppermute | solution.py:570
  17.5 8.0 %diag_build.1 = (bf16[8,256,512]{2,1,0:T(8,128)(2,1)S(1)}, bf16[8,256,512]{2,1,0:T(8,128)(2,1)S(1)}, s32[72]{0:T(128)S(1)}, f32[16,2048]{1,0:T(8,128)S(1)}, f32[16,2048]{1,0:T(8,128)S(1)}) custom-call(s32[5]{0:T(128)S(1)} %get-tuple-element.40.flags, f32[32]{0:T(128)S(1)} %get-tuple-element.43.yb0, f32[32]{0:T(128)S(1)} %get-tuple-element.44.yb1, ...), custom_call_target="tpu_custom_call" | custom-call | flops 3000000000 | bytes 1048576 | tf_op jit(solution)/shard_map/diag_build/pallas_call | solution.py:361
  25.5 5.9 %halo_build.1 = (bf16[8,256,768]{2,1,0:T(8,128)(2,1)S(1)}, s32[24]{0:T(128)S(1)}, f32[16,2048]{1,0:T(8,128)S(1)}, f32[16,2048]{1,0:T(8,128)S(1)}, f32[24,2048]{1,0:T(8,128)S(1)}) custom-call(s32[5]{0:T(128)S(1)} %get-tuple-element.40.flags, f32[32]{0:T(128)S(1)} %get-tuple-element.44.yb1, f32[24,2048]{1,0:T(8,128)S(1)} %get-tuple-element.42.s1.w1, ...), custom_call_target="tpu_custom_call" | custom-call | flops 3000000000 | bytes 1048576 | tf_op jit(solution)/shard_map/halo_build/pallas_call | solution.py:361
  32.2 3.0 %collective-permute-start.2 = (f32[16,2048]{1,0:T(8,128)S(1)}, f32[16,2048]{1,0:T(8,128)S(1)}, u32[]{:S(2)}, u32[]{:S(2)}) collective-permute-start(f32[16,2048]{1,0:T(8,128)S(1)} %get-tuple-element.57), channel_id=1, source_target_pairs={{0,1},{1,0},{2,3},{3,2},{4,5},{5,4},{6,7},{7,6},{8,9},{9,8},{10,11... | collective-permute-start | bytes 393224 | tf_op jit(solution)/shard_map/ppermute | solution.py:570
  35.1 4.4 %own_build.1 = (bf16[8,256,768]{2,1,0:T(8,128)(2,1)S(1)}, f32[16,2048]{1,0:T(8,128)S(1)}, f32[16,2048]{1,0:T(8,128)S(1)}) custom-call(s32[72]{0:T(128)S(1)} %get-tuple-element.47.tab, f32[24,2048]{1,0:T(8,128)S(1)} %get-tuple-element.41.s0.w0, f32[24,2048]{1,0:T(8,128)S(1)} %get-tuple-element.42.s1.w1, bf16[2048,64]{1,0:T(8,128)(2,1)S(1)} %get-tuple-element.45.lhs0, ...), custom_call_target="tpu_custom_call" | custom-call | flops 5000000000 | bytes 1048576 | tf_op jit(solution)/shard_map/own_build/pallas_call | solution.py:361
  39.6 1.4 %finish.2 = (f32[16,2048]{1,0:T(8,128)S(1)}, f32[16,2048]{1,0:T(8,128)S(1)}, f32[16,2048]{1,0:T(8,128)S(1)}, f32[16,2048]{1,0:T(8,128)S(1)}, f32[16,128]{1,0:T(8,128)S(1)}) custom-call(s32[5]{0:T(128)S(1)} %get-tuple-element.40.flags, s32[24]{0:T(128)S(1)} %get-tuple-element.54.tab, bf16[8,256,768]{2,1,0:T(8,128)(2,1)S(1)} %get-tuple-element.55.k12, ...), custom_call_target="tpu_custom_call" | custom-call | flops 1000000000 | bytes 1048576 | tf_op jit(solution)/shard_map/finish/pallas_call | solution.py:361
  41.8 3.7 %own_apply.2 = (f32[16,2048]{1,0:T(8,128)S(1)}, f32[16,2048]{1,0:T(8,128)S(1)}) custom-call(s32[72]{0:T(128)S(1)} %get-tuple-element.47.tab, bf16[8,256,512]{2,1,0:T(8,128)(2,1)S(1)} %get-tuple-element.48.k00, bf16[8,256,768]{2,1,0:T(8,128)(2,1)S(1)} %get-tuple-element.52.k01, bf16[8,256,512]{2,1,0:T(8,128)(2,1)S(1)} %get-tuple-element.53.k11, ...), custom_call_target="tpu_custom_call" | custom-call | flops 2000000000 | bytes 1048576 | tf_op jit(solution)/shard_map/own_apply/pallas_call | solution.py:361
  45.6 2.4 %finish.3 = (f32[16,2048]{1,0:T(8,128)S(1)}, f32[16,2048]{1,0:T(8,128)S(1)}, f32[16,2048]{1,0:T(8,128)S(1)}, f32[16,2048]{1,0:T(8,128)S(1)}, f32[16,128]{1,0:T(8,128)S(1)}) custom-call(s32[5]{0:T(128)S(1)} %get-tuple-element.40.flags, s32[24]{0:T(128)S(1)} %get-tuple-element.54.tab, bf16[8,256,768]{2,1,0:T(8,128)(2,1)S(1)} %get-tuple-element.55.k12, ...), custom_call_target="tpu_custom_call" | custom-call | flops 1000000000 | bytes 1048576 | tf_op jit(solution)/shard_map/finish/pallas_call | solution.py:361
  48.0 2.9 %collective-permute-start.6 = (f32[16,2048]{1,0:T(8,128)S(1)}, f32[16,2048]{1,0:T(8,128)S(1)}, u32[]{:S(2)}, u32[]{:S(2)}) collective-permute-start(f32[16,2048]{1,0:T(8,128)S(1)} %get-tuple-element.71), channel_id=1, source_target_pairs={{0,1},{1,0},{2,3},{3,2},{4,5},{5,4},{6,7},{7,6},{8,9},{9,8},{10,11... | collective-permute-start | bytes 393224 | tf_op jit(solution)/shard_map/ppermute | solution.py:570
  51.6 3.7 %own_apply.3 = (f32[16,2048]{1,0:T(8,128)S(1)}, f32[16,2048]{1,0:T(8,128)S(1)}) custom-call(s32[72]{0:T(128)S(1)} %get-tuple-element.47.tab, bf16[8,256,512]{2,1,0:T(8,128)(2,1)S(1)} %get-tuple-element.48.k00, bf16[8,256,768]{2,1,0:T(8,128)(2,1)S(1)} %get-tuple-element.52.k01, bf16[8,256,512]{2,1,0:T(8,128)(2,1)S(1)} %get-tuple-element.53.k11, ...), custom_call_target="tpu_custom_call" | custom-call | flops 2000000000 | bytes 1048576 | tf_op jit(solution)/shard_map/own_apply/pallas_call | solution.py:361
  56.1 27.6 %all-gather = f32[256,128]{1,0:T(8,128)} all-gather(f32[16,128]{1,0:T(8,128)S(1)} %moment.1), channel_id=2, replica_groups=mesh['groups'=2,'gx'=16] {'gx'}, dimensions={0}, use_global_device_ids=true | all-gather | bytes 139264 | tf_op jit(solution)/shard_map/all_gather | solution.py:576
  83.7 0.9 reduce_sum.9.mom
  84.6 0.9 copy-done.1
  85.6 0.9 copy-done.3
  86.5 0.9 copy-done.5
  87.4 0.9 copy-done.11
  88.3 0.9 copy-done.13
  89.2 0.9 copy-done.15
  90.1 0.9 copy-done.17
  91.0 1.6 %last.1 = (f32[16,2048]{1,0:T(8,128)S(1)}, f32[16,2048]{1,0:T(8,128)S(1)}) custom-call(s32[5]{0:T(128)S(1)} %get-tuple-element.40.flags, s32[24]{0:T(128)S(1)} %get-tuple-element.54.tab, bf16[8,256,768]{2,1,0:T(8,128)(2,1)S(1)} %get-tuple-element.55.k12, f32[24,2048]{1,0:T(8,128)S(1)} %get-tuple-element.41.s0.w0, f32[24,2048]{1,0:T(8,128)S(1)} %get-tuple-element.42.s1.w1, ...), custom_call_target="tpu_custom_call" | custom-call | flops 1000000000 | bytes 1048576 | tf_op jit(solution)/shard_map/last/pallas_call | solution.py:361
  92.6 1.3 %unsort.2.u0 = f32[48,2048]{1,0:T(8,128)S(1)} custom-call(s32[1,2048]{1,0:T(1,128)S(1)} %copy-done.22, f32[16,2048]{1,0:T(8,128)S(1)} %copy-done.9, f32[16,2048]{1,0:T(8,128)S(1)} %copy-done.5, f32[16,2048]{1,0:T(8,128)S(1)} %get-tuple-element.75.wc), custom_call_target="tpu_custom_call" | custom-call | flops 805306368 | bytes 1048576 | tf_op jit(solution)/shard_map/unsort/pallas_call | solution.py:361
  93.9 1.3 %unsort.3.u1 = f32[48,2048]{1,0:T(8,128)S(1)} custom-call(s32[1,2048]{1,0:T(1,128)S(1)} %copy-done.20, f32[16,2048]{1,0:T(8,128)S(1)} %copy-done.7, f32[16,2048]{1,0:T(8,128)S(1)} %copy-done.3, f32[16,2048]{1,0:T(8,128)S(1)} %get-tuple-element.77.wc), custom_call_target="tpu_custom_call" | custom-call | flops 805306368 | bytes 1048576 | tf_op jit(solution)/shard_map/unsort/pallas_call | solution.py:361
  95.2 1.1 %combine.1 = (f32[16,4096]{1,0:T(8,128)}, f32[16,4096]{1,0:T(8,128)}) custom-call(f32[16,128]{1,0:T(8,128)S(1)} %reduce_sum.9.mom, f32[16,4096]{1,0:T(8,128)S(1)} %copy-done.18, f32[48,2048]{1,0:T(8,128)S(1)} %unsort.2.u0, f32[48,2048]{1,0:T(8,128)S(1)} %unsort.3.u1), custom_call_target="tpu_custom_call" | custom-call | flops 1000000 | bytes 1048576 | tf_op jit(solution)/shard_map/combine/pallas_call | solution.py:361
  (54 shorter events, 3.6 us)
Async XLA Ops:
  12.4 5.1 %copy-start.19 = (s32[1,2048]{1,0:T(1,128)}, s32[1,2048]{1,0:T(1,128)S(1)}, u32[]{:S(2)}) copy-start(s32[1,2048]{1,0:T(1,128)S(1)} %get-tuple-element.76.rank_ref) | copy-start | bytes 24580
  12.4 13.1 %copy-start.21 = (s32[1,2048]{1,0:T(1,128)}, s32[1,2048]{1,0:T(1,128)S(1)}, u32[]{:S(2)}) copy-start(s32[1,2048]{1,0:T(1,128)S(1)} %get-tuple-element.74.rank_ref) | copy-start | bytes 24580
  12.4 13.1 %collective-permute-start.1 = (f32[24,2048]{1,0:T(8,128)S(1)}, f32[24,2048]{1,0:T(8,128)S(1)}, u32[]{:S(2)}, u32[]{:S(2)}) collective-permute-start(f32[24,2048]{1,0:T(8,128)S(1)} %get-tuple-element.41.s0.w0), channel_id=1, source_target_pairs={{1,2},{2,1},{3,4},{4,3},{5,6},{6,5},{7,8},{8,7},{9,10},{10,9},{11,... | collective-permute-start | bytes 589832 | tf_op jit(solution)/shard_map/ppermute | solution.py:571
  13.1 12.4 %collective-permute-start = (f32[24,2048]{1,0:T(8,128)S(1)}, f32[24,2048]{1,0:T(8,128)S(1)}, u32[]{:S(2)}, u32[]{:S(2)}) collective-permute-start(f32[24,2048]{1,0:T(8,128)S(1)} %get-tuple-element.41.s0.w0), channel_id=1, source_target_pairs={{0,1},{1,0},{2,3},{3,2},{4,5},{5,4},{6,7},{7,6},{8,9},{9,8},{10,11... | collective-permute-start | bytes 589832 | tf_op jit(solution)/shard_map/ppermute | solution.py:570
  31.5 14.1 %copy-start = (f32[24,2048]{1,0:T(8,128)}, f32[24,2048]{1,0:T(8,128)S(1)}, u32[]{:S(2)}) copy-start(f32[24,2048]{1,0:T(8,128)S(1)} %get-tuple-element.56.halo) | copy-start | bytes 589828
  31.5 8.0 %collective-permute-start.3 = (f32[16,2048]{1,0:T(8,128)S(1)}, f32[16,2048]{1,0:T(8,128)S(1)}, u32[]{:S(2)}, u32[]{:S(2)}) collective-permute-start(f32[16,2048]{1,0:T(8,128)S(1)} %get-tuple-element.57), channel_id=1, source_target_pairs={{1,2},{2,1},{3,4},{4,3},{5,6},{6,5},{7,8},{8,7},{9,10},{10,9},{11,... | collective-permute-start | bytes 393224 | tf_op jit(solution)/shard_map/ppermute | solution.py:571
  32.2 7.4 %collective-permute-start.2 = (f32[16,2048]{1,0:T(8,128)S(1)}, f32[16,2048]{1,0:T(8,128)S(1)}, u32[]{:S(2)}, u32[]{:S(2)}) collective-permute-start(f32[16,2048]{1,0:T(8,128)S(1)} %get-tuple-element.57), channel_id=1, source_target_pairs={{0,1},{1,0},{2,3},{3,2},{4,5},{5,4},{6,7},{7,6},{8,9},{9,8},{10,11... | collective-permute-start | bytes 393224 | tf_op jit(solution)/shard_map/ppermute | solution.py:570
  41.0 4.6 %copy-start.6 = (f32[16,2048]{1,0:T(8,128)}, f32[16,2048]{1,0:T(8,128)S(1)}, u32[]{:S(2)}) copy-start(f32[16,2048]{1,0:T(8,128)S(1)} %get-tuple-element.63.w1.wa) | copy-start | bytes 393220
  41.0 4.6 %copy-start.8 = (f32[16,2048]{1,0:T(8,128)}, f32[16,2048]{1,0:T(8,128)S(1)}, u32[]{:S(2)}) copy-start(f32[16,2048]{1,0:T(8,128)S(1)} %get-tuple-element.62.w0.wa) | copy-start | bytes 393220
  41.0 4.5 %collective-permute-start.4 = (f32[16,2048]{1,0:T(8,128)S(1)}, f32[16,2048]{1,0:T(8,128)S(1)}, u32[]{:S(2)}, u32[]{:S(2)}) collective-permute-start(f32[16,2048]{1,0:T(8,128)S(1)} %get-tuple-element.60), channel_id=1, source_target_pairs={{0,1},{1,0},{2,3},{3,2},{4,5},{5,4},{6,7},{7,6},{8,9},{9,8},{10,11... | collective-permute-start | bytes 393224 | tf_op jit(solution)/shard_map/ppermute | solution.py:570
  41.1 4.4 %collective-permute-start.5 = (f32[16,2048]{1,0:T(8,128)S(1)}, f32[16,2048]{1,0:T(8,128)S(1)}, u32[]{:S(2)}, u32[]{:S(2)}) collective-permute-start(f32[16,2048]{1,0:T(8,128)S(1)} %get-tuple-element.61), channel_id=1, source_target_pairs={{1,2},{2,1},{3,4},{4,3},{5,6},{6,5},{7,8},{8,7},{9,10},{10,9},{11,... | collective-permute-start | bytes 393224 | tf_op jit(solution)/shard_map/ppermute | solution.py:571
  48.0 7.4 %copy-start.2 = (f32[16,2048]{1,0:T(8,128)}, f32[16,2048]{1,0:T(8,128)S(1)}, u32[]{:S(2)}) copy-start(f32[16,2048]{1,0:T(8,128)S(1)} %get-tuple-element.68.w1.wb) | copy-start | bytes 393220
  48.0 7.4 %copy-start.4 = (f32[16,2048]{1,0:T(8,128)}, f32[16,2048]{1,0:T(8,128)S(1)}, u32[]{:S(2)}) copy-start(f32[16,2048]{1,0:T(8,128)S(1)} %get-tuple-element.67.w0.wb) | copy-start | bytes 393220
  48.0 7.4 %collective-permute-start.6 = (f32[16,2048]{1,0:T(8,128)S(1)}, f32[16,2048]{1,0:T(8,128)S(1)}, u32[]{:S(2)}, u32[]{:S(2)}) collective-permute-start(f32[16,2048]{1,0:T(8,128)S(1)} %get-tuple-element.71), channel_id=1, source_target_pairs={{0,1},{1,0},{2,3},{3,2},{4,5},{5,4},{6,7},{7,6},{8,9},{9,8},{10,11... | collective-permute-start | bytes 393224 | tf_op jit(solution)/shard_map/ppermute | solution.py:570
  50.9 4.5 %collective-permute-start.7 = (f32[16,2048]{1,0:T(8,128)S(1)}, f32[16,2048]{1,0:T(8,128)S(1)}, u32[]{:S(2)}, u32[]{:S(2)}) collective-permute-start(f32[16,2048]{1,0:T(8,128)S(1)} %get-tuple-element.72), channel_id=1, source_target_pairs={{1,2},{2,1},{3,4},{4,3},{5,6},{6,5},{7,8},{8,7},{9,10},{10,9},{11,... | collective-permute-start | bytes 393224 | tf_op jit(solution)/shard_map/ppermute | solution.py:571
  55.3 28.4 %copy-start.14 = (f32[16,2048]{1,0:T(8,128)}, f32[16,2048]{1,0:T(8,128)S(1)}, u32[]{:S(2)}) copy-start(f32[16,2048]{1,0:T(8,128)S(1)} %get-tuple-element.69.acc0) | copy-start | bytes 393220
  55.3 28.4 %copy-start.16 = (f32[16,2048]{1,0:T(8,128)}, f32[16,2048]{1,0:T(8,128)S(1)}, u32[]{:S(2)}) copy-start(f32[16,2048]{1,0:T(8,128)S(1)} %get-tuple-element.70.acc1) | copy-start | bytes 393220
  55.4 28.3 %copy-start.12 = (f32[16,2048]{1,0:T(8,128)}, f32[16,2048]{1,0:T(8,128)S(1)}, u32[]{:S(2)}) copy-start(f32[16,2048]{1,0:T(8,128)S(1)} %collective-permute-done.7.got_b) | copy-start | bytes 393220
  84.6 0.9 copy-start.1
  91.0 1.6 %copy-start.9 = (f32[16,2048]{1,0:T(8,128)S(1)}, f32[16,2048]{1,0:T(8,128)}, u32[]{:S(2)}) copy-start(f32[16,2048]{1,0:T(8,128)} %copy-done.8) | copy-start | bytes 393220
  91.0 1.6 %copy-start.22 = (s32[1,2048]{1,0:T(1,128)S(1)}, s32[1,2048]{1,0:T(1,128)}, u32[]{:S(2)}) copy-start(s32[1,2048]{1,0:T(1,128)} %copy-done.21) | copy-start | bytes 24580
  91.0 2.9 %copy-start.7 = (f32[16,2048]{1,0:T(8,128)S(1)}, f32[16,2048]{1,0:T(8,128)}, u32[]{:S(2)}) copy-start(f32[16,2048]{1,0:T(8,128)} %copy-done.6) | copy-start | bytes 393220
  91.0 2.9 %copy-start.20 = (s32[1,2048]{1,0:T(1,128)S(1)}, s32[1,2048]{1,0:T(1,128)}, u32[]{:S(2)}) copy-start(s32[1,2048]{1,0:T(1,128)} %copy-done.19) | copy-start | bytes 24580
  92.6 2.6 %copy-start.18 = (f32[16,4096]{1,0:T(8,128)S(1)}, f32[16,4096]{1,0:T(8,128)}, u32[]{:S(2)}) copy-start(f32[16,4096]{1,0:T(8,128)} %probes.1) | copy-start | bytes 786436
  (7 other events, 6.1 us)

commit v5 on v4

--- a/solution.py
+++ b/solution.py
@@ -25,8 +25,7 @@
 f32 = jnp.float32
 bf16 = jnp.bfloat16
 
-T_LIVE, T_EXTRA, T_START, T_END = 0, 1, 8, 16
-T_SIZE = 24
+T_START, T_END, T_EXTRA, T_LIVE = 0, 1, 2, 3
 
 
 def nt(left, right):
@@ -75,21 +74,67 @@
 
 
 def rank_of(y_row, key_ref):
-    lane = lax.broadcasted_iota(jnp.int32, (1, BLK), 1)
-    key_row = (y_row * 4096.0).astype(jnp.int32) * BLK + lane
+    low = jnp.min(y_row, axis=1, keepdims=True)
+    high = jnp.max(y_row, axis=1, keepdims=True)
+    scale = 255.0 / jnp.maximum(high - low, 1e-6)
+    key = jnp.clip(jnp.floor((y_row - low) * scale), 0.0, 255.0)
     for c in range(SUBS):
-        piece = jnp.broadcast_to(y_row[:, c * SUB : (c + 1) * SUB], (SUB, SUB)).T
-        sub = lax.broadcasted_iota(jnp.int32, (SUB, SUB), 0) + c * SUB
-        key_ref[c * SUB : (c + 1) * SUB, :] = (piece * 4096.0).astype(jnp.int32) * BLK + sub
-    keys = jnp.broadcast_to(key_row, (8, BLK))
-
-    def count(i, acc):
-        mine = key_ref[pl.ds(pl.multiple_of(i * 8, 8), 8), :]
-        mine = jnp.concatenate([mine] * SUBS, axis=1)
-        return acc + jnp.where(mine < keys, 1, 0)
-
-    acc = lax.fori_loop(0, BLK // 8, count, jnp.zeros((8, BLK), jnp.int32), unroll=8)
-    return jnp.sum(acc, axis=0, keepdims=True)
+        here = slice(c * SUB, (c + 1) * SUB)
+        key_ref[here, :] = jnp.broadcast_to(key[:, here], (SUB, SUB)).T.astype(bf16)
+    strict = key.astype(bf16)
+    loose = (key + 1.0).astype(bf16)
+    ones = jnp.ones((16, STRIP), bf16)
+    one = jnp.ones((STRIP, SUB), bf16)
+    zero = jnp.zeros((STRIP, SUB), bf16)
+    ranks = []
+    for j in range(STRIPS):
+        total = None
+        for i in range(STRIPS):
+            mine = key_ref[i * STRIP : (i + 1) * STRIP, :]
+            parts = []
+            for h in range(2):
+                there = slice(j * STRIP + h * SUB, j * STRIP + (h + 1) * SUB)
+                if i == j:
+                    sub = lax.broadcasted_iota(jnp.int32, (STRIP, SUB), 0).astype(f32)
+                    lane = lax.broadcasted_iota(jnp.int32, (1, SUB), 1).astype(f32) + h * SUB
+                    before = mine.astype(f32) * STRIP + sub < key[:, there] * STRIP + lane
+                    parts.append(jnp.where(before, 1.0, 0.0).astype(bf16))
+                else:
+                    row = (loose if i < j else strict)[:, there]
+                    parts.append(jnp.where(mine < jnp.broadcast_to(row, (STRIP, SUB)), one, zero))
+            part = nn(ones, jnp.concatenate(parts, axis=1))
+            total = part if total is None else total + part
+        ranks.append(total[0:1, :])
+    return jnp.concatenate(ranks, axis=1).astype(jnp.int32)
+
+
+def plan(row_side, col_side, live, diag):
+    y_row = row_side[17:18, :]
+    y_col = col_side[17:18, :]
+    strips = jnp.concatenate([y_row[:, i * STRIP : (i + 1) * STRIP] for i in range(STRIPS)], axis=0)
+    low = jnp.min(strips, axis=1, keepdims=True) - 1.0
+    high = jnp.max(strips, axis=1, keepdims=True) + 1.0
+    groups = jnp.concatenate([y_col[:, j * SUB : (j + 1) * SUB] for j in range(SUBS)], axis=0)
+    own = lax.broadcasted_iota(jnp.int32, (SUBS, SUB), 0) == lax.broadcasted_iota(jnp.int32, (SUBS, SUB), 1)
+
+    def across(value):
+        return jnp.sum(jnp.where(own, value, 0.0), axis=0, keepdims=True)
+
+    group_low = across(jnp.min(groups, axis=1, keepdims=True))
+    group_high = across(jnp.max(groups, axis=1, keepdims=True))
+    lane = lax.broadcasted_iota(jnp.int32, (STRIPS, SUB), 1)
+    place = lane.astype(f32)
+    reached = (group_low < high) & (group_high > low) & (lane < SUBS)
+    end = jnp.max(jnp.where(reached, place + 1.0, 0.0), axis=1, keepdims=True)
+    if diag:
+        start = lax.broadcasted_iota(jnp.int32, (STRIPS, 1), 0).astype(f32) * 2.0 + (DIAG_W // SUB - OFF_SUBS)
+    else:
+        first = jnp.min(jnp.where(reached, place, float(SUBS)), axis=1, keepdims=True)
+        start = jnp.minimum(first, float(SUBS - OFF_SUBS))
+    extra = jnp.sum(jnp.maximum(end - (start + OFF_SUBS), 0.0), axis=0, keepdims=True)
+    alive = live.astype(f32)
+    table = jnp.where(lane == T_START, start, jnp.where(lane == T_END, end, extra))
+    return jnp.where(lane == T_LIVE, alive, table).astype(jnp.int32)
 
 
 def row_id(width):
@@ -113,8 +158,8 @@
 
 
 def sort_kernel(
-    pts_hbm, nv_hbm, pr_hbm, pair_hbm, count, s0, s1, lhs0, lhs1, yb0, yb1, rank0, rank1, flags,
-    pts_ref, nv_ref, pr_ref, pair, key_ref, sems
+    pts_hbm, nv_hbm, pr_hbm, pair_hbm, count, s0, s1, lhs0, lhs1, rank0, rank1, flags, tab,
+    pts_ref, nv_ref, pr_ref, pair, key_ref, plan_ref, sems
 ):
     copies = [
         pltpu.make_async_copy(src, dst, sems.at[k])
@@ -134,7 +179,7 @@
             flags[2 * local + ahead] = live_flag(pair, count, local, ahead)
     flags[4] = jnp.bitwise_and(lax.shift_right_logical(pair[0, 0], 1), 1)
     place = places()
-    for blk, (out_ref, lhs_ref, rank_ref) in enumerate(((s0, lhs0, rank0), (s1, lhs1, rank1))):
+    for blk, (out_ref, rank_ref) in enumerate(((s0, rank0), (s1, rank1))):
         cols = slice(blk * BLK, (blk + 1) * BLK)
         aux = jnp.concatenate(
             [pts_ref[0:3, cols] * 2.0, nv_ref[:, cols], jnp.zeros((4, BLK), f32)], axis=0
@@ -154,25 +199,22 @@
             here = slice(g * STRIP, (g + 1) * STRIP)
             out_ref[0:16, here] = (got[0:16] + got[16:32]) + got[32:48]
             out_ref[16:24, here] = ((got[48:56] + got[56:64]) + got[64:72]) + centre
-        offset = offset_of(out_ref, out_ref)
-        rows, _ = features(offset, True)
+    plan_ref[0:8, :] = plan(s0, s0, flags[0], True)
+    plan_ref[8:16, :] = plan(s0, s1, flags[1], False)
+    plan_ref[16:24, :] = plan(s1, s1, flags[2], True)
+    copy = pltpu.make_async_copy(plan_ref, tab, sems.at[0])
+    copy.start()
+    for side, lhs_ref in ((s0, lhs0), (s1, lhs1)):
+        rows, _ = features(offset_of(side, side), True)
         for c in range(SUBS):
             here = slice(c * SUB, (c + 1) * SUB)
             lhs_ref[here, :] = rows[:, here].T.astype(bf16)
-    bounds(s0, yb0)
-    bounds(s1, yb1)
+    copy.wait()
 
 
 def offset_of(side_ref, centre_ref):
     centre = jnp.concatenate([centre_ref[20:23, 0:1], jnp.zeros((5, 1), f32)], axis=0)
     return jnp.where(row_id(BLK) < 3, side_ref[16:24, :] - centre, 0.0)
-
-
-def bounds(side_ref, yb_ref):
-    for c in range(SUBS):
-        row = side_ref[17:18, c * SUB : (c + 1) * SUB]
-        yb_ref[c] = jnp.min(row)
-        yb_ref[SUBS + c] = jnp.max(row)
 
 
 def live_flag(pair_ref, count_ref, local, ahead):
@@ -188,30 +230,6 @@
     return flag
 
 
-def fill_table(tab_ref, base, flag, own_ref, other_ref, diag):
-    slack = 1.0 + 1.0 / 1024.0
-
-    def one_strip(i, extra):
-        low = jnp.minimum(own_ref[2 * i], own_ref[2 * i + 1]) - slack
-        high = jnp.maximum(own_ref[SUBS + 2 * i], own_ref[SUBS + 2 * i + 1]) + slack
-        first = jnp.int32(0)
-        end = jnp.int32(SUBS)
-        for j in range(SUBS):
-            first = first + jnp.where(other_ref[SUBS + j] <= low, 1, 0)
-            end = end - jnp.where(other_ref[j] >= high, 1, 0)
-        if diag:
-            start = 2 * i + DIAG_W // SUB - OFF_SUBS
-        else:
-            start = jnp.minimum(first, SUBS - OFF_SUBS)
-        tab_ref[base + T_START + i] = start
-        tab_ref[base + T_END + i] = end
-        return extra + jnp.maximum(end - (start + OFF_SUBS), 0)
-
-    extra = lax.fori_loop(0, STRIPS, one_strip, jnp.int32(0))
-    tab_ref[base + T_LIVE] = flag
-    tab_ref[base + T_EXTRA] = extra * flag
-
-
 def kernel_values(squared):
     squared = jnp.maximum(squared, 1e-30)
     t = jnp.maximum(1.0 - squared * lax.rsqrt(squared), 0.0)
@@ -267,14 +285,14 @@
     @pl.when(near)
     def _():
         for i in range(STRIPS):
-            start = pl.multiple_of(tab_ref[base + T_START + i] * SUB, SUB)
+            start = pl.multiple_of(tab_ref[base + i, T_START] * SUB, SUB)
             fast_strip(k_ref, i, lhs, rhs, start, OFF_W)
             owner_strip(k_ref, i, start, v_col, acc_row)
             partner_strip(k_ref, i, start, v_row, acc_col)
 
     @pl.when(jnp.logical_not(near))
     def _():
-        slow_build(k_ref, row_side, col_side, lambda i: tab_ref[base + T_START + i], OFF_SUBS)
+        slow_build(k_ref, row_side, col_side, lambda i: tab_ref[base + i, T_START], OFF_SUBS)
         to_owner(k_ref, tab_ref, base, v_col, acc_row)
         to_partner(k_ref, tab_ref, base, v_row, acc_col)
 
@@ -304,12 +322,12 @@
 
 def to_owner(k_ref, tab_ref, base, v_col, acc_row):
     for i in range(STRIPS):
-        owner_strip(k_ref, i, pl.multiple_of(tab_ref[base + T_START + i] * SUB, SUB), v_col, acc_row)
+        owner_strip(k_ref, i, pl.multiple_of(tab_ref[base + i, T_START] * SUB, SUB), v_col, acc_row)
 
 
 def to_partner(k_ref, tab_ref, base, v_row, acc_col):
     for i in range(STRIPS):
-        partner_strip(k_ref, i, pl.multiple_of(tab_ref[base + T_START + i] * SUB, SUB), v_row, acc_col)
+        partner_strip(k_ref, i, pl.multiple_of(tab_ref[base + i, T_START] * SUB, SUB), v_row, acc_col)
 
 
 def diag_strip(k_ref, i, v_ref, acc_ref):
@@ -327,7 +345,7 @@
 
 
 def extra_tiles(tab_ref, base, row_side, col_side, tile_ref, v_row, v_col, acc_row, acc_col):
-    @pl.when(tab_ref[base + T_EXTRA] > 0)
+    @pl.when(tab_ref[base, T_EXTRA] > 0)
     def _():
         def strip(i, carry):
             here = pl.ds(pl.multiple_of(i * STRIP, STRIP), STRIP)
@@ -345,7 +363,7 @@
                 return carry
 
             return lax.fori_loop(
-                tab_ref[base + T_START + i] + OFF_SUBS, tab_ref[base + T_END + i], tile, carry
+                tab_ref[base + i, T_START] + OFF_SUBS, tab_ref[base + i, T_END], tile, carry
             )
 
         lax.fori_loop(0, STRIPS, strip, 0)
@@ -373,35 +391,34 @@
 
 
 def diag_build_kernel(
-    flags, yb0, yb1, s0, s1, lhs0, lhs1, k00, k11, tab, acc0, acc1, tile, v0, v1, rhs
+    tab, s0, s1, lhs0, lhs1, k00, k11, acc0, acc1, tile, v0, v1, rhs
 ):
-    fill_table(tab, 0 * T_SIZE, flags[0], yb0, yb0, True)
-    fill_table(tab, 1 * T_SIZE, flags[1], yb0, yb1, False)
-    fill_table(tab, 2 * T_SIZE, flags[2], yb1, yb1, True)
     acc0[...] = jnp.zeros(FIELD, f32)
     acc1[...] = jnp.zeros(FIELD, f32)
     v0[...] = split2(s0[0:16, :])
     v1[...] = split2(s1[0:16, :])
 
-    @pl.when(flags[0] > 0)
+    @pl.when(tab[0, T_LIVE] > 0)
     def _():
         diag_pair(k00, lhs0, rhs, s0, v0, acc0)
-        extra_tiles(tab, 0 * T_SIZE, s0, s0, tile, v0, v0, acc0, acc0)
-
-    @pl.when(flags[2] > 0)
+        extra_tiles(tab, 0, s0, s0, tile, v0, v0, acc0, acc0)
+
+    @pl.when(tab[16, T_LIVE] > 0)
     def _():
         diag_pair(k11, lhs1, rhs, s1, v1, acc1)
-        extra_tiles(tab, 2 * T_SIZE, s1, s1, tile, v1, v1, acc1, acc1)
+        extra_tiles(tab, 16, s1, s1, tile, v1, v1, acc1, acc1)
 
 
 def halo_build_kernel(
-    flags, yb1, s1, lhs1, got_a, got_b, acc1_in, k12, tab, acc1, back, halo, yb2, tile, v1, v2, rhs
+    flags, s1, lhs1, got_a, got_b, acc1_in, k12, tab, acc1, back, halo, plan_ref, tile, v1, v2, rhs, sem
 ):
     halo[...] = jnp.where(flags[4] == 0, got_a[...], got_b[...])
-    bounds(halo, yb2)
-    fill_table(tab, 0, flags[3], yb1, yb2, False)
+    plan_ref[...] = plan(s1, halo, flags[3], False)
+    copy = pltpu.make_async_copy(plan_ref, tab, sem.at[0])
+    copy.start()
     acc1[...] = acc1_in[...]
     back[...] = jnp.zeros(FIELD, f32)
+    copy.wait()
 
     @pl.when(flags[3] > 0)
     def _():
@@ -412,11 +429,11 @@
 
 
 def own_build_kernel(tab, s0, s1, lhs0, acc0_in, acc1_in, k01, acc0, acc1, tile, v0, v1, rhs):
-    base = 1 * T_SIZE
+    base = STRIPS
     acc0[...] = acc0_in[...]
     acc1[...] = acc1_in[...]
 
-    @pl.when(tab[base + T_LIVE] > 0)
+    @pl.when(tab[base, T_LIVE] > 0)
     def _():
         v0[...] = split2(s0[0:16, :])
         v1[...] = split2(s1[0:16, :])
@@ -430,21 +447,21 @@
     v0[...] = split2(w0[...])
     v1[...] = split2(w1[...])
 
-    @pl.when(tab[0 * T_SIZE + T_LIVE] > 0)
+    @pl.when(tab[0, T_LIVE] > 0)
     def _():
         diag_products(k00, v0, acc0)
-        extra_tiles(tab, 0 * T_SIZE, s0, s0, tile, v0, v0, acc0, acc0)
-
-    @pl.when(tab[1 * T_SIZE + T_LIVE] > 0)
-    def _():
-        to_owner(k01, tab, 1 * T_SIZE, v1, acc0)
-        to_partner(k01, tab, 1 * T_SIZE, v0, acc1)
-        extra_tiles(tab, 1 * T_SIZE, s0, s1, tile, v0, v1, acc0, acc1)
-
-    @pl.when(tab[2 * T_SIZE + T_LIVE] > 0)
+        extra_tiles(tab, 0, s0, s0, tile, v0, v0, acc0, acc0)
+
+    @pl.when(tab[8, T_LIVE] > 0)
+    def _():
+        to_owner(k01, tab, 8, v1, acc0)
+        to_partner(k01, tab, 8, v0, acc1)
+        extra_tiles(tab, 8, s0, s1, tile, v0, v1, acc0, acc1)
+
+    @pl.when(tab[16, T_LIVE] > 0)
     def _():
         diag_products(k11, v1, acc1)
-        extra_tiles(tab, 2 * T_SIZE, s1, s1, tile, v1, v1, acc1, acc1)
+        extra_tiles(tab, 16, s1, s1, tile, v1, v1, acc1, acc1)
 
 
 def inner(left, right):
@@ -456,7 +473,7 @@
     level, flags, tab, k12, s0, s1, halo, got_a, got_b, acc0, acc1, w0, w1, mom_in,
     n0, n1, send_a, send_b, mom, tile, v1, v2, acc, back
 ):
-    live = tab[T_LIVE] > 0
+    live = tab[0, T_LIVE] > 0
     acc[...] = acc1[...]
     if level > 1:
 
@@ -509,7 +526,7 @@
     n1[...] = s1[19:20, :] * w1[...] + acc1[...]
     n0[...] = s0[19:20, :] * w0[...] + (acc0[...] + arrived)
 
-    @pl.when(tab[T_LIVE] > 0)
+    @pl.when(tab[0, T_LIVE] > 0)
     def _():
         v2[...] = split2(jnp.where(flags[4] == 0, got_a[...], got_b[...]))
         to_owner(k12, tab, 0, v2, n1)
@@ -573,7 +590,20 @@
 
 
 def sum_over(value, axis):
-    return jnp.sum(lax.all_gather(value, axis), axis=0)
+    count = lax.axis_size(axis)
+    if count & (count - 1):
+        return lax.psum(value, axis)
+    step = 1
+    while step < count:
+        radix = min(4, count // step)
+        parts = [value] + [
+            lax.ppermute(value, axis, [(k, k ^ (m * step)) for k in range(count)]) for m in range(1, radix)
+        ]
+        while len(parts) > 1:
+            parts = [parts[m] + parts[m + 1] for m in range(0, len(parts), 2)]
+        value = parts[0]
+        step *= radix
+    return value
 
 
 def on_device(points, noise_var, probes, pair_list, counts):
@@ -582,20 +612,22 @@
     side = pltpu.VMEM((24, BLK), f32)
     left = pltpu.VMEM((BLK, N_FEATURES), bf16)
     right = pltpu.VMEM((N_FEATURES, BLK), bf16)
-    limits = jax.ShapeDtypeStruct((2 * SUBS,), f32)
+    table = pltpu.SMEM((STRIPS, SUB), jnp.int32)
+    tables = pltpu.SMEM((3 * STRIPS, SUB), jnp.int32)
     ranks = pltpu.VMEM((1, BLK), jnp.int32)
     far_space = pl.BlockSpec(memory_space=pltpu.HBM)
-    s0, s1, lhs0, lhs1, yb0, yb1, rank0, rank1, flags = call(
+    s0, s1, lhs0, lhs1, rank0, rank1, flags, tabb = call(
         sort_kernel,
-        (side, side, left, left, limits, limits, ranks, ranks, jax.ShapeDtypeStruct((5,), jnp.int32)),
+        (side, side, left, left, ranks, ranks, pltpu.SMEM((5,), jnp.int32), tables),
         [far_space] * 4 + [SMEM],
-        (VMEM,) * 4 + (SMEM,) * 2 + (VMEM,) * 2 + (SMEM,),
+        (VMEM,) * 6 + (SMEM,) * 2,
         [
             pltpu.VMEM(points.shape, f32),
             pltpu.VMEM(noise.shape, f32),
             pltpu.VMEM(probes.shape, f32),
             pltpu.SMEM(pair_list.shape[::-1], jnp.int32),
-            pltpu.VMEM((BLK, SUB), jnp.int32),
+            pltpu.VMEM((BLK, SUB), bf16),
+            pltpu.VMEM((3 * STRIPS, SUB), jnp.int32),
             pltpu.SemaphoreType.DMA((4,)),
         ],
         10**9,
@@ -605,24 +637,24 @@
     halos = swapped_both(s0, s0)
     off = pltpu.VMEM((STRIPS, STRIP, OFF_W), bf16)
     diag = pltpu.VMEM((STRIPS, STRIP, DIAG_W), bf16)
-    k00, k11, tabb, acc0, acc1 = call(
+    k00, k11, acc0, acc1 = call(
         diag_build_kernel,
-        (diag, diag, jax.ShapeDtypeStruct((3 * T_SIZE,), jnp.int32), field, field),
-        [SMEM] * 3 + [VMEM] * 4,
-        (VMEM, VMEM, SMEM, VMEM, VMEM),
+        (diag, diag, field, field),
+        [SMEM] + [VMEM] * 4,
+        (VMEM,) * 4,
         [TILE, SPLIT, SPLIT, right],
         3 * 10**9,
         "diag_build",
-    )(flags, yb0, yb1, s0, s1, lhs0, lhs1)
+    )(tabb, s0, s1, lhs0, lhs1)
     k12, tabc, acc1, back, halo = call(
         halo_build_kernel,
-        (off, jax.ShapeDtypeStruct((T_SIZE,), jnp.int32), field, field, side),
-        [SMEM] * 2 + [VMEM] * 5,
+        (off, table, field, field, side),
+        [SMEM] + [VMEM] * 5,
         (VMEM, SMEM, VMEM, VMEM, VMEM),
-        [pltpu.SMEM((2 * SUBS,), f32), TILE, SPLIT, SPLIT, right],
+        [pltpu.VMEM((STRIPS, SUB), jnp.int32), TILE, SPLIT, SPLIT, right, pltpu.SemaphoreType.DMA((1,))],
         3 * 10**9,
         "halo_build",
-    )(flags, yb1, s1, lhs1, *halos, acc1)
+    )(flags, s1, lhs1, *halos, acc1)
     got = swapped_both(back, back)
     k01, acc0, acc1 = call(
         own_build_kernel,

time: 95.8 us -> 69.8 us (0.73)
  the two profiles are of different devices: /device:TPU:0 before, /device:TPU:2 now
where the time goes in v5:
time: 69.8 us; the launch traced here: 68.8 us
  Pallas kernels  44.8 us (64%)
  starting transfers between devices  19.9 us (29%)
  waiting for transfers between devices  2.72 us (4%)
  between operations  1.47 us (2%)
    pallas_call x13, Pallas kernels, run(): pl.pallas_call(body, out_shape=outs, in_specs=ins, out_specs=out_specs, s...  44.8 us
    ppermute x6, starting transfers between devices, sum_over(): lax.ppermute(value, axis, [(k, k ^ m * step) for k in range(count)])  11.3 us
    ppermute x4, starting transfers between devices, swapped_both(): a = lax.ppermute(to_a, 'gx', [(k, k ^ 1) for k in range(count)])  5.89 us
    ppermute x4, starting transfers between devices, swapped_both(): lax.ppermute(to_b, 'gx', [(k, (k + 1 ^ 1) - 1) for k in range(1, count -...  2.67 us
    ppermute x6, waiting for transfers between devices, sum_over(): lax.ppermute(value, axis, [(k, k ^ m * step) for k in range(count)])  2.65 us
  transfers between devices with their start and end apart: 14, of which 1 were waited for; matrix products, arithmetic and copies ran while one was open for 0% of the time, Pallas kernels for 33%

profile of v5, /device:TPU:2, one launch (start us, length us, event | category | flops | bytes accessed | tf_op | source)
XLA Modules:
  0.0 68.8 jit_solution(6906285273632220418)
XLA Ops:
  1.3 10.1 %sort_blocks.1 = (f32[24,2048]{1,0:T(8,128)S(1)}, f32[24,2048]{1,0:T(8,128)S(1)}, bf16[2048,64]{1,0:T(8,128)(2,1)S(1)}, bf16[2048,64]{1,0:T(8,128)(2,1)S(1)}, s3...) custom-call(f32[3,4096]{1,0:T(4,128)} %pts_hbm.1, f32[1,4096]{1,0:T(1,128)} %bitcast.2, ...), custom_call_target="tpu_custom_call" | custom-call | flops 1000000000 | bytes 1048576 | tf_op jit(solution)/shard_map/sort_blocks/pallas_call | solution.py:379
  11.3 0.7 collective-permute-start.1
  12.0 2.9 %collective-permute-start = (f32[24,2048]{1,0:T(8,128)S(1)}, f32[24,2048]{1,0:T(8,128)S(1)}, u32[]{:S(2)}, u32[]{:S(2)}) collective-permute-start(f32[24,2048]{1,0:T(8,128)S(1)} %get-tuple-element.39.s0.w0), channel_id=1, source_target_pairs={{0,1},{1,0},{2,3},{3,2},{4,5},{5,4},{6,7},{7,6},{8,9},{9,8},{10,11... | collective-permute-start | bytes 589832 | tf_op jit(solution)/shard_map/ppermute | solution.py:587
  15.0 5.9 %diag_build.1 = (bf16[8,256,512]{2,1,0:T(8,128)(2,1)S(1)}, bf16[8,256,512]{2,1,0:T(8,128)(2,1)S(1)}, f32[16,2048]{1,0:T(8,128)S(1)}, f32[16,2048]{1,0:T(8,128)S(1)}) custom-call(s32[24,128]{1,0:T(8,128)S(4)} %get-tuple-element.41.tab, f32[24,2048]{1,0:T(8,128)S(1)} %get-tuple-element.39.s0.w0, f32[24,2048]{1,0:T(8,128)S(1)} %get-tuple-element.40.s1.w1, ...), custom_call_target="tpu_custom_call" | custom-call | flops 3000000000 | bytes 1048576 | tf_op jit(solution)/shard_map/diag_build/pallas_call | solution.py:379
  20.9 5.8 %halo_build.1 = (bf16[8,256,768]{2,1,0:T(8,128)(2,1)S(1)}, s32[8,128]{1,0:T(8,128)S(4)}, f32[16,2048]{1,0:T(8,128)S(1)}, f32[16,2048]{1,0:T(8,128)S(1)}, f32[24,2048]{1,0:T(8,128)S(1)}) custom-call(s32[5]{0:T(128)S(4)} %get-tuple-element.38.flags, f32[24,2048]{1,0:T(8,128)S(1)} %get-tuple-element.40.s1.w1, bf16[2048,64]{1,0:T(8,128)(2,1)S(1)} %get-tuple-element.43.lhs1, ...), custom_call_target="tpu_custom_call" | custom-call | flops 3000000000 | bytes 1048576 | tf_op jit(solution)/shard_map/halo_build/pallas_call | solution.py:379
  26.7 0.7 collective-permute-start.3
  27.4 2.1 %collective-permute-start.2 = (f32[16,2048]{1,0:T(8,128)S(1)}, f32[16,2048]{1,0:T(8,128)S(1)}, u32[]{:S(2)}, u32[]{:S(2)}) collective-permute-start(f32[16,2048]{1,0:T(8,128)S(1)} %get-tuple-element.53), channel_id=1, source_target_pairs={{0,1},{1,0},{2,3},{3,2},{4,5},{5,4},{6,7},{7,6},{8,9},{9,8},{10,11... | collective-permute-start | bytes 393224 | tf_op jit(solution)/shard_map/ppermute | solution.py:587
  29.5 4.6 %own_build.1 = (bf16[8,256,768]{2,1,0:T(8,128)(2,1)S(1)}, f32[16,2048]{1,0:T(8,128)S(1)}, f32[16,2048]{1,0:T(8,128)S(1)}) custom-call(s32[24,128]{1,0:T(8,128)S(4)} %get-tuple-element.41.tab, f32[24,2048]{1,0:T(8,128)S(1)} %get-tuple-element.39.s0.w0, f32[24,2048]{1,0:T(8,128)S(1)} %get-tuple-element.40.s1.w1, bf16[2048,64]{1,0:T(8,128)(2,1)S(1)} %get-tuple-element.42.lhs0, ...), custom_call_target="tpu_custom_call" | custom-call | flops 5000000000 | bytes 1048576 | tf_op jit(solution)/shard_map/own_build/pallas_call | solution.py:379
  34.2 1.6 %finish.2 = (f32[16,2048]{1,0:T(8,128)S(1)}, f32[16,2048]{1,0:T(8,128)S(1)}, f32[16,2048]{1,0:T(8,128)S(1)}, f32[16,2048]{1,0:T(8,128)S(1)}, f32[16,128]{1,0:T(8,128)S(1)}) custom-call(s32[5]{0:T(128)S(4)} %get-tuple-element.38.flags, s32[8,128]{1,0:T(8,128)S(4)} %get-tuple-element.50.tab, bf16[8,256,768]{2,1,0:T(8,128)(2,1)S(1)} %get-tuple-element.51.k12, ...), custom_call_target="tpu_custom_call" | custom-call | flops 1000000000 | bytes 1048576 | tf_op jit(solution)/shard_map/finish/pallas_call | solution.py:379
  35.8 0.7 collective-permute-start.5
  36.5 3.9 %own_apply.2 = (f32[16,2048]{1,0:T(8,128)S(1)}, f32[16,2048]{1,0:T(8,128)S(1)}) custom-call(s32[24,128]{1,0:T(8,128)S(4)} %get-tuple-element.41.tab, bf16[8,256,512]{2,1,0:T(8,128)(2,1)S(1)} %get-tuple-element.44.k00, bf16[8,256,768]{2,1,0:T(8,128)(2,1)S(1)} %get-tuple-element.48.k01, bf16[8,256,512]{2,1,0:T(8,128)(2,1)S(1)} %get-tuple-element.49.k11, ...), custom_call_target="tpu_custom_call" | custom-call | flops 2000000000 | bytes 1048576 | tf_op jit(solution)/shard_map/own_apply/pallas_call | solution.py:379
  40.5 3.3 %finish.3 = (f32[16,2048]{1,0:T(8,128)S(1)}, f32[16,2048]{1,0:T(8,128)S(1)}, f32[16,2048]{1,0:T(8,128)S(1)}, f32[16,2048]{1,0:T(8,128)S(1)}, f32[16,128]{1,0:T(8,128)S(1)}) custom-call(s32[5]{0:T(128)S(4)} %get-tuple-element.38.flags, s32[8,128]{1,0:T(8,128)S(4)} %get-tuple-element.50.tab, bf16[8,256,768]{2,1,0:T(8,128)(2,1)S(1)} %get-tuple-element.51.k12, ...), custom_call_target="tpu_custom_call" | custom-call | flops 1000000000 | bytes 1048576 | tf_op jit(solution)/shard_map/finish/pallas_call | solution.py:379
  43.7 0.8 %collective-permute-start.6 = (f32[16,2048]{1,0:T(8,128)S(1)}, f32[16,2048]{1,0:T(8,128)S(1)}, u32[]{:S(2)}, u32[]{:S(2)}) collective-permute-start(f32[16,2048]{1,0:T(8,128)S(1)} %get-tuple-element.67), channel_id=1, source_target_pairs={{0,1},{1,0},{2,3},{3,2},{4,5},{5,4},{6,7},{7,6},{8,9},{9,8},{10,11... | collective-permute-start | bytes 393224 | tf_op jit(solution)/shard_map/ppermute | solution.py:587
  44.5 0.7 collective-permute-start.7
  45.1 3.9 %own_apply.3 = (f32[16,2048]{1,0:T(8,128)S(1)}, f32[16,2048]{1,0:T(8,128)S(1)}) custom-call(s32[24,128]{1,0:T(8,128)S(4)} %get-tuple-element.41.tab, bf16[8,256,512]{2,1,0:T(8,128)(2,1)S(1)} %get-tuple-element.44.k00, bf16[8,256,768]{2,1,0:T(8,128)(2,1)S(1)} %get-tuple-element.48.k01, bf16[8,256,512]{2,1,0:T(8,128)(2,1)S(1)} %get-tuple-element.49.k11, ...), custom_call_target="tpu_custom_call" | custom-call | flops 2000000000 | bytes 1048576 | tf_op jit(solution)/shard_map/own_apply/pallas_call | solution.py:379
  49.3 5.9 %collective-permute-start.10 = (f32[16,128]{1,0:T(8,128)S(1)}, f32[16,128]{1,0:T(8,128)S(1)}, u32[]{:S(2)}, u32[]{:S(2)}) collective-permute-start(f32[16,128]{1,0:T(8,128)S(1)} %moment.1), channel_id=1, source_target_pairs={{0,3},{1,2},{2,1},{3,0},{4,7},{5,6},{6,5},{7,4},{8,11},{9,10},{10,... | collective-permute-start | bytes 24584 | tf_op jit(solution)/shard_map/ppermute | solution.py:600
  55.2 0.8 %collective-permute-start.9 = (f32[16,128]{1,0:T(8,128)S(1)}, f32[16,128]{1,0:T(8,128)S(1)}, u32[]{:S(2)}, u32[]{:S(2)}) collective-permute-start(f32[16,128]{1,0:T(8,128)S(1)} %moment.1), channel_id=1, source_target_pairs={{0,2},{1,3},{2,0},{3,1},{4,6},{5,7},{6,4},{7,5},{8,10},{9,11},{10,... | collective-permute-start | bytes 24584 | tf_op jit(solution)/shard_map/ppermute | solution.py:600
  56.1 1.9 %last.1 = (f32[16,2048]{1,0:T(8,128)S(1)}, f32[16,2048]{1,0:T(8,128)S(1)}) custom-call(s32[5]{0:T(128)S(4)} %get-tuple-element.38.flags, s32[8,128]{1,0:T(8,128)S(4)} %get-tuple-element.50.tab, bf16[8,256,768]{2,1,0:T(8,128)(2,1)S(1)} %get-tuple-element.51.k12, f32[24,2048]{1,0:T(8,128)S(1)} %get-tuple-element.39.s0.w0, ...), custom_call_target="tpu_custom_call" | custom-call | flops 1000000000 | bytes 1048576 | tf_op jit(solution)/shard_map/last/pallas_call | solution.py:379
  58.0 1.3 %unsort.2.u0 = f32[48,2048]{1,0:T(8,128)S(1)} custom-call(s32[1,2048]{1,0:T(1,128)S(1)} %get-tuple-element.70.rank_ref, f32[16,2048]{1,0:T(8,128)S(1)} %get-tuple-element.58.w0.wa, f32[16,2048]{1,0:T(8,128)S(1)} %get-tuple-element.63.w0.wb, f32[16,2048]{1,0:T(8,128)S(1)} %get-tuple-element.71.wc), custom_call_target="tpu_custom_call" | custom-call | flops 805306368 | bytes 1048576 | tf_op jit(solution)/shard_map/unsort/pallas_call | solution.py:379
  59.3 3.9 %collective-permute-start.13 = (f32[16,128]{1,0:T(8,128)S(1)}, f32[16,128]{1,0:T(8,128)S(1)}, u32[]{:S(2)}, u32[]{:S(2)}) collective-permute-start(f32[16,128]{1,0:T(8,128)S(1)} %add_add_fusion.1), channel_id=1, source_target_pairs={{0,12},{1,13},{2,14},{3,15},{4,8},{5,9},{6,10},{7,11},{8,4},{9,5},... | collective-permute-start | bytes 24584 | tf_op jit(solution)/shard_map/ppermute | solution.py:600
  63.2 0.6 collective-permute-start.11
  63.9 1.3 %unsort.3.u1 = f32[48,2048]{1,0:T(8,128)S(1)} custom-call(s32[1,2048]{1,0:T(1,128)S(1)} %get-tuple-element.72.rank_ref, f32[16,2048]{1,0:T(8,128)S(1)} %get-tuple-element.59.w1.wa, f32[16,2048]{1,0:T(8,128)S(1)} %get-tuple-element.64.w1.wb, f32[16,2048]{1,0:T(8,128)S(1)} %get-tuple-element.73.wc), custom_call_target="tpu_custom_call" | custom-call | flops 805306368 | bytes 1048576 | tf_op jit(solution)/shard_map/unsort/pallas_call | solution.py:379
  65.2 2.6 %collective-permute-done.12 = f32[16,128]{1,0:T(8,128)S(1)} collective-permute-done((f32[16,128]{1,0:T(8,128)S(1)}, f32[16,128]{1,0:T(8,128)S(1)}, u32[]{:S(2)}, u32[]{:S(2)}) %collective-permute-start.12) | collective-permute-done | bytes 8224 | tf_op jit(solution)/shard_map/ppermute | solution.py:600
  67.8 1.0 %combine.1 = (f32[16,4096]{1,0:T(8,128)}, f32[16,4096]{1,0:T(8,128)}) custom-call(f32[16,128]{1,0:T(8,128)S(1)} %add_add_fusion.mom, f32[16,4096]{1,0:T(8,128)S(1)} %copy-done, f32[48,2048]{1,0:T(8,128)S(1)} %unsort.2.u0, f32[48,2048]{1,0:T(8,128)S(1)} %unsort.3.u1), custom_call_target="tpu_custom_call" | custom-call | flops 1000000 | bytes 1048576 | tf_op jit(solution)/shard_map/combine/pallas_call | solution.py:379
  (22 shorter events, 0.4 us)
Async XLA Ops:
  11.3 9.5 %collective-permute-start.1 = (f32[24,2048]{1,0:T(8,128)S(1)}, f32[24,2048]{1,0:T(8,128)S(1)}, u32[]{:S(2)}, u32[]{:S(2)}) collective-permute-start(f32[24,2048]{1,0:T(8,128)S(1)} %get-tuple-element.39.s0.w0), channel_id=1, source_target_pairs={{1,2},{2,1},{3,4},{4,3},{5,6},{6,5},{7,8},{8,7},{9,10},{10,9},{11,... | collective-permute-start | bytes 589832 | tf_op jit(solution)/shard_map/ppermute | solution.py:588
  12.0 8.9 %collective-permute-start = (f32[24,2048]{1,0:T(8,128)S(1)}, f32[24,2048]{1,0:T(8,128)S(1)}, u32[]{:S(2)}, u32[]{:S(2)}) collective-permute-start(f32[24,2048]{1,0:T(8,128)S(1)} %get-tuple-element.39.s0.w0), channel_id=1, source_target_pairs={{0,1},{1,0},{2,3},{3,2},{4,5},{5,4},{6,7},{7,6},{8,9},{9,8},{10,11... | collective-permute-start | bytes 589832 | tf_op jit(solution)/shard_map/ppermute | solution.py:587
  26.7 7.4 %collective-permute-start.3 = (f32[16,2048]{1,0:T(8,128)S(1)}, f32[16,2048]{1,0:T(8,128)S(1)}, u32[]{:S(2)}, u32[]{:S(2)}) collective-permute-start(f32[16,2048]{1,0:T(8,128)S(1)} %get-tuple-element.53), channel_id=1, source_target_pairs={{1,2},{2,1},{3,4},{4,3},{5,6},{6,5},{7,8},{8,7},{9,10},{10,9},{11,... | collective-permute-start | bytes 393224 | tf_op jit(solution)/shard_map/ppermute | solution.py:588
  27.4 6.7 %collective-permute-start.2 = (f32[16,2048]{1,0:T(8,128)S(1)}, f32[16,2048]{1,0:T(8,128)S(1)}, u32[]{:S(2)}, u32[]{:S(2)}) collective-permute-start(f32[16,2048]{1,0:T(8,128)S(1)} %get-tuple-element.53), channel_id=1, source_target_pairs={{0,1},{1,0},{2,3},{3,2},{4,5},{5,4},{6,7},{7,6},{8,9},{9,8},{10,11... | collective-permute-start | bytes 393224 | tf_op jit(solution)/shard_map/ppermute | solution.py:587
  35.7 4.7 %collective-permute-start.4 = (f32[16,2048]{1,0:T(8,128)S(1)}, f32[16,2048]{1,0:T(8,128)S(1)}, u32[]{:S(2)}, u32[]{:S(2)}) collective-permute-start(f32[16,2048]{1,0:T(8,128)S(1)} %get-tuple-element.56), channel_id=1, source_target_pairs={{0,1},{1,0},{2,3},{3,2},{4,5},{5,4},{6,7},{7,6},{8,9},{9,8},{10,11... | collective-permute-start | bytes 393224 | tf_op jit(solution)/shard_map/ppermute | solution.py:587
  35.8 4.6 %collective-permute-start.5 = (f32[16,2048]{1,0:T(8,128)S(1)}, f32[16,2048]{1,0:T(8,128)S(1)}, u32[]{:S(2)}, u32[]{:S(2)}) collective-permute-start(f32[16,2048]{1,0:T(8,128)S(1)} %get-tuple-element.57), channel_id=1, source_target_pairs={{1,2},{2,1},{3,4},{4,3},{5,6},{6,5},{7,8},{8,7},{9,10},{10,9},{11,... | collective-permute-start | bytes 393224 | tf_op jit(solution)/shard_map/ppermute | solution.py:588
  43.7 5.4 %collective-permute-start.6 = (f32[16,2048]{1,0:T(8,128)S(1)}, f32[16,2048]{1,0:T(8,128)S(1)}, u32[]{:S(2)}, u32[]{:S(2)}) collective-permute-start(f32[16,2048]{1,0:T(8,128)S(1)} %get-tuple-element.67), channel_id=1, source_target_pairs={{0,1},{1,0},{2,3},{3,2},{4,5},{5,4},{6,7},{7,6},{8,9},{9,8},{10,11... | collective-permute-start | bytes 393224 | tf_op jit(solution)/shard_map/ppermute | solution.py:587
  44.5 4.6 %collective-permute-start.7 = (f32[16,2048]{1,0:T(8,128)S(1)}, f32[16,2048]{1,0:T(8,128)S(1)}, u32[]{:S(2)}, u32[]{:S(2)}) collective-permute-start(f32[16,2048]{1,0:T(8,128)S(1)} %get-tuple-element.68), channel_id=1, source_target_pairs={{1,2},{2,1},{3,4},{4,3},{5,6},{6,5},{7,8},{8,7},{9,10},{10,9},{11,... | collective-permute-start | bytes 393224 | tf_op jit(solution)/shard_map/ppermute | solution.py:588
  49.3 10.0 %collective-permute-start.10 = (f32[16,128]{1,0:T(8,128)S(1)}, f32[16,128]{1,0:T(8,128)S(1)}, u32[]{:S(2)}, u32[]{:S(2)}) collective-permute-start(f32[16,128]{1,0:T(8,128)S(1)} %moment.1), channel_id=1, source_target_pairs={{0,3},{1,2},{2,1},{3,0},{4,7},{5,6},{6,5},{7,4},{8,11},{9,10},{10,... | collective-permute-start | bytes 24584 | tf_op jit(solution)/shard_map/ppermute | solution.py:600
  55.2 4.1 %collective-permute-start.9 = (f32[16,128]{1,0:T(8,128)S(1)}, f32[16,128]{1,0:T(8,128)S(1)}, u32[]{:S(2)}, u32[]{:S(2)}) collective-permute-start(f32[16,128]{1,0:T(8,128)S(1)} %moment.1), channel_id=1, source_target_pairs={{0,2},{1,3},{2,0},{3,1},{4,6},{5,7},{6,4},{7,5},{8,10},{9,11},{10,... | collective-permute-start | bytes 24584 | tf_op jit(solution)/shard_map/ppermute | solution.py:600
  56.0 3.3 %collective-permute-start.8 = (f32[16,128]{1,0:T(8,128)S(1)}, f32[16,128]{1,0:T(8,128)S(1)}, u32[]{:S(2)}, u32[]{:S(2)}) collective-permute-start(f32[16,128]{1,0:T(8,128)S(1)} %moment.1), channel_id=1, source_target_pairs={{0,1},{1,0},{2,3},{3,2},{4,5},{5,4},{6,7},{7,6},{8,9},{9,8},{10,11... | collective-permute-start | bytes 24584 | tf_op jit(solution)/shard_map/ppermute | solution.py:600
  58.0 9.8 %copy-start = (f32[16,4096]{1,0:T(8,128)S(1)}, f32[16,4096]{1,0:T(8,128)}, u32[]{:S(2)}) copy-start(f32[16,4096]{1,0:T(8,128)} %probes.1) | copy-start | bytes 786436
  59.3 5.8 %collective-permute-start.13 = (f32[16,128]{1,0:T(8,128)S(1)}, f32[16,128]{1,0:T(8,128)S(1)}, u32[]{:S(2)}, u32[]{:S(2)}) collective-permute-start(f32[16,128]{1,0:T(8,128)S(1)} %add_add_fusion.1), channel_id=1, source_target_pairs={{0,12},{1,13},{2,14},{3,15},{4,8},{5,9},{6,10},{7,11},{8,4},{9,5},... | collective-permute-start | bytes 24584 | tf_op jit(solution)/shard_map/ppermute | solution.py:600
  63.2 4.5 %collective-permute-start.12 = (f32[16,128]{1,0:T(8,128)S(1)}, f32[16,128]{1,0:T(8,128)S(1)}, u32[]{:S(2)}, u32[]{:S(2)}) collective-permute-start(f32[16,128]{1,0:T(8,128)S(1)} %add_add_fusion.1), channel_id=1, source_target_pairs={{0,8},{1,9},{2,10},{3,11},{4,12},{5,13},{6,14},{7,15},{8,0},{9,1},... | collective-permute-start | bytes 24584 | tf_op jit(solution)/shard_map/ppermute | solution.py:600
  63.2 4.5 %collective-permute-start.11 = (f32[16,128]{1,0:T(8,128)S(1)}, f32[16,128]{1,0:T(8,128)S(1)}, u32[]{:S(2)}, u32[]{:S(2)}) collective-permute-start(f32[16,128]{1,0:T(8,128)S(1)} %add_add_fusion.1), channel_id=1, source_target_pairs={{0,4},{1,5},{2,6},{3,7},{4,0},{5,1},{6,2},{7,3},{8,12},{9,13},{10,... | collective-permute-start | bytes 24584 | tf_op jit(solution)/shard_map/ppermute | solution.py:600

commit v6 on v5

--- a/solution.py
+++ b/solution.py
@@ -73,15 +73,21 @@
     return jnp.where(group == g, within, -1).astype(f32).astype(bf16)
 
 
+def turned(value):
+    shape = (STRIP, STRIP)
+    same = lax.broadcasted_iota(jnp.int32, shape, 0) == lax.broadcasted_iota(jnp.int32, shape, 1)
+    return nt(jnp.where(same, 1.0, 0.0).astype(bf16), value).astype(bf16)
+
+
 def rank_of(y_row, key_ref):
     low = jnp.min(y_row, axis=1, keepdims=True)
     high = jnp.max(y_row, axis=1, keepdims=True)
     scale = 255.0 / jnp.maximum(high - low, 1e-6)
     key = jnp.clip(jnp.floor((y_row - low) * scale), 0.0, 255.0)
-    for c in range(SUBS):
-        here = slice(c * SUB, (c + 1) * SUB)
-        key_ref[here, :] = jnp.broadcast_to(key[:, here], (SUB, SUB)).T.astype(bf16)
     strict = key.astype(bf16)
+    for c in range(STRIPS):
+        here = slice(c * STRIP, (c + 1) * STRIP)
+        key_ref[here, :] = turned(jnp.broadcast_to(key[:, here], (SUB, STRIP)).astype(bf16))
     loose = (key + 1.0).astype(bf16)
     ones = jnp.ones((16, STRIP), bf16)
     one = jnp.ones((STRIP, SUB), bf16)
@@ -177,7 +183,9 @@
     for local in range(2):
         for ahead in range(2):
             flags[2 * local + ahead] = live_flag(pair, count, local, ahead)
-    flags[4] = jnp.bitwise_and(lax.shift_right_logical(pair[0, 0], 1), 1)
+    position = lax.shift_right_logical(pair[0, 0], 1)
+    flags[4] = jnp.bitwise_and(position, 1)
+    flags[5] = jnp.where(position > 0, 1, 0)
     place = places()
     for blk, (out_ref, rank_ref) in enumerate(((s0, rank0), (s1, rank1))):
         cols = slice(blk * BLK, (blk + 1) * BLK)
@@ -206,9 +214,10 @@
     copy.start()
     for side, lhs_ref in ((s0, lhs0), (s1, lhs1)):
         rows, _ = features(offset_of(side, side), True)
-        for c in range(SUBS):
-            here = slice(c * SUB, (c + 1) * SUB)
-            lhs_ref[here, :] = rows[:, here].T.astype(bf16)
+        rows = rows.astype(bf16)
+        for c in range(STRIPS):
+            here = slice(c * STRIP, (c + 1) * STRIP)
+            lhs_ref[here, :] = turned(rows[:, here])
     copy.wait()
 
 
@@ -296,6 +305,8 @@
         to_owner(k_ref, tab_ref, base, v_col, acc_row)
         to_partner(k_ref, tab_ref, base, v_row, acc_col)
 
+    return near, lhs, rhs
+
 
 def diag_pair(k_ref, lhs, rhs, side, v, acc):
     near = right_features(rhs, side, side)
@@ -344,27 +355,51 @@
         diag_strip(k_ref, i, v_ref, acc_ref)
 
 
-def extra_tiles(tab_ref, base, row_side, col_side, tile_ref, v_row, v_col, acc_row, acc_col):
+def extra_tiles(
+    tab_ref, base, row_side, col_side, tile_ref, v_row, v_col, acc_row, acc_col, kept=None, fill=None
+):
     @pl.when(tab_ref[base, T_EXTRA] > 0)
     def _():
         def strip(i, carry):
             here = pl.ds(pl.multiple_of(i * STRIP, STRIP), STRIP)
+            first = tab_ref[base + i, T_START] + OFF_SUBS
 
             def tile(j, carry):
                 col_at = pl.multiple_of(j * SUB, SUB)
                 there = pl.ds(col_at, SUB)
-                for g in range(STRIP // SUB):
-                    row_at = pl.multiple_of(i * STRIP + g * SUB, SUB)
-                    tile_ref[g * SUB : (g + 1) * SUB, :] = tile_by_difference(row_side, row_at, col_side, col_at)
+
+                def by_difference():
+                    for g in range(STRIP // SUB):
+                        row_at = pl.multiple_of(i * STRIP + g * SUB, SUB)
+                        tile_ref[g * SUB : (g + 1) * SUB, :] = tile_by_difference(row_side, row_at, col_side, col_at)
+
+                if kept is None:
+                    by_difference()
+                elif fill is None:
+                    pl.when(j > first)(by_difference)
+
+                    @pl.when(j == first)
+                    def _():
+                        tile_ref[...] = kept[i]
+                else:
+                    near, lhs, rhs = fill
+                    pl.when(jnp.logical_not(near))(by_difference)
+
+                    @pl.when(near)
+                    def _():
+                        tile_ref[...] = kernel_values(nn(lhs[here, :], rhs[:, there]))
+
+                    @pl.when(j == first)
+                    def _():
+                        kept[i] = tile_ref[...]
+
                 if acc_row is not None:
                     acc_row[:, here] += halves(nt(v_col[:, there], tile_ref[...]))
                 if acc_col is not None:
                     acc_col[:, there] += halves(nn(v_row[:, here], tile_ref[...]))
                 return carry
 
-            return lax.fori_loop(
-                tab_ref[base + i, T_START] + OFF_SUBS, tab_ref[base + i, T_END], tile, carry
-            )
+            return lax.fori_loop(first, tab_ref[base + i, T_END], tile, carry)
 
         lax.fori_loop(0, STRIPS, strip, 0)
 
@@ -410,7 +445,7 @@
 
 
 def halo_build_kernel(
-    flags, s1, lhs1, got_a, got_b, acc1_in, k12, tab, acc1, back, halo, plan_ref, tile, v1, v2, rhs, sem
+    flags, s1, lhs1, got_a, got_b, acc1_in, k12, x12, tab, acc1, back, halo, plan_ref, tile, v1, v2, rhs, sem
 ):
     halo[...] = jnp.where(flags[4] == 0, got_a[...], got_b[...])
     plan_ref[...] = plan(s1, halo, flags[3], False)
@@ -424,11 +459,11 @@
     def _():
         v1[...] = split2(s1[0:16, :])
         v2[...] = split2(halo[0:16, :])
-        off_pair(k12, tab, 0, lhs1, rhs, s1, halo, v1, v2, acc1, back)
-        extra_tiles(tab, 0, s1, halo, tile, v1, v2, acc1, back)
-
-
-def own_build_kernel(tab, s0, s1, lhs0, acc0_in, acc1_in, k01, acc0, acc1, tile, v0, v1, rhs):
+        fill = off_pair(k12, tab, 0, lhs1, rhs, s1, halo, v1, v2, acc1, back)
+        extra_tiles(tab, 0, s1, halo, tile, v1, v2, acc1, back, x12, fill)
+
+
+def own_build_kernel(tab, s0, s1, lhs0, acc0_in, acc1_in, k01, x01, acc0, acc1, tile, v0, v1, rhs):
     base = STRIPS
     acc0[...] = acc0_in[...]
     acc1[...] = acc1_in[...]
@@ -437,11 +472,11 @@
     def _():
         v0[...] = split2(s0[0:16, :])
         v1[...] = split2(s1[0:16, :])
-        off_pair(k01, tab, base, lhs0, rhs, s0, s1, v0, v1, acc0, acc1)
-        extra_tiles(tab, base, s0, s1, tile, v0, v1, acc0, acc1)
-
-
-def own_apply_kernel(tab, k00, k01, k11, s0, s1, w0, w1, acc0, acc1, tile, v0, v1):
+        fill = off_pair(k01, tab, base, lhs0, rhs, s0, s1, v0, v1, acc0, acc1)
+        extra_tiles(tab, base, s0, s1, tile, v0, v1, acc0, acc1, x01, fill)
+
+
+def own_apply_kernel(tab, k00, k01, x01, k11, s0, s1, w0, w1, acc0, acc1, tile, v0, v1):
     acc0[...] = jnp.zeros(FIELD, f32)
     acc1[...] = jnp.zeros(FIELD, f32)
     v0[...] = split2(w0[...])
@@ -456,12 +491,17 @@
     def _():
         to_owner(k01, tab, 8, v1, acc0)
         to_partner(k01, tab, 8, v0, acc1)
-        extra_tiles(tab, 8, s0, s1, tile, v0, v1, acc0, acc1)
+        extra_tiles(tab, 8, s0, s1, tile, v0, v1, acc0, acc1, x01)
 
     @pl.when(tab[16, T_LIVE] > 0)
     def _():
         diag_products(k11, v1, acc1)
         extra_tiles(tab, 16, s1, s1, tile, v1, v1, acc1, acc1)
+
+
+def from_left(flags, got_a, got_b):
+    arrived = jnp.where(flags[4] == 0, got_b[...], got_a[...])
+    return jnp.where(flags[5] > 0, arrived, 0.0)
 
 
 def inner(left, right):
@@ -470,7 +510,7 @@
 
 
 def finish_kernel(
-    level, flags, tab, k12, s0, s1, halo, got_a, got_b, acc0, acc1, w0, w1, mom_in,
+    level, flags, tab, k12, x12, s0, s1, halo, got_a, got_b, acc0, acc1, w0, w1, mom_in,
     n0, n1, send_a, send_b, mom, tile, v1, v2, acc, back
 ):
     live = tab[0, T_LIVE] > 0
@@ -481,7 +521,7 @@
         def _():
             v2[...] = split2(jnp.where(flags[4] == 0, got_a[...], got_b[...]))
             to_owner(k12, tab, 0, v2, acc)
-            extra_tiles(tab, 0, s1, halo, tile, None, v2, acc, None)
+            extra_tiles(tab, 0, s1, halo, tile, None, v2, acc, None, x12)
 
     before0 = w0[0:16, :]
     before1 = w1[0:16, :]
@@ -493,9 +533,9 @@
     def _():
         v1[...] = split2(next1)
         to_partner(k12, tab, 0, v1, back)
-        extra_tiles(tab, 0, s1, halo, tile, v1, None, None, back)
-
-    arrived = jnp.where(flags[4] == 0, got_b[...], got_a[...])
+        extra_tiles(tab, 0, s1, halo, tile, v1, None, None, back, x12)
+
+    arrived = from_left(flags, got_a, got_b)
     next0 = s0[19:20, :] * before0 + (acc0[...] + arrived)
     n0[...] = next0
     send_a[...] = jnp.where(flags[4] == 0, back[...], next0)
@@ -515,14 +555,14 @@
     lane = lax.broadcasted_iota(jnp.int32, (N_PROBES, SUB), 1)
     one = w0[...]
     two = w1[...]
-    arrived = jnp.where(flags[4] == 0, got_b[...], got_a[...])
+    arrived = from_left(flags, got_a, got_b)
     cross = inner(one, s0[19:20, :] * one + (acc0[...] + 2.0 * arrived))
     cross = cross + inner(two, s1[19:20, :] * two + acc1[...])
     mom[...] = mom_in[...] + jnp.where(lane == 5, cross, 0.0)
 
 
-def last_kernel(flags, tab, k12, s0, s1, halo, got_a, got_b, acc0, acc1, w0, w1, n0, n1, tile, v2):
-    arrived = jnp.where(flags[4] == 0, got_b[...], got_a[...])
+def last_kernel(flags, tab, k12, x12, s0, s1, halo, got_a, got_b, acc0, acc1, w0, w1, n0, n1, tile, v2):
+    arrived = from_left(flags, got_a, got_b)
     n1[...] = s1[19:20, :] * w1[...] + acc1[...]
     n0[...] = s0[19:20, :] * w0[...] + (acc0[...] + arrived)
 
@@ -530,7 +570,7 @@
     def _():
         v2[...] = split2(jnp.where(flags[4] == 0, got_a[...], got_b[...]))
         to_owner(k12, tab, 0, v2, n1)
-        extra_tiles(tab, 0, s1, halo, tile, None, v2, n1, None)
+        extra_tiles(tab, 0, s1, halo, tile, None, v2, n1, None, x12)
 
 
 def unsort_kernel(rank_ref, wa, wb, wc, out):
@@ -585,7 +625,8 @@
 def swapped_both(to_a, to_b):
     count = lax.axis_size("gx")
     a = lax.ppermute(to_a, "gx", [(k, k ^ 1) for k in range(count)])
-    b = lax.ppermute(to_b, "gx", [(k, ((k + 1) ^ 1) - 1) for k in range(1, count - 1)])
+    ends = [(0, 0), (count - 1, count - 1)]
+    b = lax.ppermute(to_b, "gx", ends + [(k, ((k + 1) ^ 1) - 1) for k in range(1, count - 1)])
     return a, b
 
 
@@ -618,7 +659,7 @@
     far_space = pl.BlockSpec(memory_space=pltpu.HBM)
     s0, s1, lhs0, lhs1, rank0, rank1, flags, tabb = call(
         sort_kernel,
-        (side, side, left, left, ranks, ranks, pltpu.SMEM((5,), jnp.int32), tables),
+        (side, side, left, left, ranks, ranks, pltpu.SMEM((6,), jnp.int32), tables),
         [far_space] * 4 + [SMEM],
         (VMEM,) * 6 + (SMEM,) * 2,
         [
@@ -637,6 +678,7 @@
     halos = swapped_both(s0, s0)
     off = pltpu.VMEM((STRIPS, STRIP, OFF_W), bf16)
     diag = pltpu.VMEM((STRIPS, STRIP, DIAG_W), bf16)
+    outside = pltpu.VMEM((STRIPS, STRIP, SUB), bf16)
     k00, k11, acc0, acc1 = call(
         diag_build_kernel,
         (diag, diag, field, field),
@@ -646,21 +688,21 @@
         3 * 10**9,
         "diag_build",
     )(tabb, s0, s1, lhs0, lhs1)
-    k12, tabc, acc1, back, halo = call(
+    k12, x12, tabc, acc1, back, halo = call(
         halo_build_kernel,
-        (off, table, field, field, side),
+        (off, outside, table, field, field, side),
         [SMEM] + [VMEM] * 5,
-        (VMEM, SMEM, VMEM, VMEM, VMEM),
+        (VMEM, VMEM, SMEM, VMEM, VMEM, VMEM),
         [pltpu.VMEM((STRIPS, SUB), jnp.int32), TILE, SPLIT, SPLIT, right, pltpu.SemaphoreType.DMA((1,))],
         3 * 10**9,
         "halo_build",
     )(flags, s1, lhs1, *halos, acc1)
     got = swapped_both(back, back)
-    k01, acc0, acc1 = call(
+    k01, x01, acc0, acc1 = call(
         own_build_kernel,
-        (off, field, field),
+        (off, outside, field, field),
         [SMEM] + [VMEM] * 5,
-        (VMEM,) * 3,
+        (VMEM,) * 4,
         [TILE, SPLIT, SPLIT, right],
         5 * 10**9,
         "own_build",
@@ -674,30 +716,30 @@
         w0, w1, send_a, send_b, mom = call(
             functools.partial(finish_kernel, level),
             (field,) * 4 + (moments,),
-            [SMEM] * 2 + [VMEM] * 11,
+            [SMEM] * 2 + [VMEM] * 12,
             (VMEM,) * 5,
             [TILE, SPLIT, SPLIT, pltpu.VMEM(FIELD, f32), pltpu.VMEM(FIELD, f32)],
             10**9,
             "finish",
-        )(flags, tabc, k12, s0, s1, halo, *got, acc0, acc1, w0, w1, mom)
+        )(flags, tabc, k12, x12, s0, s1, halo, *got, acc0, acc1, w0, w1, mom)
         kept.append((w0, w1))
         got = swapped_both(send_a, send_b)
         acc0, acc1 = call(
             own_apply_kernel,
             (field, field),
-            [SMEM] + [VMEM] * 7,
+            [SMEM] + [VMEM] * 8,
             (VMEM, VMEM),
             [TILE, SPLIT, SPLIT],
             2 * 10**9,
             "own_apply",
-        )(tabb, k00, k01, k11, s0, s1, w0, w1)
+        )(tabb, k00, k01, x01, k11, s0, s1, w0, w1)
     mom = call(moment_kernel, moments, [SMEM] + [VMEM] * 9, VMEM, [], 10**7, "moment")(
         flags, s0, s1, acc0, acc1, *got, w0, w1, mom
     )
     total = sum_over(mom, "gx")
     kept.append(
-        call(last_kernel, (field, field), [SMEM] * 2 + [VMEM] * 10, (VMEM, VMEM), [TILE, SPLIT], 10**9, "last")(
-            flags, tabc, k12, s0, s1, halo, *got, acc0, acc1, w0, w1
+        call(last_kernel, (field, field), [SMEM] * 2 + [VMEM] * 11, (VMEM, VMEM), [TILE, SPLIT], 10**9, "last")(
+            flags, tabc, k12, x12, s0, s1, halo, *got, acc0, acc1, w0, w1
         )
     )
     given = []

time: 69.8 us -> 68 us (0.974)
  the two profiles are of different devices: /device:TPU:2 before, /device:TPU:0 now
where the time goes in v6:
time: 68 us; the launch traced here: 67.6 us
  Pallas kernels  40.1 us (59%)
  starting transfers between devices  24.1 us (35%)
  waiting for transfers between devices  2.01 us (3%)
  between operations  1.44 us (2%)
    pallas_call x13, Pallas kernels, run(): pl.pallas_call(body, out_shape=outs, in_specs=ins, out_specs=out_specs, s...  40.1 us
    ppermute x6, starting transfers between devices, sum_over(): lax.ppermute(value, axis, [(k, k ^ m * step) for k in range(count)])  12 us
    ppermute x4, starting transfers between devices, swapped_both(): a = lax.ppermute(to_a, 'gx', [(k, k ^ 1) for k in range(count)])  9.47 us
    ppermute x4, starting transfers between devices, swapped_both(): lax.ppermute(to_b, 'gx', ends + [(k, (k + 1 ^ 1) - 1) for k in range(1, c...  2.67 us
    ppermute x6, waiting for transfers between devices, sum_over(): lax.ppermute(value, axis, [(k, k ^ m * step) for k in range(count)])  1.95 us
  transfers between devices with their start and end apart: 14, of which 3 were waited for; matrix products, arithmetic and copies ran while one was open for 0% of the time, Pallas kernels for 30%

profile of v6, /device:TPU:0, one launch (start us, length us, event | category | flops | bytes accessed | tf_op | source)
XLA Modules:
  0.0 67.6 jit_solution(13802684594275981961)
XLA Ops:
  1.3 10.5 %sort_blocks.1 = (f32[24,2048]{1,0:T(8,128)S(1)}, f32[24,2048]{1,0:T(8,128)S(1)}, bf16[2048,64]{1,0:T(8,128)(2,1)S(1)}, bf16[2048,64]{1,0:T(8,128)(2,1)S(1)}, s3...) custom-call(f32[3,4096]{1,0:T(4,128)} %pts_hbm.1, f32[1,4096]{1,0:T(1,128)} %bitcast.2, ...), custom_call_target="tpu_custom_call" | custom-call | flops 1000000000 | bytes 1048576 | tf_op jit(solution)/shard_map/sort_blocks/pallas_call | solution.py:414
  11.7 0.7 collective-permute-start.1
  12.4 4.4 %collective-permute-start = (f32[24,2048]{1,0:T(8,128)S(1)}, f32[24,2048]{1,0:T(8,128)S(1)}, u32[]{:S(2)}, u32[]{:S(2)}) collective-permute-start(f32[24,2048]{1,0:T(8,128)S(1)} %get-tuple-element.41.s0.w0), channel_id=1, source_target_pairs={{0,1},{1,0},{2,3},{3,2},{4,5},{5,4},{6,7},{7,6},{8,9},{9,8},{10,11... | collective-permute-start | bytes 589832 | tf_op jit(solution)/shard_map/ppermute | solution.py:627
  16.8 6.0 %diag_build.1 = (bf16[8,256,512]{2,1,0:T(8,128)(2,1)S(1)}, bf16[8,256,512]{2,1,0:T(8,128)(2,1)S(1)}, f32[16,2048]{1,0:T(8,128)S(1)}, f32[16,2048]{1,0:T(8,128)S(1)}) custom-call(s32[24,128]{1,0:T(8,128)S(4)} %get-tuple-element.43.tab, f32[24,2048]{1,0:T(8,128)S(1)} %get-tuple-element.41.s0.w0, f32[24,2048]{1,0:T(8,128)S(1)} %get-tuple-element.42.s1.w1, ...), custom_call_target="tpu_custom_call" | custom-call | flops 3000000000 | bytes 1048576 | tf_op jit(solution)/shard_map/diag_build/pallas_call | solution.py:414
  22.8 5.1 %halo_build.1 = (bf16[8,256,768]{2,1,0:T(8,128)(2,1)S(1)}, bf16[8,256,128]{2,1,0:T(8,128)(2,1)S(1)}, s32[8,128]{1,0:T(8,128)S(4)}, f32[16,2048]{1,0:T(8,128)S(1)...) custom-call(s32[6]{0:T(128)S(4)} %get-tuple-element.40.flags, f32[24,2048]{1,0:T(8,128)S(1)} %get-tuple-element.42.s1.w1, ...), custom_call_target="tpu_custom_call" | custom-call | flops 3000000000 | bytes 1048576 | tf_op jit(solution)/shard_map/halo_build/pallas_call | solution.py:414
  27.9 0.7 collective-permute-start.3
  28.6 2.5 %collective-permute-start.2 = (f32[16,2048]{1,0:T(8,128)S(1)}, f32[16,2048]{1,0:T(8,128)S(1)}, u32[]{:S(2)}, u32[]{:S(2)}) collective-permute-start(f32[16,2048]{1,0:T(8,128)S(1)} %get-tuple-element.57), channel_id=1, source_target_pairs={{0,1},{1,0},{2,3},{3,2},{4,5},{5,4},{6,7},{7,6},{8,9},{9,8},{10,11... | collective-permute-start | bytes 393224 | tf_op jit(solution)/shard_map/ppermute | solution.py:627
  31.2 3.9 %own_build.1 = (bf16[8,256,768]{2,1,0:T(8,128)(2,1)S(1)}, bf16[8,256,128]{2,1,0:T(8,128)(2,1)S(1)}, f32[16,2048]{1,0:T(8,128)S(1)}, f32[16,2048]{1,0:T(8,128)S(1)}) custom-call(s32[24,128]{1,0:T(8,128)S(4)} %get-tuple-element.43.tab, f32[24,2048]{1,0:T(8,128)S(1)} %get-tuple-element.41.s0.w0, f32[24,2048]{1,0:T(8,128)S(1)} %get-tuple-element.42.s1.w1, ...), custom_call_target="tpu_custom_call" | custom-call | flops 5000000000 | bytes 1048576 | tf_op jit(solution)/shard_map/own_build/pallas_call | solution.py:414
  35.1 1.0 %finish.2 = (f32[16,2048]{1,0:T(8,128)S(1)}, f32[16,2048]{1,0:T(8,128)S(1)}, f32[16,2048]{1,0:T(8,128)S(1)}, f32[16,2048]{1,0:T(8,128)S(1)}, f32[16,128]{1,0:T(8,128)S(1)}) custom-call(s32[6]{0:T(128)S(4)} %get-tuple-element.40.flags, s32[8,128]{1,0:T(8,128)S(4)} %get-tuple-element.53.tab, bf16[8,256,768]{2,1,0:T(8,128)(2,1)S(1)} %get-tuple-element.54.k12, ...), custom_call_target="tpu_custom_call" | custom-call | flops 1000000000 | bytes 1048576 | tf_op jit(solution)/shard_map/finish/pallas_call | solution.py:414
  36.1 0.7 collective-permute-start.5
  36.8 3.3 %own_apply.2 = (f32[16,2048]{1,0:T(8,128)S(1)}, f32[16,2048]{1,0:T(8,128)S(1)}) custom-call(s32[24,128]{1,0:T(8,128)S(4)} %get-tuple-element.43.tab, bf16[8,256,512]{2,1,0:T(8,128)(2,1)S(1)} %get-tuple-element.46.k00, bf16[8,256,768]{2,1,0:T(8,128)(2,1)S(1)} %get-tuple-element.50.k01, bf16[8,256,128]{2,1,0:T(8,128)(2,1)S(1)} %get-tuple-element.51.x01, ...), custom_call_target="tpu_custom_call" | custom-call | flops 2000000000 | bytes 1048576 | tf_op jit(solution)/shard_map/own_apply/pallas_call | solution.py:414
  40.2 2.2 %finish.3 = (f32[16,2048]{1,0:T(8,128)S(1)}, f32[16,2048]{1,0:T(8,128)S(1)}, f32[16,2048]{1,0:T(8,128)S(1)}, f32[16,2048]{1,0:T(8,128)S(1)}, f32[16,128]{1,0:T(8,128)S(1)}) custom-call(s32[6]{0:T(128)S(4)} %get-tuple-element.40.flags, s32[8,128]{1,0:T(8,128)S(4)} %get-tuple-element.53.tab, bf16[8,256,768]{2,1,0:T(8,128)(2,1)S(1)} %get-tuple-element.54.k12, ...), custom_call_target="tpu_custom_call" | custom-call | flops 1000000000 | bytes 1048576 | tf_op jit(solution)/shard_map/finish/pallas_call | solution.py:414
  42.3 2.5 %collective-permute-start.6 = (f32[16,2048]{1,0:T(8,128)S(1)}, f32[16,2048]{1,0:T(8,128)S(1)}, u32[]{:S(2)}, u32[]{:S(2)}) collective-permute-start(f32[16,2048]{1,0:T(8,128)S(1)} %get-tuple-element.71), channel_id=1, source_target_pairs={{0,1},{1,0},{2,3},{3,2},{4,5},{5,4},{6,7},{7,6},{8,9},{9,8},{10,11... | collective-permute-start | bytes 393224 | tf_op jit(solution)/shard_map/ppermute | solution.py:627
  44.8 0.7 collective-permute-start.7
  45.5 3.2 %own_apply.3 = (f32[16,2048]{1,0:T(8,128)S(1)}, f32[16,2048]{1,0:T(8,128)S(1)}) custom-call(s32[24,128]{1,0:T(8,128)S(4)} %get-tuple-element.43.tab, bf16[8,256,512]{2,1,0:T(8,128)(2,1)S(1)} %get-tuple-element.46.k00, bf16[8,256,768]{2,1,0:T(8,128)(2,1)S(1)} %get-tuple-element.50.k01, bf16[8,256,128]{2,1,0:T(8,128)(2,1)S(1)} %get-tuple-element.51.x01, ...), custom_call_target="tpu_custom_call" | custom-call | flops 2000000000 | bytes 1048576 | tf_op jit(solution)/shard_map/own_apply/pallas_call | solution.py:414
  48.9 7.3 %collective-permute-start.10 = (f32[16,128]{1,0:T(8,128)S(1)}, f32[16,128]{1,0:T(8,128)S(1)}, u32[]{:S(2)}, u32[]{:S(2)}) collective-permute-start(f32[16,128]{1,0:T(8,128)S(1)} %moment.1), channel_id=1, source_target_pairs={{0,3},{1,2},{2,1},{3,0},{4,7},{5,6},{6,5},{7,4},{8,11},{9,10},{10,... | collective-permute-start | bytes 24584 | tf_op jit(solution)/shard_map/ppermute | solution.py:641
  56.4 1.2 %last.1 = (f32[16,2048]{1,0:T(8,128)S(1)}, f32[16,2048]{1,0:T(8,128)S(1)}) custom-call(s32[6]{0:T(128)S(4)} %get-tuple-element.40.flags, s32[8,128]{1,0:T(8,128)S(4)} %get-tuple-element.53.tab, bf16[8,256,768]{2,1,0:T(8,128)(2,1)S(1)} %get-tuple-element.54.k12, bf16[8,256,128]{2,1,0:T(8,128)(2,1)S(1)} %get-tuple-element.55.x12, ...), custom_call_target="tpu_custom_call" | custom-call | flops 1000000000 | bytes 1048576 | tf_op jit(solution)/shard_map/last/pallas_call | solution.py:414
  57.6 1.3 %unsort.2.u0 = f32[48,2048]{1,0:T(8,128)S(1)} custom-call(s32[1,2048]{1,0:T(1,128)S(1)} %get-tuple-element.74.rank_ref, f32[16,2048]{1,0:T(8,128)S(1)} %get-tuple-element.62.w0.wa, f32[16,2048]{1,0:T(8,128)S(1)} %get-tuple-element.67.w0.wb, f32[16,2048]{1,0:T(8,128)S(1)} %get-tuple-element.75.wc), custom_call_target="tpu_custom_call" | custom-call | flops 805306368 | bytes 1048576 | tf_op jit(solution)/shard_map/unsort/pallas_call | solution.py:414
  58.9 0.9 %collective-permute-done.9 = f32[16,128]{1,0:T(8,128)S(1)} collective-permute-done((f32[16,128]{1,0:T(8,128)S(1)}, f32[16,128]{1,0:T(8,128)S(1)}, u32[]{:S(2)}, u32[]{:S(2)}) %collective-permute-start.9) | collective-permute-done | bytes 8224 | tf_op jit(solution)/shard_map/ppermute | solution.py:641
  59.8 1.6 %collective-permute-start.13 = (f32[16,128]{1,0:T(8,128)S(1)}, f32[16,128]{1,0:T(8,128)S(1)}, u32[]{:S(2)}, u32[]{:S(2)}) collective-permute-start(f32[16,128]{1,0:T(8,128)S(1)} %add_add_fusion.1), channel_id=1, source_target_pairs={{0,12},{1,13},{2,14},{3,15},{4,8},{5,9},{6,10},{7,11},{8,4},{9,5},... | collective-permute-start | bytes 24584 | tf_op jit(solution)/shard_map/ppermute | solution.py:641
  61.4 1.5 %collective-permute-start.12 = (f32[16,128]{1,0:T(8,128)S(1)}, f32[16,128]{1,0:T(8,128)S(1)}, u32[]{:S(2)}, u32[]{:S(2)}) collective-permute-start(f32[16,128]{1,0:T(8,128)S(1)} %add_add_fusion.1), channel_id=1, source_target_pairs={{0,8},{1,9},{2,10},{3,11},{4,12},{5,13},{6,14},{7,15},{8,0},{9,1},... | collective-permute-start | bytes 24584 | tf_op jit(solution)/shard_map/ppermute | solution.py:641
  62.9 1.4 %collective-permute-start.11 = (f32[16,128]{1,0:T(8,128)S(1)}, f32[16,128]{1,0:T(8,128)S(1)}, u32[]{:S(2)}, u32[]{:S(2)}) collective-permute-start(f32[16,128]{1,0:T(8,128)S(1)} %add_add_fusion.1), channel_id=1, source_target_pairs={{0,4},{1,5},{2,6},{3,7},{4,0},{5,1},{6,2},{7,3},{8,12},{9,13},{10,... | collective-permute-start | bytes 24584 | tf_op jit(solution)/shard_map/ppermute | solution.py:641
  64.3 1.3 %unsort.3.u1 = f32[48,2048]{1,0:T(8,128)S(1)} custom-call(s32[1,2048]{1,0:T(1,128)S(1)} %get-tuple-element.76.rank_ref, f32[16,2048]{1,0:T(8,128)S(1)} %get-tuple-element.63.w1.wa, f32[16,2048]{1,0:T(8,128)S(1)} %get-tuple-element.68.w1.wb, f32[16,2048]{1,0:T(8,128)S(1)} %get-tuple-element.77.wc), custom_call_target="tpu_custom_call" | custom-call | flops 805306368 | bytes 1048576 | tf_op jit(solution)/shard_map/unsort/pallas_call | solution.py:414
  66.6 1.0 %combine.1 = (f32[16,4096]{1,0:T(8,128)}, f32[16,4096]{1,0:T(8,128)}) custom-call(f32[16,128]{1,0:T(8,128)S(1)} %add_add_fusion.mom, f32[16,4096]{1,0:T(8,128)S(1)} %copy-done, f32[48,2048]{1,0:T(8,128)S(1)} %unsort.2.u0, f32[48,2048]{1,0:T(8,128)S(1)} %unsort.3.u1), custom_call_target="tpu_custom_call" | custom-call | flops 1000000 | bytes 1048576 | tf_op jit(solution)/shard_map/combine/pallas_call | solution.py:414
  (22 shorter events, 1.5 us)
Async XLA Ops:
  11.7 11.1 %collective-permute-start.1 = (f32[24,2048]{1,0:T(8,128)S(1)}, f32[24,2048]{1,0:T(8,128)S(1)}, u32[]{:S(2)}, u32[]{:S(2)}) collective-permute-start(f32[24,2048]{1,0:T(8,128)S(1)} %get-tuple-element.41.s0.w0), channel_id=1, source_target_pairs={{0,0},{15,15},{1,2},{2,1},{3,4},{4,3},{5,6},{6,5},{7,8},{8,7},{9,1... | collective-permute-start | bytes 589832 | tf_op jit(solution)/shard_map/ppermute | solution.py:629
  12.4 10.4 %collective-permute-start = (f32[24,2048]{1,0:T(8,128)S(1)}, f32[24,2048]{1,0:T(8,128)S(1)}, u32[]{:S(2)}, u32[]{:S(2)}) collective-permute-start(f32[24,2048]{1,0:T(8,128)S(1)} %get-tuple-element.41.s0.w0), channel_id=1, source_target_pairs={{0,1},{1,0},{2,3},{3,2},{4,5},{5,4},{6,7},{7,6},{8,9},{9,8},{10,11... | collective-permute-start | bytes 589832 | tf_op jit(solution)/shard_map/ppermute | solution.py:627
  27.9 7.1 %collective-permute-start.3 = (f32[16,2048]{1,0:T(8,128)S(1)}, f32[16,2048]{1,0:T(8,128)S(1)}, u32[]{:S(2)}, u32[]{:S(2)}) collective-permute-start(f32[16,2048]{1,0:T(8,128)S(1)} %get-tuple-element.57), channel_id=1, source_target_pairs={{0,0},{15,15},{1,2},{2,1},{3,4},{4,3},{5,6},{6,5},{7,8},{8,7},{9,1... | collective-permute-start | bytes 393224 | tf_op jit(solution)/shard_map/ppermute | solution.py:629
  28.6 6.4 %collective-permute-start.2 = (f32[16,2048]{1,0:T(8,128)S(1)}, f32[16,2048]{1,0:T(8,128)S(1)}, u32[]{:S(2)}, u32[]{:S(2)}) collective-permute-start(f32[16,2048]{1,0:T(8,128)S(1)} %get-tuple-element.57), channel_id=1, source_target_pairs={{0,1},{1,0},{2,3},{3,2},{4,5},{5,4},{6,7},{7,6},{8,9},{9,8},{10,11... | collective-permute-start | bytes 393224 | tf_op jit(solution)/shard_map/ppermute | solution.py:627
  36.1 4.1 %collective-permute-start.4 = (f32[16,2048]{1,0:T(8,128)S(1)}, f32[16,2048]{1,0:T(8,128)S(1)}, u32[]{:S(2)}, u32[]{:S(2)}) collective-permute-start(f32[16,2048]{1,0:T(8,128)S(1)} %get-tuple-element.60), channel_id=1, source_target_pairs={{0,1},{1,0},{2,3},{3,2},{4,5},{5,4},{6,7},{7,6},{8,9},{9,8},{10,11... | collective-permute-start | bytes 393224 | tf_op jit(solution)/shard_map/ppermute | solution.py:627
  36.1 4.0 %collective-permute-start.5 = (f32[16,2048]{1,0:T(8,128)S(1)}, f32[16,2048]{1,0:T(8,128)S(1)}, u32[]{:S(2)}, u32[]{:S(2)}) collective-permute-start(f32[16,2048]{1,0:T(8,128)S(1)} %get-tuple-element.61), channel_id=1, source_target_pairs={{0,0},{15,15},{1,2},{2,1},{3,4},{4,3},{5,6},{6,5},{7,8},{8,7},{9,1... | collective-permute-start | bytes 393224 | tf_op jit(solution)/shard_map/ppermute | solution.py:629
  42.3 6.3 %collective-permute-start.6 = (f32[16,2048]{1,0:T(8,128)S(1)}, f32[16,2048]{1,0:T(8,128)S(1)}, u32[]{:S(2)}, u32[]{:S(2)}) collective-permute-start(f32[16,2048]{1,0:T(8,128)S(1)} %get-tuple-element.71), channel_id=1, source_target_pairs={{0,1},{1,0},{2,3},{3,2},{4,5},{5,4},{6,7},{7,6},{8,9},{9,8},{10,11... | collective-permute-start | bytes 393224 | tf_op jit(solution)/shard_map/ppermute | solution.py:627
  44.8 3.9 %collective-permute-start.7 = (f32[16,2048]{1,0:T(8,128)S(1)}, f32[16,2048]{1,0:T(8,128)S(1)}, u32[]{:S(2)}, u32[]{:S(2)}) collective-permute-start(f32[16,2048]{1,0:T(8,128)S(1)} %get-tuple-element.72), channel_id=1, source_target_pairs={{0,0},{15,15},{1,2},{2,1},{3,4},{4,3},{5,6},{6,5},{7,8},{8,7},{9,1... | collective-permute-start | bytes 393224 | tf_op jit(solution)/shard_map/ppermute | solution.py:629
  48.9 10.0 %collective-permute-start.10 = (f32[16,128]{1,0:T(8,128)S(1)}, f32[16,128]{1,0:T(8,128)S(1)}, u32[]{:S(2)}, u32[]{:S(2)}) collective-permute-start(f32[16,128]{1,0:T(8,128)S(1)} %moment.1), channel_id=1, source_target_pairs={{0,3},{1,2},{2,1},{3,0},{4,7},{5,6},{6,5},{7,4},{8,11},{9,10},{10,... | collective-permute-start | bytes 24584 | tf_op jit(solution)/shard_map/ppermute | solution.py:641
  56.2 3.7 %collective-permute-start.9 = (f32[16,128]{1,0:T(8,128)S(1)}, f32[16,128]{1,0:T(8,128)S(1)}, u32[]{:S(2)}, u32[]{:S(2)}) collective-permute-start(f32[16,128]{1,0:T(8,128)S(1)} %moment.1), channel_id=1, source_target_pairs={{0,2},{1,3},{2,0},{3,1},{4,6},{5,7},{6,4},{7,5},{8,10},{9,11},{10,... | collective-permute-start | bytes 24584 | tf_op jit(solution)/shard_map/ppermute | solution.py:641
  56.2 3.7 %collective-permute-start.8 = (f32[16,128]{1,0:T(8,128)S(1)}, f32[16,128]{1,0:T(8,128)S(1)}, u32[]{:S(2)}, u32[]{:S(2)}) collective-permute-start(f32[16,128]{1,0:T(8,128)S(1)} %moment.1), channel_id=1, source_target_pairs={{0,1},{1,0},{2,3},{3,2},{4,5},{5,4},{6,7},{7,6},{8,9},{9,8},{10,11... | collective-permute-start | bytes 24584 | tf_op jit(solution)/shard_map/ppermute | solution.py:641
  57.6 9.0 %copy-start = (f32[16,4096]{1,0:T(8,128)S(1)}, f32[16,4096]{1,0:T(8,128)}, u32[]{:S(2)}) copy-start(f32[16,4096]{1,0:T(8,128)} %probes.1) | copy-start | bytes 786436
  59.8 5.7 %collective-permute-start.13 = (f32[16,128]{1,0:T(8,128)S(1)}, f32[16,128]{1,0:T(8,128)S(1)}, u32[]{:S(2)}, u32[]{:S(2)}) collective-permute-start(f32[16,128]{1,0:T(8,128)S(1)} %add_add_fusion.1), channel_id=1, source_target_pairs={{0,12},{1,13},{2,14},{3,15},{4,8},{5,9},{6,10},{7,11},{8,4},{9,5},... | collective-permute-start | bytes 24584 | tf_op jit(solution)/shard_map/ppermute | solution.py:641
  61.4 4.5 %collective-permute-start.12 = (f32[16,128]{1,0:T(8,128)S(1)}, f32[16,128]{1,0:T(8,128)S(1)}, u32[]{:S(2)}, u32[]{:S(2)}) collective-permute-start(f32[16,128]{1,0:T(8,128)S(1)} %add_add_fusion.1), channel_id=1, source_target_pairs={{0,8},{1,9},{2,10},{3,11},{4,12},{5,13},{6,14},{7,15},{8,0},{9,1},... | collective-permute-start | bytes 24584 | tf_op jit(solution)/shard_map/ppermute | solution.py:641
  62.9 3.7 %collective-permute-start.11 = (f32[16,128]{1,0:T(8,128)S(1)}, f32[16,128]{1,0:T(8,128)S(1)}, u32[]{:S(2)}, u32[]{:S(2)}) collective-permute-start(f32[16,128]{1,0:T(8,128)S(1)} %add_add_fusion.1), channel_id=1, source_target_pairs={{0,4},{1,5},{2,6},{3,7},{4,0},{5,1},{6,2},{7,3},{8,12},{9,13},{10,... | collective-permute-start | bytes 24584 | tf_op jit(solution)/shard_map/ppermute | solution.py:641
